TPU v7x, 256 devices: a whole 4x4x8 slice. The times are simulated.
256 devices in a mesh: row: 16 (over y, z_lo), col: 16 (over x, z_hi, core).
Axes of the slice: x: 4, y: 4, z: 8 (z_hi: 2, z_lo: 4; z = z_hi * 4 + z_lo), core: 2. Of those that a mesh axis runs over, the one named last changes fastest.
Arguments:
- pair: bfloat16 [768, 768, 128], P('row', 'col'), may hold values from -6 to 6
- norm_gain: float32 [2, 128], replicated, may hold values from 0.1 to 1.9
- proj_weight: bfloat16 [2, 128, 256], replicated, may hold values from -0.5 to 0.5
- hid_gain: float32 [2, 64], replicated, may hold values from 0.1 to 1.9
- out_weight: bfloat16 [2, 64, 128], replicated, may hold values from -0.75 to 0.75
- gate_weight: bfloat16 [2, 128, 128], replicated, may hold values from -0.5 to 0.5
Outputs:
- updated: bfloat16 [768, 768, 128], P('row', 'col')
All inputs are finite; a program needn't handle non-finite values.
Results may differ from a plain program's by a relative error of at most 0.022.
Values may be sent and summed in bfloat16 or wider, within the bound.
No kernel may reach another device: no remote copies, remote signals or barrier semaphores. Data moves between devices by JAX's collectives and lax.ppermute only.
A program may use at most 128 MiB of HBM per device.

v0:
```python
import jax
import jax.numpy as jnp
from jax import lax
from jax.sharding import PartitionSpec as P


def layer_norm(values, gain):
    mean = jnp.mean(values, axis=-1, keepdims=True)
    centred = values - mean
    var = jnp.mean(centred * centred, axis=-1, keepdims=True)
    return centred * jax.lax.rsqrt(var + 1e-05) * gain


def project(block, gain, weight):
    normed = layer_norm(block.astype(jnp.float32), gain).astype(jnp.bfloat16)
    proj = jnp.einsum("ijd,de->ije", normed, weight, preferred_element_type=jnp.float32)
    width = weight.shape[1] // 4
    left = (jax.nn.sigmoid(proj[..., :width]) * proj[..., width : 2 * width]).astype(jnp.bfloat16)
    right = (jax.nn.sigmoid(proj[..., 2 * width : 3 * width]) * proj[..., 3 * width :]).astype(
        jnp.bfloat16
    )
    return (normed, jnp.transpose(left, (2, 0, 1)), jnp.transpose(right, (2, 0, 1)))


def finish(block, normed, mixed, hgain, oweight, gweight):
    hidden = layer_norm(jnp.transpose(mixed, (1, 2, 0)), hgain).astype(jnp.bfloat16)
    gate = jax.nn.sigmoid(
        jnp.einsum("ijd,de->ije", normed, gweight, preferred_element_type=jnp.float32)
    )
    update = jnp.einsum("ijc,cd->ijd", hidden, oweight, preferred_element_type=jnp.float32)
    return (block.astype(jnp.float32) + gate * update).astype(jnp.bfloat16)


def body(pair, norm_gain, proj_weight, hid_gain, out_weight, gate_weight):
    normed, left, right = project(pair, norm_gain[0], proj_weight[0])
    right_cols = lax.all_gather(right, "row", axis=1, tiled=True)
    partial_sum = jnp.einsum("cik,cjk->cij", left, right_cols, preferred_element_type=jnp.float32)
    mixed = lax.psum_scatter(
        partial_sum.astype(jnp.bfloat16), "col", scatter_dimension=2, tiled=True
    ).astype(jnp.float32)
    first = finish(pair, normed, mixed, hid_gain[0], out_weight[0], gate_weight[0])
    normed, left, right = project(first, norm_gain[1], proj_weight[1])
    left_rows = lax.all_gather(left, "col", axis=2, tiled=True)
    partial_sum = jnp.einsum("cki,ckj->cij", left_rows, right, preferred_element_type=jnp.float32)
    mixed = lax.psum_scatter(
        partial_sum.astype(jnp.bfloat16), "row", scatter_dimension=1, tiled=True
    ).astype(jnp.float32)
    return finish(first, normed, mixed, hid_gain[1], out_weight[1], gate_weight[1])


def solution(mesh):
    placed = (P("row", "col", None), P(), P(), P(), P(), P())
    return jax.shard_map(
        body, mesh=mesh, in_specs=placed, out_specs=P("row", "col", None), check_vma=False
    )
```

profile of v0, /device:TPU:2, one launch (start us, length us, event | category | flops | bytes accessed | tf_op | source)
XLA Modules:
  0.0 843.9 jit_solution(16434930799012498157)
XLA Ops:
  6.5 1.5 convert_reduce_fusion.1
  8.1 1.8 fusion.20
  9.9 0.8 fusion.50
  10.7 1.5 fusion.47
  12.3 0.6 copy.35
  12.9 211.4 %all-gather.3.cloned.1.call-done = bf16[64,768,48]{0,2,1:T(8,128)(2,1)} async-done(((bf16[64,48,48]{0,2,1:T(8,128)(2,1)}), bf16[64,768,48]{0,2,1:T(8,128)(2,1)}) %all-gather.3.cloned.1.call-update) | async-done | bytes 4718608 | tf_op jit(solution)/shard_map/all_gather | solution.py:36
  224.3 16.9 %copy.36 = bf16[64,768,48]{2,1,0:T(8,128)(2,1)} copy(bf16[64,768,48]{0,2,1:T(8,128)(2,1)} %all-gather.3.cloned.1.call-done) | data formatting | bytes 9437184 | tf_op jit(solution)/shard_map/all_gather | solution.py:36
  241.3 11.2 %convolution_convert_fusion.1 = bf16[64,48,768]{2,1,0:T(8,128)(2,1)} fusion(bf16[64,48,48]{2,1,0:T(8,128)(2,1)S(1)} %copy.35, bf16[64,768,48]{2,1,0:T(8,128)(2,1)} %copy.36), kind=kOutput, calls=%fused_computation.1 | convolution fusion | flops 228851712 | bytes 9732096 | tf_op jit(solution)/shard_map/cik,cjk->cij/dot_general | solution.py:37
  252.4 16.1 %copy.37 = bf16[64,48,768]{0,1,2:T(8,128)(2,1)} copy(bf16[64,48,768]{2,1,0:T(8,128)(2,1)} %convolution_convert_fusion.1) | data formatting | bytes 9437184 | tf_op jit(solution)/shard_map/convert_element_type | solution.py:39
  268.5 0.2 all-gather.5.cloned.1.call-start
  268.7 0.4 copy-done.6
  269.2 0.2 copy-done.7
  269.3 0.8 fusion.14
  270.1 147.6 %reduce-scatter.3.cloned.1.call-done = bf16[64,48,48]{0,1,2:T(8,128)(2,1)} async-done(((bf16[64,48,768]{0,1,2:T(8,128)(2,1)}), bf16[64,48,48]{0,1,2:T(8,128)(2,1)}) %reduce-scatter.3.cloned.1.call-update) | async-done | bytes 294928 | tf_op jit(solution)/shard_map/reduce_scatter | solution.py:38
  417.8 1.5 bitcast_reduce_fusion.1
  419.4 1.8 fusion.41
  421.3 0.1 copy.41
  421.4 0.8 fusion.43
  422.2 0.5 convert_reduce_fusion
  422.8 0.7 fusion.17
  423.5 0.8 fusion.53
  424.3 1.5 fusion.49
  425.8 0.6 copy.44
  426.5 110.6 %all-gather.5.cloned.1.call-done = bf16[64,48,768]{0,2,1:T(8,128)(2,1)} async-done(((bf16[64,48,48]{0,2,1:T(8,128)(2,1)}), bf16[64,48,768]{0,2,1:T(8,128)(2,1)}) %all-gather.5.cloned.1.call-update) | async-done | bytes 4718608 | tf_op jit(solution)/shard_map/all_gather | solution.py:43
  537.1 20.0 %copy.43 = bf16[64,48,768]{1,2,0:T(8,128)(2,1)} copy(bf16[64,48,768]{0,2,1:T(8,128)(2,1)} %all-gather.5.cloned.1.call-done) | data formatting | bytes 9437184 | tf_op jit(solution)/shard_map/all_gather | solution.py:43
  557.1 9.0 %convolution_convert_fusion = bf16[64,768,48]{2,1,0:T(8,128)(2,1)} fusion(bf16[64,48,768]{1,2,0:T(8,128)(2,1)} %copy.43, bf16[64,48,48]{2,1,0:T(8,128)(2,1)S(1)} %copy.44), kind=kOutput, calls=%fused_computation | convolution fusion | flops 228851712 | bytes 9732096 | tf_op jit(solution)/shard_map/cki,ckj->cij/dot_general | solution.py:44
  566.1 0.8 fusion.11
  566.9 267.2 %reduce-scatter.5.cloned.1.call-done = bf16[64,48,48]{2,1,0:T(8,128)(2,1)} async-done(((bf16[64,768,48]{2,1,0:T(8,128)(2,1)}), bf16[64,48,48]{2,1,0:T(8,128)(2,1)}) %reduce-scatter.5.cloned.1.call-update) | async-done | bytes 294928 | tf_op jit(solution)/shard_map/reduce_scatter | solution.py:45
  834.1 1.4 bitcast_reduce_fusion
  835.5 0.3 fusion.2
  835.8 0.3 fusion.4
  836.1 1.2 fusion.16
  (34 shorter events, 0.5 us)
Async XLA Ops:
  6.5 3.3 copy-start
  6.5 3.3 copy-start.5
  6.5 3.4 copy-start.3
  6.5 217.8 %all-gather.3.cloned.1.call-start = ((), (), s32[]{:S(2)}) async-start(), calls=%async_computation.2 | async-start | bytes 10027008 | tf_op jit(solution)/shard_map/all_gather | solution.py:36
  12.2 405.6 %reduce-scatter.3.cloned.1.call-start = ((), (), s32[]{:S(2)}) async-start(), calls=%async_computation.3 | async-start | bytes 10027008 | tf_op jit(solution)/shard_map/reduce_scatter | solution.py:38
  268.5 0.7 copy-start.6
  268.5 0.9 copy-start.7
  268.5 268.6 %all-gather.5.cloned.1.call-start = ((), (), s32[]{:S(2)}) async-start(), calls=%async_computation.4 | async-start | bytes 10027008 | tf_op jit(solution)/shard_map/all_gather | solution.py:43
  417.8 3.6 copy-start.2
  419.3 2.9 copy-start.4
  425.8 408.3 %reduce-scatter.5.cloned.1.call-start = ((), (), s32[]{:S(2)}) async-start(), calls=%async_computation.5 | async-start | bytes 13369344 | tf_op jit(solution)/shard_map/reduce_scatter | solution.py:45
  834.1 1.4 copy-start.1
Sparse Core Ops, SparseCore 0:
  12.3 211.9 all-gather.2
  268.6 149.0 reduce-scatter.2
  425.9 111.1 all-gather.4
  566.2 267.8 reduce-scatter.4
where the time goes:
time: 846 us; the launch traced here: 844 us
  waiting for transfers between devices  737 us (87%)
  local copies, waits for them, and re-layouts  55.2 us (7%)
  matrix products  25.2 us (3%)
  between operations  13.3 us (2%)
  other arithmetic  13 us (2%)
    reduce_scatter x1, waiting for transfers between devices, body(): lax.psum_scatter(partial_sum.astype(jnp.bfloat16), 'row', scatter_dimensi...  267 us
    all_gather x1, waiting for transfers between devices, body(): right_cols = lax.all_gather(right, 'row', axis=1, tiled=True)  211 us
    reduce_scatter x1, waiting for transfers between devices, body(): lax.psum_scatter(partial_sum.astype(jnp.bfloat16), 'col', scatter_dimensi...  148 us
    all_gather x1, waiting for transfers between devices, body(): left_rows = lax.all_gather(left, 'col', axis=2, tiled=True)  111 us
    all_gather x1, local copies, waits for them, and re-layouts, body(): left_rows = lax.all_gather(left, 'col', axis=2, tiled=True)  20 us
    all_gather x1, local copies, waits for them, and re-layouts, body(): right_cols = lax.all_gather(right, 'row', axis=1, tiled=True)  16.9 us
  transfers between devices with their start and end apart: 4, of which 4 were waited for; matrix products, arithmetic and copies ran while one was open for 0% of the time, Pallas kernels for 0%

commit v1 on v0

v1 whole, which is shorter than its diff:
```python
import functools

import jax
import jax.numpy as jnp
from jax import lax
from jax.experimental import pallas as pl
from jax.experimental.pallas import tpu as pltpu
from jax.sharding import Mesh
from jax.sharding import PartitionSpec as P

F32, BF16 = jnp.float32, jnp.bfloat16
SIDE = 48
HALF = SIDE // 2
SLOT = 64
CH = 64
EPS = 1e-05
NT = (((1,), (1,)), ((), ()))
TN = (((0,), (0,)), ((), ()))
PARAMS = pltpu.CompilerParams(vmem_limit_bytes=56 * 1024 * 1024)
VMEM = pl.BlockSpec(memory_space=pltpu.VMEM)


def call(kernel, outs, n_in, scratch=(), smem=0):
    return pl.pallas_call(
        kernel,
        out_shape=[jax.ShapeDtypeStruct(shape, BF16) for shape in outs],
        in_specs=[VMEM] * n_in + [pl.BlockSpec(memory_space=pltpu.SMEM)] * smem,
        out_specs=[VMEM] * len(outs),
        scratch_shapes=scratch,
        compiler_params=PARAMS,
    )


def low_lanes(rows):
    return lax.broadcasted_iota(jnp.int32, (rows, 2 * SLOT), 1) < SLOT


def pair_up(first, second):
    low = low_lanes(first.shape[0])
    return (
        jnp.where(low, first, pltpu.roll(second, SLOT, 1)),
        jnp.where(low, pltpu.roll(first, SLOT, 1), second),
    )


def layer_norm(values, gain, axis):
    mean = jnp.mean(values, axis=axis, keepdims=True)
    centred = values - mean
    var = jnp.mean(centred * centred, axis=axis, keepdims=True)
    return centred * lax.rsqrt(var + EPS) * gain


def two_rows(ref, s):
    pad = jnp.zeros((SLOT - SIDE, 128), F32)
    return jnp.concatenate([ref[s].astype(F32), pad, ref[s + HALF].astype(F32), pad], axis=0)


def project(rows, s, gain, weight, staged):
    normed = layer_norm(rows, gain, 1).astype(BF16)
    proj = lax.dot_general(weight, normed, NT, preferred_element_type=F32)
    left = jax.nn.sigmoid(proj[:CH]) * proj[CH : 2 * CH]
    right = jax.nn.sigmoid(proj[2 * CH : 3 * CH]) * proj[3 * CH :]
    first, second = pair_up(left, right)
    staged[:, s, :] = first
    staged[:, s + HALF, :] = second


def project_kernel(pair, gain, weight, out, staged):
    wt = weight[...].astype(F32).T.astype(BF16)
    for s in range(HALF):
        project(two_rows(pair, s), s, gain[...], wt, staged)
    out[...] = staged[...].astype(BF16)


def finish(pair, mixed, s, gain, hgain, oweight, gweight):
    rows = two_rows(pair, s)
    normed = layer_norm(rows, gain, 1).astype(BF16)
    gate = jax.nn.sigmoid(jnp.dot(normed, gweight, preferred_element_type=F32))
    hidden = layer_norm(mixed[:, s, :], hgain, 0).astype(BF16)
    update = lax.dot_general(hidden, oweight, TN, preferred_element_type=F32)
    return (rows + gate * update).astype(BF16)


def middle_kernel(pair, mixed, gain, hgain, oweight, gweight, gain2, weight2, z_out, out, mixed32, staged):
    wt = weight2[...].astype(F32).T.astype(BF16)
    hcol = hgain[...].T
    mixed32[...] = mixed[...].astype(F32)
    keep = lax.broadcasted_iota(jnp.int32, (2 * SLOT, 128), 0) % SLOT < SIDE
    for s in range(HALF):
        z = finish(pair, mixed32, s, gain[...], hcol, oweight[...], gweight[...])
        z_out[s] = z[:SIDE]
        z_out[s + HALF] = z[SLOT : SLOT + SIDE]
        rows = jnp.where(keep, z.astype(F32), 0.0)
        project(rows, s, gain2[...], wt, staged)
    out[...] = staged[...].astype(BF16)


def last_kernel(pair, mixed, gain, hgain, oweight, gweight, z_out, mixed32):
    hcol = hgain[...].T
    mixed32[...] = mixed[...].astype(F32)
    for s in range(HALF):
        z = finish(pair, mixed32, s, gain[...], hcol, oweight[...], gweight[...])
        z_out[s] = z[:SIDE]
        z_out[s + HALF] = z[SLOT : SLOT + SIDE]


def lanes_of(ref, which, base):
    return jnp.concatenate([ref[p][:, base : base + SIDE] for p in which], axis=1)


def split_out_kernel(got, left, right):
    for a in range(4):
        rows = slice(a * SIDE, (a + 1) * SIDE)
        which = range(a * 16, a * 16 + 16)
        left[rows, :] = lanes_of(got, which, 0)
        right[rows, :] = lanes_of(got, which, SLOT)


def send_back(total, place, out):
    for a in range(4):
        for b in range(0, 4, 2):
            tile = total[a * SIDE : (a + 1) * SIDE, b * SLOT : (b + 2) * SLOT]
            first, second = pair_up(tile[:HALF], tile[HALF:])
            out[place(a, b)] = first.astype(BF16)
            out[place(a, b + 1)] = second.astype(BF16)


def mix_out_kernel(left, r0, r1, r2, r3, me, out):
    pad = jnp.zeros((SLOT - SIDE, 768), BF16)
    for step, ref in enumerate((r0, r1, r2, r3)):
        pieces = []
        for b in range(4):
            pieces += [ref[b * SIDE : (b + 1) * SIDE, :], pad]
        total = lax.dot_general(left[...], jnp.concatenate(pieces, axis=0), NT, preferred_element_type=F32)
        owner = lax.rem(me[0] + step, 4)
        send_back(total, lambda a, b: a * 16 + owner * 4 + b, out)


def split_in_kernel(got, left, right):
    for r in range(8):
        rows = slice(r * SIDE, (r + 1) * SIDE)
        which = list(range(r * 4, r * 4 + 4)) + list(range((r + 8) * 4, (r + 8) * 4 + 4))
        left[rows, :] = lanes_of(got, which, 0)
    for r in range(16):
        for b in range(0, 4, 2):
            first, second = got[r * 4 + b].astype(F32), got[r * 4 + b + 1].astype(F32)
            low = low_lanes(SIDE)
            tile = jnp.where(low, pltpu.roll(first, SLOT, 1), second)
            right[r * SIDE : (r + 1) * SIDE, b * SLOT : (b + 2) * SLOT] = tile.astype(BF16)


def mix_in_kernel(right, l0, l1, l2, l3, me, out):
    for step, ref in enumerate((l0, l1, l2, l3)):
        total = lax.dot_general(
            ref[:, :192], right[:384, :], TN, preferred_element_type=F32
        ) + lax.dot_general(ref[:, 192:], right[384:, :], TN, preferred_element_type=F32)
        owner = lax.rem(me[0] + step, 4)
        send_back(total, lambda a, b: owner * 16 + a * 4 + b, out)


def around(values, axis):
    return [values] + [
        lax.ppermute(values, axis, [((i + step) % 4, i) for i in range(4)]) for step in (1, 2, 3)
    ]


MESSAGE = (64, SIDE, 128)
BACK = (64, HALF, 128)
BLOCK = (SIDE, SIDE, 128)


def body(pair, norm_gain, proj_weight, hid_gain, out_weight, gate_weight):
    staged = pltpu.VMEM(MESSAGE, F32)
    mixed32 = pltpu.VMEM(BACK, F32)
    gain = [norm_gain[p : p + 1] for p in range(2)]
    hgain = [hid_gain[p : p + 1] for p in range(2)]
    out_axes, in_axes = ("zl", "x", "zh", "c"), ("y", "zl", "zh", "c")

    (sent,) = call(project_kernel, [MESSAGE], 3, [staged])(pair, gain[0], proj_weight[0])
    got = lax.all_to_all(sent, out_axes, 0, 0, tiled=True)
    left, right = call(split_out_kernel, [(192, 768)] * 2, 1)(got)
    me = lax.axis_index("y").reshape(1)
    (sent,) = call(mix_out_kernel, [BACK], 5, smem=1)(left, *around(right, "y"), me)
    mixed = lax.all_to_all(sent, out_axes, 0, 0, tiled=True)
    first, sent = call(middle_kernel, [BLOCK, MESSAGE], 8, [mixed32, staged])(
        pair, mixed, gain[0], hgain[0], out_weight[0], gate_weight[0], gain[1], proj_weight[1]
    )
    got = lax.all_to_all(sent, in_axes, 0, 0, tiled=True)
    left, right = call(split_in_kernel, [(384, 384), (768, 256)], 1)(got)
    me = lax.axis_index("x").reshape(1)
    (sent,) = call(mix_in_kernel, [BACK], 5, smem=1)(right, *around(left, "x"), me)
    mixed = lax.all_to_all(sent, in_axes, 0, 0, tiled=True)
    (updated,) = call(last_kernel, [BLOCK], 6, [mixed32])(
        first, mixed, gain[1], hgain[1], out_weight[1], gate_weight[1]
    )
    return updated


def solution(mesh):
    fine = Mesh(mesh.devices.reshape(4, 4, 4, 2, 2), ("y", "zl", "x", "zh", "c"))
    spec = P(("y", "zl"), ("x", "zh", "c"), None)
    return jax.shard_map(
        body,
        mesh=fine,
        in_specs=(spec, P(), P(), P(), P(), P()),
        out_specs=spec,
        check_vma=False,
    )
```

time: 846 us -> 190 us (0.22)
  waiting for transfers between devices: 737 us -> 40.2 us
  blocking collectives: 0 us -> 85.7 us
  local copies, waits for them, and re-layouts: 55.2 us -> 6.99 us
  Pallas kernels: 0 us -> 37.8 us
  matrix products: 25.2 us -> 0 us
  starting transfers between devices: 0.31 us -> 15.8 us
  between operations: 13.3 us -> 0.05 us
  other arithmetic: 13 us -> 0 us
    reduce_scatter x2 -> x0, waiting for transfers between devices: 415 us -> none  [the longest x1 267 us: body(): lax.psum_scatter(partial_sum.astype(jnp.bfloat16), 'row', scatter_dimensi...]
    all_gather x2 -> x0, waiting for transfers between devices: 322 us -> none  [the longest x1 211 us: body(): right_cols = lax.all_gather(right, 'row', axis=1, tiled=True)]
    all_to_all x0 -> x3, blocking collectives: none -> 85.7 us  [the longest x1 34.5 us: body(): got = lax.all_to_all(sent, out_axes, 0, 0, tiled=True)]
    pallas_call x0 -> x7, Pallas kernels: none -> 37.8 us  [the longest x1 14.7 us: body(): call(middle_kernel, [BLOCK, MESSAGE], 8, [mixed32, staged])]
    all_gather x2 -> x0, local copies, waits for them, and re-layouts: 36.9 us -> none  [the longest x1 20 us: body(): left_rows = lax.all_gather(left, 'col', axis=2, tiled=True)]
    ppermute x0 -> x6, waiting for transfers between devices: none -> 27.3 us  [around(): lax.ppermute(values, axis, [((i + step) % 4, i) for i in range(4)])]
    dot_general x8 -> x0, matrix products: 25.2 us -> none  [the longest x1 11.2 us: body(): jnp.einsum('cik,cjk->cij', left, right_cols, preferred_element_type=jnp.f...]
    convert_element_type x1 -> x0, local copies, waits for them, and re-layouts: 16.1 us -> none  [body(): partial_sum.astype(jnp.bfloat16)]
  transfers between devices with their start and end apart: 4 -> 7, of which waited for: 4 -> 6; matrix products, arithmetic and copies ran while one was open for 0% -> 1% of each run, Pallas kernels for 0% -> 0%
where the time goes in v1:
time: 190 us; the launch traced here: 187 us
  blocking collectives  85.7 us (45%)
  waiting for transfers between devices  40.2 us (21%)
  Pallas kernels  37.8 us (20%)
  starting transfers between devices  15.8 us (8%)
  local copies, waits for them, and re-layouts  6.99 us (4%)
    all_to_all x1, blocking collectives, body(): got = lax.all_to_all(sent, out_axes, 0, 0, tiled=True)  34.5 us
    all_to_all x1, blocking collectives, body(): got = lax.all_to_all(sent, in_axes, 0, 0, tiled=True)  29.7 us
    ppermute x6, waiting for transfers between devices, around(): lax.ppermute(values, axis, [((i + step) % 4, i) for i in range(4)])  27.3 us
    all_to_all x1, blocking collectives, body(): mixed = lax.all_to_all(sent, in_axes, 0, 0, tiled=True)  21.6 us
    pallas_call x1, Pallas kernels, body(): call(middle_kernel, [BLOCK, MESSAGE], 8, [mixed32, staged])  14.7 us
    all_to_all x1, waiting for transfers between devices, body(): mixed = lax.all_to_all(sent, out_axes, 0, 0, tiled=True)  13 us
    ppermute x6, starting transfers between devices, around(): lax.ppermute(values, axis, [((i + step) % 4, i) for i in range(4)])  9.78 us
    pallas_call x1, Pallas kernels, body(): call(project_kernel, [MESSAGE], 3, [staged])(pair, gain[0], proj_weight[0])  7.84 us
  transfers between devices with their start and end apart: 7, of which 6 were waited for; matrix products, arithmetic and copies ran while one was open for 1% of the time, Pallas kernels for 0%

profile of v1, /device:TPU:2, one launch (start us, length us, event | category | flops | bytes accessed | tf_op | source)
XLA Modules:
  0.0 186.6 jit_solution(4280490723064091804)
XLA Ops:
  0.0 1.4 fusion.1
  1.4 1.5 slice_bitcast_fusion
  2.9 7.8 %shard_map.64 = bf16[64,48,128]{2,1,0:T(8,128)(2,1)} custom-call(bf16[48,48,128]{2,1,0:T(8,128)(2,1)} %pair.3, f32[1,128]{1,0:T(1,128)} %get-tuple-element.26.gain, bf16[128,256]{1,0:T(8,128)(2,1)} %get-tuple-element.18.weight), custom_call_target="tpu_custom_call" | custom-call | tf_op jit(solution)/shard_map/pallas_call | solution.py:179
  10.7 34.5 %all_to_all.20.got = bf16[64,48,128]{2,1,0:T(8,128)(2,1)} all-to-all(bf16[64,48,128]{2,1,0:T(8,128)(2,1)} %shard_map.64), channel_id=1, replica_groups=mesh['y'=4,'zl'=4,'x'=4,'zh'=2,'c'=2] {'zl','x','zh','c'}, dimensions={0} | all-to-all | bytes 1572864 | tf_op jit(solution)/shard_map/all_to_all | solution.py:180
  45.2 2.4 %shard_map.65 = (bf16[192,768]{1,0:T(8,128)(2,1)}, bf16[192,768]{1,0:T(8,128)(2,1)}) custom-call(bf16[64,48,128]{2,1,0:T(8,128)(2,1)} %all_to_all.20.got), custom_call_target="tpu_custom_call" | custom-call | tf_op jit(solution)/shard_map/pallas_call | solution.py:181
  47.6 1.6 collective-permute-start.2
  49.2 2.9 %collective-permute-start.1 = (bf16[192,768]{1,0:T(8,128)(2,1)}, bf16[192,768]{1,0:T(8,128)(2,1)S(1)}, u32[]{:S(2)}, u32[]{:S(2)}) collective-permute-start(bf16[192,768]{1,0:T(8,128)(2,1)} %get-tuple-element.12.r0), channel_id=1, source_target_pairs={{128,0},{192,64},{0,128},{64,192},{129,1},{193,65},{1,129},{65,193... | collective-permute-start | bytes 884744 | tf_op jit(solution)/shard_map/ppermute | solution.py:163
  52.1 1.3 collective-permute-start
  53.4 5.3 %collective-permute-done.2.r3 = bf16[192,768]{1,0:T(8,128)(2,1)S(1)} collective-permute-done((bf16[192,768]{1,0:T(8,128)(2,1)}, bf16[192,768]{1,0:T(8,128)(2,1)S(1)}, u32[]{:S(2)}, u32[]{:S(2)}) %collective-permute-start.2) | collective-permute-done | bytes 294944 | tf_op jit(solution)/shard_map/ppermute | solution.py:163
  58.7 7.6 %collective-permute-done.1.r2 = bf16[192,768]{1,0:T(8,128)(2,1)S(1)} collective-permute-done((bf16[192,768]{1,0:T(8,128)(2,1)}, bf16[192,768]{1,0:T(8,128)(2,1)S(1)}, u32[]{:S(2)}, u32[]{:S(2)}) %collective-permute-start.1) | collective-permute-done | bytes 294944 | tf_op jit(solution)/shard_map/ppermute | solution.py:163
  66.3 0.7 copy-done.4
  67.0 0.1 copy-done.6
  67.1 2.8 %shard_map.66 = bf16[64,24,128]{2,1,0:T(8,128)(2,1)} custom-call(bf16[192,768]{1,0:T(8,128)(2,1)} %get-tuple-element.11.left, bf16[192,768]{1,0:T(8,128)(2,1)} %get-tuple-element.12.r0, bf16[192,768]{1,0:T(8,128)(2,1)} %copy-done.6, bf16[192,768]{1,0:T(8,128)(2,1)} %copy-done.4, bf16[192,768]{1,0:T(8,128)(2,1)} %copy-done.2, s32[1]{0:T(128)} %bitcast.1.me), custom_call_target="tpu_custom_call" | custom-call | tf_op jit(solution)/shard_map/pallas_call | solution.py:183
  69.9 6.0 %all-to-all-start.1 = ((bf16[64,24,128]{2,1,0:T(8,128)(2,1)}), bf16[64,24,128]{2,1,0:T(8,128)(2,1)S(1)}, u32[]{:S(2)}, u32[]{:S(2)}) async-start(bf16[64,24,128]{2,1,0:T(8,128)(2,1)} %shard_map.66), calls=%async_computation.1 | async-start | bytes 786432 | tf_op jit(solution)/shard_map/all_to_all | solution.py:184
  75.9 0.6 fusion
  76.5 0.6 slice_bitcast_fusion.4
  77.1 0.6 slice_bitcast_fusion.2
  77.8 13.0 %all-to-all-done.1.mixed = bf16[64,24,128]{2,1,0:T(8,128)(2,1)S(1)} async-done(((bf16[64,24,128]{2,1,0:T(8,128)(2,1)}), bf16[64,24,128]{2,1,0:T(8,128)(2,1)S(1)}, u32[]{:S(2)}, u32[]{:S(2)}) %all-to-all-start.1) | async-done | bytes 393248 | tf_op jit(solution)/shard_map/all_to_all | solution.py:184
  90.7 0.7 copy-done
  91.5 14.7 %shard_map.67 = (bf16[48,48,128]{2,1,0:T(8,128)(2,1)}, bf16[64,48,128]{2,1,0:T(8,128)(2,1)}) custom-call(bf16[48,48,128]{2,1,0:T(8,128)(2,1)} %pair.3, bf16[64,24,128]{2,1,0:T(8,128)(2,1)} %copy-done, f32[1,128]{1,0:T(1,128)} %get-tuple-element.26.gain, f32[1,64]{1,0:T(1,128)} %get-tuple-element.24.hgain, bf16[64,128]{1,0:T(8,128)(2,1)} %get-tuple-element.22.oweight, ...), custom_call_target="tpu_custom_call" | custom-call | tf_op jit(solution)/shard_map/pallas_call | solution.py:185
  106.1 29.7 %all_to_all.21.got = bf16[64,48,128]{2,1,0:T(8,128)(2,1)} all-to-all(bf16[64,48,128]{2,1,0:T(8,128)(2,1)} %get-tuple-element.14), channel_id=1, replica_groups=mesh['y'=4,'zl'=4,'x'=4,'zh'=2,'c'=2] {'y','zl','zh','c'}, dimensions={0} | all-to-all | bytes 1572864 | tf_op jit(solution)/shard_map/all_to_all | solution.py:188
  135.8 2.2 %shard_map.68 = (bf16[384,384]{1,0:T(8,128)(2,1)}, bf16[768,256]{1,0:T(8,128)(2,1)}) custom-call(bf16[64,48,128]{2,1,0:T(8,128)(2,1)} %all_to_all.21.got), custom_call_target="tpu_custom_call" | custom-call | tf_op jit(solution)/shard_map/pallas_call | solution.py:189
  138.0 0.4 collective-permute-start.5
  138.5 3.0 %collective-permute-start.4 = (bf16[384,384]{1,0:T(8,128)(2,1)}, bf16[384,384]{1,0:T(8,128)(2,1)S(1)}, u32[]{:S(2)}, u32[]{:S(2)}) collective-permute-start(bf16[384,384]{1,0:T(8,128)(2,1)} %get-tuple-element.16.l0), channel_id=1, source_target_pairs={{8,0},{12,4},{0,8},{4,12},{9,1},{13,5},{1,9},{5,13},{10,2},{14,6},... | collective-permute-start | bytes 884744 | tf_op jit(solution)/shard_map/ppermute | solution.py:163
  141.5 0.5 collective-permute-start.3
  142.0 5.9 %collective-permute-done.5.l3 = bf16[384,384]{1,0:T(8,128)(2,1)S(1)} collective-permute-done((bf16[384,384]{1,0:T(8,128)(2,1)}, bf16[384,384]{1,0:T(8,128)(2,1)S(1)}, u32[]{:S(2)}, u32[]{:S(2)}) %collective-permute-start.5) | collective-permute-done | bytes 294944 | tf_op jit(solution)/shard_map/ppermute | solution.py:163
  147.8 2.3 %collective-permute-done.4.l2 = bf16[384,384]{1,0:T(8,128)(2,1)S(1)} collective-permute-done((bf16[384,384]{1,0:T(8,128)(2,1)}, bf16[384,384]{1,0:T(8,128)(2,1)S(1)}, u32[]{:S(2)}, u32[]{:S(2)}) %collective-permute-start.4) | collective-permute-done | bytes 294944 | tf_op jit(solution)/shard_map/ppermute | solution.py:163
  150.2 6.2 %collective-permute-done.3.l1 = bf16[384,384]{1,0:T(8,128)(2,1)S(1)} collective-permute-done((bf16[384,384]{1,0:T(8,128)(2,1)}, bf16[384,384]{1,0:T(8,128)(2,1)S(1)}, u32[]{:S(2)}, u32[]{:S(2)}) %collective-permute-start.3) | collective-permute-done | bytes 294944 | tf_op jit(solution)/shard_map/ppermute | solution.py:163
  156.4 0.7 copy-done.5
  157.1 3.3 %shard_map.69 = bf16[64,24,128]{2,1,0:T(8,128)(2,1)} custom-call(bf16[768,256]{1,0:T(8,128)(2,1)} %get-tuple-element.15.right, bf16[384,384]{1,0:T(8,128)(2,1)} %get-tuple-element.16.l0, bf16[384,384]{1,0:T(8,128)(2,1)} %copy-done.5, bf16[384,384]{1,0:T(8,128)(2,1)} %copy-done.3, bf16[384,384]{1,0:T(8,128)(2,1)} %copy-done.1, s32[1]{0:T(128)} %bitcast.5.me), custom_call_target="tpu_custom_call" | custom-call | tf_op jit(solution)/shard_map/pallas_call | solution.py:191
  160.4 21.6 %all_to_all.22.mixed = bf16[64,24,128]{2,1,0:T(8,128)(2,1)} all-to-all(bf16[64,24,128]{2,1,0:T(8,128)(2,1)} %shard_map.69), channel_id=1, replica_groups=mesh['y'=4,'zl'=4,'x'=4,'zh'=2,'c'=2] {'y','zl','zh','c'}, dimensions={0} | all-to-all | bytes 786432 | tf_op jit(solution)/shard_map/all_to_all | solution.py:192
  182.0 4.6 %shard_map.70 = bf16[48,48,128]{2,1,0:T(8,128)(2,1)} custom-call(bf16[48,48,128]{2,1,0:T(8,128)(2,1)} %get-tuple-element.13.pair, bf16[64,24,128]{2,1,0:T(8,128)(2,1)} %all_to_all.22.mixed, f32[1,128]{1,0:T(1,128)} %get-tuple-element.25.gain2.gain, f32[1,64]{1,0:T(1,128)} %get-tuple-element.23.hgain, bf16[64,128]{1,0:T(8,128)(2,1)} %get-tuple-element.21.oweight, ...), custom_call_target="tpu_custom_call" | custom-call | tf_op jit(solution)/shard_map/pallas_call | solution.py:193
  (17 shorter events, 0.0 us)
Async XLA Ops:
  47.6 11.1 %collective-permute-start.2 = (bf16[192,768]{1,0:T(8,128)(2,1)}, bf16[192,768]{1,0:T(8,128)(2,1)S(1)}, u32[]{:S(2)}, u32[]{:S(2)}) collective-permute-start(bf16[192,768]{1,0:T(8,128)(2,1)} %get-tuple-element.12.r0), channel_id=1, source_target_pairs={{192,0},{0,64},{64,128},{128,192},{193,1},{1,65},{65,129},{129,193... | collective-permute-start | bytes 884744 | tf_op jit(solution)/shard_map/ppermute | solution.py:163
  49.2 17.1 %collective-permute-start.1 = (bf16[192,768]{1,0:T(8,128)(2,1)}, bf16[192,768]{1,0:T(8,128)(2,1)S(1)}, u32[]{:S(2)}, u32[]{:S(2)}) collective-permute-start(bf16[192,768]{1,0:T(8,128)(2,1)} %get-tuple-element.12.r0), channel_id=1, source_target_pairs={{128,0},{192,64},{0,128},{64,192},{129,1},{193,65},{1,129},{65,193... | collective-permute-start | bytes 884744 | tf_op jit(solution)/shard_map/ppermute | solution.py:163
  52.1 14.2 %collective-permute-start = (bf16[192,768]{1,0:T(8,128)(2,1)}, bf16[192,768]{1,0:T(8,128)(2,1)S(1)}, u32[]{:S(2)}, u32[]{:S(2)}) collective-permute-start(bf16[192,768]{1,0:T(8,128)(2,1)} %get-tuple-element.12.r0), channel_id=1, source_target_pairs={{64,0},{128,64},{192,128},{0,192},{65,1},{129,65},{193,129},{1,193... | collective-permute-start | bytes 884744 | tf_op jit(solution)/shard_map/ppermute | solution.py:163
  58.7 7.6 %copy-start.2 = (bf16[192,768]{1,0:T(8,128)(2,1)}, bf16[192,768]{1,0:T(8,128)(2,1)S(1)}, u32[]{:S(2)}) copy-start(bf16[192,768]{1,0:T(8,128)(2,1)S(1)} %collective-permute-done.2.r3) | copy-start | bytes 884740
  66.3 0.7 copy-start.4
  66.3 0.8 copy-start.6
  69.9 6.0 %copy-start.9 = (f32[2,64]{1,0:T(2,128)S(1)}, f32[2,64]{1,0:T(2,128)}, u32[]{:S(2)}) copy-start(f32[2,64]{1,0:T(2,128)} %param.9) | copy-start | bytes 1540
  69.9 6.6 %copy-start.8 = (bf16[2,64,128]{2,1,0:T(8,128)(2,1)S(1)}, bf16[2,64,128]{2,1,0:T(8,128)(2,1)}, u32[]{:S(2)}) copy-start(bf16[2,64,128]{2,1,0:T(8,128)(2,1)} %param.10) | copy-start | bytes 98308
  69.9 20.8 %all-to-all-start.1 = ((bf16[64,24,128]{2,1,0:T(8,128)(2,1)}), bf16[64,24,128]{2,1,0:T(8,128)(2,1)S(1)}, u32[]{:S(2)}, u32[]{:S(2)}) async-start(bf16[64,24,128]{2,1,0:T(8,128)(2,1)} %shard_map.66), calls=%async_computation.1 | async-start | bytes 786432 | tf_op jit(solution)/shard_map/all_to_all | solution.py:184
  75.9 1.2 copy-start.7
  90.7 0.7 copy-start
  138.0 9.8 %collective-permute-start.5 = (bf16[384,384]{1,0:T(8,128)(2,1)}, bf16[384,384]{1,0:T(8,128)(2,1)S(1)}, u32[]{:S(2)}, u32[]{:S(2)}) collective-permute-start(bf16[384,384]{1,0:T(8,128)(2,1)} %get-tuple-element.16.l0), channel_id=1, source_target_pairs={{12,0},{0,4},{4,8},{8,12},{13,1},{1,5},{5,9},{9,13},{14,2},{2,6},{... | collective-permute-start | bytes 884744 | tf_op jit(solution)/shard_map/ppermute | solution.py:163
  138.5 11.7 %collective-permute-start.4 = (bf16[384,384]{1,0:T(8,128)(2,1)}, bf16[384,384]{1,0:T(8,128)(2,1)S(1)}, u32[]{:S(2)}, u32[]{:S(2)}) collective-permute-start(bf16[384,384]{1,0:T(8,128)(2,1)} %get-tuple-element.16.l0), channel_id=1, source_target_pairs={{8,0},{12,4},{0,8},{4,12},{9,1},{13,5},{1,9},{5,13},{10,2},{14,6},... | collective-permute-start | bytes 884744 | tf_op jit(solution)/shard_map/ppermute | solution.py:163
  141.5 14.9 %collective-permute-start.3 = (bf16[384,384]{1,0:T(8,128)(2,1)}, bf16[384,384]{1,0:T(8,128)(2,1)S(1)}, u32[]{:S(2)}, u32[]{:S(2)}) collective-permute-start(bf16[384,384]{1,0:T(8,128)(2,1)} %get-tuple-element.16.l0), channel_id=1, source_target_pairs={{4,0},{8,4},{12,8},{0,12},{5,1},{9,5},{13,9},{1,13},{6,2},{10,6},{... | collective-permute-start | bytes 884744 | tf_op jit(solution)/shard_map/ppermute | solution.py:163
  147.8 8.5 %copy-start.1 = (bf16[384,384]{1,0:T(8,128)(2,1)}, bf16[384,384]{1,0:T(8,128)(2,1)S(1)}, u32[]{:S(2)}) copy-start(bf16[384,384]{1,0:T(8,128)(2,1)S(1)} %collective-permute-done.5.l3) | copy-start | bytes 884740
  150.2 6.2 %copy-start.3 = (bf16[384,384]{1,0:T(8,128)(2,1)}, bf16[384,384]{1,0:T(8,128)(2,1)S(1)}, u32[]{:S(2)}) copy-start(bf16[384,384]{1,0:T(8,128)(2,1)S(1)} %collective-permute-done.4.l2) | copy-start | bytes 884740
  156.4 0.7 copy-start.5

commit v2 on v1

v2 whole, which is shorter than its diff:
```python
import jax
import jax.numpy as jnp
from jax import lax
from jax.experimental import pallas as pl
from jax.experimental.pallas import tpu as pltpu
from jax.sharding import Mesh
from jax.sharding import PartitionSpec as P

F32, BF16 = jnp.float32, jnp.bfloat16
SIDE = 48
HALF = SIDE // 2
SLOT = 64
MAIN = 40
EXTRA = SIDE - MAIN
PIECE = 16
CH = 64
LANES = 128
EPS = 1e-05
NT = (((1,), (1,)), ((), ()))
TN = (((0,), (0,)), ((), ()))
VMEM = pl.BlockSpec(memory_space=pltpu.VMEM)
SMEM = pl.BlockSpec(memory_space=pltpu.SMEM)


def call(kernel, outs, n_in, scratch=(), smem=0):
    return pl.pallas_call(
        kernel,
        out_shape=[jax.ShapeDtypeStruct(shape, BF16) for shape in outs],
        in_specs=[VMEM] * n_in + [SMEM] * smem,
        out_specs=[VMEM] * len(outs),
        scratch_shapes=scratch,
        compiler_params=pltpu.CompilerParams(vmem_limit_bytes=16 * 1024 * 1024),
    )


def lane_of(rows):
    return lax.broadcasted_iota(jnp.int32, (rows, LANES), 1)


def layer_norm(values, gain, axis):
    mean = jnp.mean(values, axis=axis, keepdims=True)
    centred = values - mean
    var = jnp.mean(centred * centred, axis=axis, keepdims=True)
    return centred * lax.rsqrt(var + EPS) * gain


def sigmoid(values):
    return 0.5 * jnp.tanh(0.5 * values) + 0.5


def two_rows(ref, s):
    pad = jnp.zeros((SLOT - SIDE, LANES), F32)
    return jnp.concatenate([ref[s].astype(F32), pad, ref[s + HALF].astype(F32), pad], axis=0)


def project(rows, s, gain, weight, staged, extra):
    normed = layer_norm(rows, gain, 1).astype(BF16)
    proj = lax.dot_general(weight, normed, NT, preferred_element_type=F32)
    left = sigmoid(proj[:CH]) * proj[CH : 2 * CH]
    right = sigmoid(proj[2 * CH : 3 * CH]) * proj[3 * CH :]
    lane = lane_of(CH)
    first = jnp.where(lane < SIDE, left, pltpu.roll(right, SIDE, 1))
    second = jnp.where(lane < SIDE, pltpu.roll(left, SLOT, 1), pltpu.roll(right, LANES + SIDE - SLOT, 1))
    if s + HALF >= MAIN:
        for g in range(SIDE // PIECE):
            moved = jnp.where(
                lane < 2 * SIDE + PIECE,
                pltpu.roll(second, 2 * SIDE - g * PIECE, 1),
                pltpu.roll(second, SIDE + PIECE - g * PIECE, 1),
            )
            extra[g * EXTRA + s + HALF - MAIN] = moved
    else:
        staged[pl.ds((s + HALF) * CH, CH), :] = second
    staged[pl.ds(s * CH, CH), :] = jnp.where(lane < 2 * SIDE, first, extra[s])


ORDER = [*range(HALF - EXTRA, HALF), *range(HALF - EXTRA)]


def write_messages(staged, out):
    for channel in range(CH):
        out[channel] = staged[pl.ds(channel, MAIN, stride=CH), :].astype(BF16)


def project_kernel(pair, gain, weight, out, staged, extra):
    wt = weight[0].astype(F32).T.astype(BF16)
    for s in ORDER:
        project(two_rows(pair, s), s, gain[0:1, :], wt, staged, extra)
    write_messages(staged, out)


def finish(pair, mixed, s, gain, hgain, oweight, gweight):
    rows = two_rows(pair, s)
    normed = layer_norm(rows, gain, 1).astype(BF16)
    gate = sigmoid(jnp.dot(normed, gweight, preferred_element_type=F32))
    sums = mixed[pl.ds(s, CH, stride=HALF), :]
    hidden = layer_norm(sums, hgain, 0).astype(BF16)
    update = lax.dot_general(hidden, oweight, TN, preferred_element_type=F32)
    return (rows + gate * update).astype(BF16)


def read_sums(mixed, mixed32):
    for channel in range(CH):
        mixed32[pl.ds(channel * HALF, HALF), :] = mixed[channel].astype(F32)


def middle_kernel(pair, mixed, gain, hgain, oweight, gweight, weight, z_out, out, mixed32, staged, extra):
    wt = weight[1].astype(F32).T.astype(BF16)
    hcol = hgain[...].T[:, 0:1]
    read_sums(mixed, mixed32)
    keep = lax.broadcasted_iota(jnp.int32, (2 * SLOT, LANES), 0) % SLOT < SIDE
    for s in ORDER:
        z = finish(pair, mixed32, s, gain[0:1, :], hcol, oweight[0], gweight[0])
        z_out[s] = z[:SIDE]
        z_out[s + HALF] = z[SLOT : SLOT + SIDE]
        rows = jnp.where(keep, z.astype(F32), 0.0)
        project(rows, s, gain[1:2, :], wt, staged, extra)
    write_messages(staged, out)


def last_kernel(pair, mixed, gain, hgain, oweight, gweight, z_out, mixed32):
    hcol = hgain[...].T[:, 1:2]
    read_sums(mixed, mixed32)
    for s in range(HALF):
        z = finish(pair, mixed32, s, gain[1:2, :], hcol, oweight[1], gweight[1])
        z_out[s] = z[:SIDE]
        z_out[s + HALF] = z[SLOT : SLOT + SIDE]


def block_of(ref, p, base):
    values = ref[p].astype(F32)
    start = 2 * SIDE + (PIECE if base else 0)
    tail = [values[g * EXTRA : (g + 1) * EXTRA, start : start + PIECE] for g in range(SIDE // PIECE)]
    return jnp.concatenate([values[:, base : base + SIDE], jnp.concatenate(tail, axis=1)], axis=0)


def blocks_of(ref, which, base):
    return jnp.concatenate([block_of(ref, p, base) for p in which], axis=1).astype(BF16)


def split_out_kernel(got, me, left, kept, given):
    for a in range(8):
        left[a * SIDE : (a + 1) * SIDE, :] = blocks_of(got, [a * 8 + b for b in range(8)], 0)
    for a in range(4):
        rows = slice(a * SIDE, (a + 1) * SIDE)
        mine, other = (2 * a + me[0]) * 8, (2 * a + 1 - me[0]) * 8
        kept[rows, :] = blocks_of(got, [mine + b for b in range(8)], SIDE)
        given[rows, :] = blocks_of(got, [other + b for b in range(8)], SIDE)


def send_back(total, blocks, place, out):
    lane = lane_of(HALF)
    for a in range(blocks):
        for b in range(0, 4, 2):
            tile = total[a * SIDE : (a + 1) * SIDE, b * SLOT : (b + 2) * SLOT]
            low, high = tile[:HALF], tile[HALF:]
            out[place(a, b)] = jnp.where(lane < SLOT, low, pltpu.roll(high, SLOT, 1)).astype(BF16)
            out[place(a, b + 1)] = jnp.where(lane < SLOT, pltpu.roll(low, SLOT, 1), high).astype(BF16)


def padded(ref):
    pad = jnp.zeros((SLOT - SIDE, ref.shape[1]), BF16)
    pieces = []
    for b in range(4):
        pieces += [ref[b * SIDE : (b + 1) * SIDE, :], pad]
    return jnp.concatenate(pieces, axis=0)


def mix_out_kernel(left, left_c, kept, given_c, kept_y, given_d, me, out):
    for step, (near, far) in enumerate(((kept, given_c), (kept_y, given_d))):
        total = lax.dot_general(left[...], padded(near), NT, preferred_element_type=F32)
        total += lax.dot_general(left_c[...], padded(far), NT, preferred_element_type=F32)
        owner = me[0] if step == 0 else 1 - me[0]
        send_back(total, 8, lambda a, b: a * 8 + (2 * (b // 2) + owner) * 2 + b % 2, out)


def split_in_kernel(got, left, right):
    for r in range(8):
        rows = slice(r * SIDE, (r + 1) * SIDE)
        left[rows, :] = blocks_of(got, [(r + 8 * h) * 4 + b for h in range(2) for b in range(4)], 0)
    pad = jnp.zeros((SIDE, SLOT - SIDE), F32)
    for r in range(16):
        pieces = []
        for b in range(4):
            pieces += [block_of(got, r * 4 + b, SIDE), pad]
        right[r * SIDE : (r + 1) * SIDE, :] = jnp.concatenate(pieces, axis=1).astype(BF16)


def mix_in_kernel(right, left, left_c, left_x, left_d, me, out):
    for step, ref in enumerate((left, left_c, left_x, left_d)):
        total = lax.dot_general(ref[:, :192], right[:384, :], TN, preferred_element_type=F32)
        total += lax.dot_general(ref[:, 192:], right[384:, :], TN, preferred_element_type=F32)
        core = me[1] if step % 2 == 0 else 1 - me[1]
        low = me[0] if step < 2 else 1 - me[0]
        send_back(
            total,
            4,
            lambda a, b: (2 * (a // 2) + low) * 16 + (2 * (a % 2) + core) * 4 + b,
            out,
        )


def swap(values, *axes):
    n = 1 << len(axes)
    return lax.ppermute(values, axes, [(i, n - 1 - i) for i in range(n)])


MESSAGE = (CH, MAIN, LANES)
BACK = (CH, HALF, LANES)
BLOCK = (SIDE, SIDE, LANES)


def body(pair, norm_gain, proj_weight, hid_gain, out_weight, gate_weight):
    staged = pltpu.VMEM((MAIN * CH, LANES), F32)
    extra = pltpu.VMEM((HALF, CH, LANES), F32)
    mixed32 = pltpu.VMEM((CH * HALF, LANES), F32)
    out_axes, in_axes = ("yh", "zl", "xh", "xl", "zh"), ("yh", "yl", "zl", "xh", "zh")
    core = lax.axis_index("c")

    (sent,) = call(project_kernel, [MESSAGE], 3, [staged, extra])(pair, norm_gain, proj_weight)
    got = lax.all_to_all(sent, out_axes, 0, 0, tiled=True)
    left, kept, given = call(split_out_kernel, [(384, 384), (192, 384), (192, 384)], 1, smem=1)(
        got, core.reshape(1)
    )
    (sent,) = call(mix_out_kernel, [BACK], 6, smem=1)(
        left,
        swap(left, "c"),
        kept,
        swap(given, "c"),
        swap(kept, "yl"),
        swap(given, "yl", "c"),
        lax.axis_index("yl").reshape(1),
    )
    mixed = lax.all_to_all(sent, out_axes, 0, 0, tiled=True)
    first, sent = call(middle_kernel, [BLOCK, MESSAGE], 7, [mixed32, staged, extra])(
        pair, mixed, norm_gain, hid_gain, out_weight, gate_weight, proj_weight
    )
    got = lax.all_to_all(sent, in_axes, 0, 0, tiled=True)
    left, right = call(split_in_kernel, [(384, 384), (768, 256)], 1)(got)
    (sent,) = call(mix_in_kernel, [BACK], 5, smem=1)(
        right,
        left,
        swap(left, "c"),
        swap(left, "xl"),
        swap(left, "xl", "c"),
        jnp.stack([lax.axis_index("xl"), core]),
    )
    mixed = lax.all_to_all(sent, in_axes, 0, 0, tiled=True)
    (updated,) = call(last_kernel, [BLOCK], 6, [mixed32])(
        first, mixed, norm_gain, hid_gain, out_weight, gate_weight
    )
    return updated


def solution(mesh):
    names = ("yh", "yl", "zl", "xh", "xl", "zh", "c")
    fine = Mesh(mesh.devices.reshape(2, 2, 4, 2, 2, 2, 2), names)
    spec = P(names[:3], names[3:], None)
    return jax.shard_map(
        body,
        mesh=fine,
        in_specs=(spec, P(), P(), P(), P(), P()),
        out_specs=spec,
        check_vma=False,
    )
```

time: 190 us -> 177 us (0.932); the launches traced: 187 us -> 176 us
  blocking collectives: 85.7 us -> 72.5 us
  local copies, waits for them, and re-layouts: 6.99 us -> 2.68 us
  starting transfers between devices: 15.8 us -> 18.9 us
  Pallas kernels: 37.8 us -> 40.2 us
    all_to_all x1, blocking collectives: 34.5 us -> 23 us  [body(): mixed = lax.all_to_all(sent, out_axes, 0, 0, tiled=True)]
    all_to_all x1, starting transfers between devices: 6.01 us -> 14.6 us  [body(): got = lax.all_to_all(sent, out_axes, 0, 0, tiled=True)]
    all_to_all x1, waiting for transfers between devices: 13 us -> 21.5 us  [body(): got = lax.all_to_all(sent, out_axes, 0, 0, tiled=True)]
    ppermute x6 -> x7, waiting for transfers between devices: 27.3 us -> 20.4 us  [swap(): return lax.ppermute(values, axes, [(i, n - 1 - i) for i in range(n)])]
    ppermute x6 -> x7, starting transfers between devices: 9.78 us -> 4.26 us  [swap(): return lax.ppermute(values, axes, [(i, n - 1 - i) for i in range(n)])]
    pallas_call x1, Pallas kernels: 2.23 us -> 5.72 us  [body(): left, right = call(split_in_kernel, [(384, 384), (768, 256)], 1)(got)]
    squeeze x3 -> x0, local copies, waits for them, and re-layouts: 2.76 us -> none  [the longest x1 1.53 us: body(): proj_weight[1]]
    all_to_all x1, blocking collectives: 29.7 us -> 27.3 us  [body(): got = lax.all_to_all(sent, in_axes, 0, 0, tiled=True)]
  transfers between devices with their start and end apart: 7 -> 8, of which waited for: 6 -> 5; matrix products, arithmetic and copies ran while one was open for 1% -> 0% of each run, Pallas kernels for 0% -> 0%
where the time goes in v2:
time: 177 us; the launch traced here: 176 us
  blocking collectives  72.5 us (41%)
  waiting for transfers between devices  41.9 us (24%)
  Pallas kernels  40.2 us (23%)
  starting transfers between devices  18.9 us (11%)
  local copies, waits for them, and re-layouts  2.68 us (2%)
    all_to_all x1, blocking collectives, body(): got = lax.all_to_all(sent, in_axes, 0, 0, tiled=True)  27.3 us
    all_to_all x1, blocking collectives, body(): mixed = lax.all_to_all(sent, out_axes, 0, 0, tiled=True)  23 us
    all_to_all x1, blocking collectives, body(): mixed = lax.all_to_all(sent, in_axes, 0, 0, tiled=True)  22.2 us
    all_to_all x1, waiting for transfers between devices, body(): got = lax.all_to_all(sent, out_axes, 0, 0, tiled=True)  21.5 us
    ppermute x7, waiting for transfers between devices, swap(): return lax.ppermute(values, axes, [(i, n - 1 - i) for i in range(n)])  20.4 us
    all_to_all x1, starting transfers between devices, body(): got = lax.all_to_all(sent, out_axes, 0, 0, tiled=True)  14.6 us
    pallas_call x1, Pallas kernels, body(): call(middle_kernel, [BLOCK, MESSAGE], 7, [mixed32, staged, extra])  14.5 us
    pallas_call x1, Pallas kernels, body(): call(project_kernel, [MESSAGE], 3, [staged, extra])  8.83 us
  transfers between devices with their start and end apart: 8, of which 5 were waited for; matrix products, arithmetic and copies ran while one was open for 0% of the time, Pallas kernels for 0%

profile of v2, /device:TPU:2, one launch (start us, length us, event | category | flops | bytes accessed | tf_op | source)
XLA Modules:
  0.0 176.4 jit_solution(9545806352368863237)
XLA Ops:
  0.0 1.1 copy-done
  1.1 0.9 copy-done.2
  2.0 0.7 copy-done.6
  2.6 8.8 %shard_map.64 = bf16[64,40,128]{2,1,0:T(8,128)(2,1)} custom-call(bf16[48,48,128]{2,1,0:T(8,128)(2,1)S(1)} %copy-done, f32[2,128]{1,0:T(2,128)S(1)} %copy-done.6, bf16[2,128,256]{2,1,0:T(8,128)(2,1)S(1)} %copy-done.2), custom_call_target="tpu_custom_call" | custom-call | tf_op jit(solution)/shard_map/pallas_call | solution.py:220
  11.5 14.6 %all-to-all-start = ((bf16[64,40,128]{2,1,0:T(8,128)(2,1)}), bf16[64,40,128]{2,1,0:T(8,128)(2,1)S(1)}, u32[]{:S(2)}, u32[]{:S(2)}) async-start(bf16[64,40,128]{2,1,0:T(8,128)(2,1)} %shard_map.64), calls=%async_computation | async-start | bytes 1310720 | tf_op jit(solution)/shard_map/all_to_all | solution.py:221
  26.1 21.5 %all-to-all-done.got = bf16[64,40,128]{2,1,0:T(8,128)(2,1)S(1)} async-done(((bf16[64,40,128]{2,1,0:T(8,128)(2,1)}), bf16[64,40,128]{2,1,0:T(8,128)(2,1)S(1)}, u32[]{:S(2)}, u32[]{:S(2)}) %all-to-all-start) | async-done | bytes 655392 | tf_op jit(solution)/shard_map/all_to_all | solution.py:221
  47.6 5.3 %shard_map.65 = (bf16[384,384]{1,0:T(8,128)(2,1)S(1)}, bf16[192,384]{1,0:T(8,128)(2,1)S(1)}, bf16[192,384]{1,0:T(8,128)(2,1)S(1)}) custom-call(bf16[64,40,128]{2,1,0:T(8,128)(2,1)S(1)} %all-to-all-done.got, s32[1]{0:T(128)} %bitcast.me), custom_call_target="tpu_custom_call" | custom-call | tf_op jit(solution)/shard_map/pallas_call | solution.py:222
  52.9 0.1 collective-permute-start
  53.0 0.8 collective-permute-start.2
  53.8 1.1 collective-permute-start.3
  54.9 0.4 collective-permute-start.1
  55.2 4.5 %collective-permute-done.2.kept_y = bf16[192,384]{1,0:T(8,128)(2,1)S(1)} collective-permute-done((bf16[192,384]{1,0:T(8,128)(2,1)S(1)}, bf16[192,384]{1,0:T(8,128)(2,1)S(1)}, u32[]{:S(2)}, u32[]{:S(2)}) %collective-permute-start.2) | collective-permute-done | bytes 147488 | tf_op jit(solution)/shard_map/ppermute | solution.py:205
  59.8 2.2 %collective-permute-done.3.given_d = bf16[192,384]{1,0:T(8,128)(2,1)S(1)} collective-permute-done((bf16[192,384]{1,0:T(8,128)(2,1)S(1)}, bf16[192,384]{1,0:T(8,128)(2,1)S(1)}, u32[]{:S(2)}, u32[]{:S(2)}) %collective-permute-start.3) | collective-permute-done | bytes 147488 | tf_op jit(solution)/shard_map/ppermute | solution.py:205
  62.0 0.0 copy-start.7
  62.0 0.0 copy-start.8
  62.0 0.7 shard_map.66
  62.7 0.0 copy-start.1
  62.7 0.0 copy-start.3
  62.7 0.0 copy-start.4
  62.7 23.0 %all_to_all.20.mixed = bf16[64,24,128]{2,1,0:T(8,128)(2,1)S(1)} all-to-all(bf16[64,24,128]{2,1,0:T(8,128)(2,1)S(1)} %shard_map.66), channel_id=1, replica_groups=mesh['yh'=2,'yl'=2,'zl'=4,'xh'=2,'xl'=2,'zh'=2,'c'=2] {'yh','zl','xh','x..., dimensions={0} | all-to-all | bytes 786432 | tf_op jit(solution)/shard_map/all_to_all | solution.py:234
  85.7 14.5 %shard_map.67 = (bf16[48,48,128]{2,1,0:T(8,128)(2,1)S(1)}, bf16[64,40,128]{2,1,0:T(8,128)(2,1)S(1)}) custom-call(bf16[48,48,128]{2,1,0:T(8,128)(2,1)S(1)} %copy-done.1, bf16[64,24,128]{2,1,0:T(8,128)(2,1)S(1)} %all_to_all.20.mixed, f32[2,128]{1,0:T(2,128)S(1)} %copy-done.7, f32[2,64]{1,0:T(2,128)S(1)} %copy-done.8, bf16[2,64,128]{2,1,0:T(8,128)(2,1)S(1)} %copy-done.5, ...), custom_call_target="tpu_custom_call" | custom-call | tf_op jit(solution)/shard_map/pallas_call | solution.py:235
  100.2 27.3 %all_to_all.21.got = bf16[64,40,128]{2,1,0:T(8,128)(2,1)S(1)} all-to-all(bf16[64,40,128]{2,1,0:T(8,128)(2,1)S(1)} %get-tuple-element.16), channel_id=1, replica_groups=mesh['yh'=2,'yl'=2,'zl'=4,'xh'=2,'xl'=2,'zh'=2,'c'=2] {'yh','yl','zl','x..., dimensions={0} | all-to-all | bytes 1310720 | tf_op jit(solution)/shard_map/all_to_all | solution.py:238
  127.5 5.7 %shard_map.68 = (bf16[384,384]{1,0:T(8,128)(2,1)S(1)}, bf16[768,256]{1,0:T(8,128)(2,1)S(1)}) custom-call(bf16[64,40,128]{2,1,0:T(8,128)(2,1)S(1)} %all_to_all.21.got), custom_call_target="tpu_custom_call" | custom-call | tf_op jit(solution)/shard_map/pallas_call | solution.py:239
  133.2 0.1 collective-permute-start.6
  133.3 1.6 collective-permute-start.5
  134.9 0.3 collective-permute-start.4
  135.2 0.1 pad_add_fusion.me
  135.3 7.3 %collective-permute-done.6.left_d = bf16[384,384]{1,0:T(8,128)(2,1)S(1)} collective-permute-done((bf16[384,384]{1,0:T(8,128)(2,1)S(1)}, bf16[384,384]{1,0:T(8,128)(2,1)S(1)}, u32[]{:S(2)}, u32[]{:S(2)}) %collective-permute-start.6) | collective-permute-done | bytes 294944 | tf_op jit(solution)/shard_map/ppermute | solution.py:205
  142.6 6.3 %collective-permute-done.5.left_x = bf16[384,384]{1,0:T(8,128)(2,1)S(1)} collective-permute-done((bf16[384,384]{1,0:T(8,128)(2,1)S(1)}, bf16[384,384]{1,0:T(8,128)(2,1)S(1)}, u32[]{:S(2)}, u32[]{:S(2)}) %collective-permute-start.5) | collective-permute-done | bytes 294944 | tf_op jit(solution)/shard_map/ppermute | solution.py:205
  149.0 1.8 %shard_map.69 = bf16[64,24,128]{2,1,0:T(8,128)(2,1)S(1)} custom-call(bf16[768,256]{1,0:T(8,128)(2,1)S(1)} %get-tuple-element.17.right, bf16[384,384]{1,0:T(8,128)(2,1)S(1)} %get-tuple-element.18.left, bf16[384,384]{1,0:T(8,128)(2,1)S(1)} %collective-permute-done.4.left_c, bf16[384,384]{1,0:T(8,128)(2,1)S(1)} %collective-permute-done.5.left_x, ...), custom_call_target="tpu_custom_call" | custom-call | tf_op jit(solution)/shard_map/pallas_call | solution.py:240
  150.8 22.2 %all_to_all.22.mixed = bf16[64,24,128]{2,1,0:T(8,128)(2,1)S(1)} all-to-all(bf16[64,24,128]{2,1,0:T(8,128)(2,1)S(1)} %shard_map.69), channel_id=1, replica_groups=mesh['yh'=2,'yl'=2,'zl'=4,'xh'=2,'xl'=2,'zh'=2,'c'=2] {'yh','yl','zl','x..., dimensions={0} | all-to-all | bytes 786432 | tf_op jit(solution)/shard_map/all_to_all | solution.py:248
  173.0 3.4 %shard_map.70 = bf16[48,48,128]{2,1,0:T(8,128)(2,1)} custom-call(bf16[48,48,128]{2,1,0:T(8,128)(2,1)S(1)} %get-tuple-element.15.pair, bf16[64,24,128]{2,1,0:T(8,128)(2,1)S(1)} %all_to_all.22.mixed, f32[2,128]{1,0:T(2,128)S(1)} %copy-done.7, f32[2,64]{1,0:T(2,128)S(1)} %copy-done.8, bf16[2,64,128]{2,1,0:T(8,128)(2,1)S(1)} %copy-done.5, ...), custom_call_target="tpu_custom_call" | custom-call | tf_op jit(solution)/shard_map/pallas_call | solution.py:249
  (13 shorter events, 0.0 us)
Async XLA Ops:
  0.0 1.1 copy-start
  1.1 0.9 copy-start.2
  2.0 0.7 copy-start.6
  11.5 36.1 %all-to-all-start = ((bf16[64,40,128]{2,1,0:T(8,128)(2,1)}), bf16[64,40,128]{2,1,0:T(8,128)(2,1)S(1)}, u32[]{:S(2)}, u32[]{:S(2)}) async-start(bf16[64,40,128]{2,1,0:T(8,128)(2,1)} %shard_map.64), calls=%async_computation | async-start | bytes 1310720 | tf_op jit(solution)/shard_map/all_to_all | solution.py:221
  52.9 9.1 %collective-permute-start = (bf16[384,384]{1,0:T(8,128)(2,1)S(1)}, bf16[384,384]{1,0:T(8,128)(2,1)S(1)}, u32[]{:S(2)}, u32[]{:S(2)}) collective-permute-start(bf16[384,384]{1,0:T(8,128)(2,1)S(1)} %get-tuple-element.12.left), channel_id=1, source_target_pairs={{0,1},{1,0},{2,3},{3,2},{4,5},{5,4},{6,7},{7,6},{8,9},{9,8},{10,11... | collective-permute-start | bytes 884744 | tf_op jit(solution)/shard_map/ppermute | solution.py:205
  53.0 6.7 %collective-permute-start.2 = (bf16[192,384]{1,0:T(8,128)(2,1)S(1)}, bf16[192,384]{1,0:T(8,128)(2,1)S(1)}, u32[]{:S(2)}, u32[]{:S(2)}) collective-permute-start(bf16[192,384]{1,0:T(8,128)(2,1)S(1)} %get-tuple-element.13.kept), channel_id=1, source_target_pairs={{0,64},{64,0},{1,65},{65,1},{2,66},{66,2},{3,67},{67,3},{4,68},{68... | collective-permute-start | bytes 442376 | tf_op jit(solution)/shard_map/ppermute | solution.py:205
  53.8 8.2 %collective-permute-start.3 = (bf16[192,384]{1,0:T(8,128)(2,1)S(1)}, bf16[192,384]{1,0:T(8,128)(2,1)S(1)}, u32[]{:S(2)}, u32[]{:S(2)}) collective-permute-start(bf16[192,384]{1,0:T(8,128)(2,1)S(1)} %get-tuple-element.14), channel_id=1, source_target_pairs={{0,65},{1,64},{64,1},{65,0},{2,67},{3,66},{66,3},{67,2},{4,69},{5,... | collective-permute-start | bytes 442376 | tf_op jit(solution)/shard_map/ppermute | solution.py:205
  54.9 7.1 %collective-permute-start.1 = (bf16[192,384]{1,0:T(8,128)(2,1)S(1)}, bf16[192,384]{1,0:T(8,128)(2,1)S(1)}, u32[]{:S(2)}, u32[]{:S(2)}) collective-permute-start(bf16[192,384]{1,0:T(8,128)(2,1)S(1)} %get-tuple-element.14), channel_id=1, source_target_pairs={{0,1},{1,0},{2,3},{3,2},{4,5},{5,4},{6,7},{7,6},{8,9},{9,8},{10,11... | collective-permute-start | bytes 442376 | tf_op jit(solution)/shard_map/ppermute | solution.py:205
  62.0 23.7 %copy-start.5 = (bf16[2,64,128]{2,1,0:T(8,128)(2,1)S(1)}, bf16[2,64,128]{2,1,0:T(8,128)(2,1)}, u32[]{:S(2)}) copy-start(bf16[2,64,128]{2,1,0:T(8,128)(2,1)} %oweight.3) | copy-start | bytes 98308
  62.0 23.7 %copy-start.7 = (f32[2,128]{1,0:T(2,128)S(1)}, f32[2,128]{1,0:T(2,128)}, u32[]{:S(2)}) copy-start(f32[2,128]{1,0:T(2,128)} %gain.5) | copy-start | bytes 3076
  62.0 23.7 %copy-start.8 = (f32[2,64]{1,0:T(2,128)S(1)}, f32[2,64]{1,0:T(2,128)}, u32[]{:S(2)}) copy-start(f32[2,64]{1,0:T(2,128)} %hgain.3) | copy-start | bytes 1540
  62.7 23.0 %copy-start.1 = (bf16[48,48,128]{2,1,0:T(8,128)(2,1)S(1)}, bf16[48,48,128]{2,1,0:T(8,128)(2,1)}, u32[]{:S(2)}) copy-start(bf16[48,48,128]{2,1,0:T(8,128)(2,1)} %pair.3) | copy-start | bytes 1769476
  62.7 23.0 %copy-start.3 = (bf16[2,128,256]{2,1,0:T(8,128)(2,1)S(1)}, bf16[2,128,256]{2,1,0:T(8,128)(2,1)}, u32[]{:S(2)}) copy-start(bf16[2,128,256]{2,1,0:T(8,128)(2,1)} %weight.3) | copy-start | bytes 393220
  62.7 23.0 %copy-start.4 = (bf16[2,128,128]{2,1,0:T(8,128)(2,1)S(1)}, bf16[2,128,128]{2,1,0:T(8,128)(2,1)}, u32[]{:S(2)}) copy-start(bf16[2,128,128]{2,1,0:T(8,128)(2,1)} %gweight.3) | copy-start | bytes 196612
  133.2 9.4 %collective-permute-start.6 = (bf16[384,384]{1,0:T(8,128)(2,1)S(1)}, bf16[384,384]{1,0:T(8,128)(2,1)S(1)}, u32[]{:S(2)}, u32[]{:S(2)}) collective-permute-start(bf16[384,384]{1,0:T(8,128)(2,1)S(1)} %get-tuple-element.18.left), channel_id=1, source_target_pairs={{0,5},{1,4},{4,1},{5,0},{2,7},{3,6},{6,3},{7,2},{8,13},{9,12},{12,... | collective-permute-start | bytes 884744 | tf_op jit(solution)/shard_map/ppermute | solution.py:205
  133.3 15.6 %collective-permute-start.5 = (bf16[384,384]{1,0:T(8,128)(2,1)S(1)}, bf16[384,384]{1,0:T(8,128)(2,1)S(1)}, u32[]{:S(2)}, u32[]{:S(2)}) collective-permute-start(bf16[384,384]{1,0:T(8,128)(2,1)S(1)} %get-tuple-element.18.left), channel_id=1, source_target_pairs={{0,4},{4,0},{1,5},{5,1},{2,6},{6,2},{3,7},{7,3},{8,12},{12,8},{9,1... | collective-permute-start | bytes 884744 | tf_op jit(solution)/shard_map/ppermute | solution.py:205
  134.9 14.1 %collective-permute-start.4 = (bf16[384,384]{1,0:T(8,128)(2,1)S(1)}, bf16[384,384]{1,0:T(8,128)(2,1)S(1)}, u32[]{:S(2)}, u32[]{:S(2)}) collective-permute-start(bf16[384,384]{1,0:T(8,128)(2,1)S(1)} %get-tuple-element.18.left), channel_id=1, source_target_pairs={{0,1},{1,0},{2,3},{3,2},{4,5},{5,4},{6,7},{7,6},{8,9},{9,8},{10,11... | collective-permute-start | bytes 884744 | tf_op jit(solution)/shard_map/ppermute | solution.py:205

commit v3 on v2

v3 whole, which is shorter than its diff:
```python
import jax
import jax.numpy as jnp
from jax import lax
from jax.experimental import pallas as pl
from jax.experimental.pallas import tpu as pltpu
from jax.sharding import Mesh
from jax.sharding import PartitionSpec as P

F32, BF16 = jnp.float32, jnp.bfloat16
SIDE = 48
HALF = SIDE // 2
SLOT = 64
MAIN = 40
EXTRA = SIDE - MAIN
STRIDE = 72
GROUP = 8
PIECE = 16
CH = 64
LANES = 128
EPS = 1e-05
NT = (((1,), (1,)), ((), ()))
TN = (((0,), (0,)), ((), ()))
VMEM = pl.BlockSpec(memory_space=pltpu.VMEM)
SMEM = pl.BlockSpec(memory_space=pltpu.SMEM)


def call(kernel, outs, n_in, scratch=(), smem=0):
    return pl.pallas_call(
        kernel,
        out_shape=[jax.ShapeDtypeStruct(shape, BF16) for shape in outs],
        in_specs=[VMEM] * n_in + [SMEM] * smem,
        out_specs=[VMEM] * len(outs),
        scratch_shapes=scratch,
        compiler_params=pltpu.CompilerParams(vmem_limit_bytes=16 * 1024 * 1024),
    )


def lane_of(rows):
    return lax.broadcasted_iota(jnp.int32, (rows, LANES), 1)


def layer_norm(values, gain, axis):
    mean = jnp.mean(values, axis=axis, keepdims=True)
    centred = values - mean
    var = jnp.mean(centred * centred, axis=axis, keepdims=True)
    return centred * lax.rsqrt(var + EPS) * gain


def sigmoid(values):
    return 0.5 * jnp.tanh(0.5 * values) + 0.5


def normalize(block, gain, normed):
    pad = jnp.zeros((SLOT - SIDE, LANES), BF16)
    for start in range(0, SIDE, GROUP):
        rows = layer_norm(block[start : start + GROUP].astype(F32), gain.reshape(1, 1, LANES), 2)
        rows = rows.astype(BF16)
        for i in range(GROUP):
            base = place_of(start + i)
            normed[base : base + SIDE, :] = rows[i]
            normed[base + SIDE : base + SLOT, :] = pad


def place_of(i):
    return (i % HALF) * LANES + (i // HALF) * SLOT


def project(normed, weight, staged, extra):
    wt = weight.astype(F32).T.astype(BF16)
    lane = lane_of(CH)
    for s in ORDER:
        proj = lax.dot_general(wt, normed[s * LANES : (s + 1) * LANES, :], NT, preferred_element_type=F32)
        left = sigmoid(proj[:CH]) * proj[CH : 2 * CH]
        right = sigmoid(proj[2 * CH : 3 * CH]) * proj[3 * CH :]
        first = jnp.where(lane < SLOT, left, pltpu.roll(right, SLOT, 1))
        second = jnp.where(lane < SLOT, pltpu.roll(left, SLOT, 1), right)
        if s + HALF >= MAIN:
            for g in range(SIDE // PIECE):
                extra[g * EXTRA + s + HALF - MAIN] = pltpu.roll(second, SIDE - g * PIECE, 1)
        else:
            staged[pl.ds((s + HALF) * STRIDE, CH), :] = second
        staged[pl.ds(s * STRIDE, CH), :] = jnp.where(lane % SLOT < SIDE, first, extra[s])


ORDER = [*range(HALF - EXTRA, HALF), *range(HALF - EXTRA)]


def write_messages(staged, out):
    for channel in range(CH):
        out[channel] = staged[pl.ds(channel, MAIN, stride=STRIDE), :].astype(BF16)


def project_kernel(pair, gain, weight, out, normed, staged, extra):
    normalize(pair, gain[0:1, :], normed)
    project(normed, weight[0], staged, extra)
    write_messages(staged, out)


def read_sums(mixed, mixed32):
    for channel in range(CH):
        mixed32[pl.ds(channel * HALF, HALF), :] = mixed[channel].astype(F32)


def finish(pair, normed, mixed, hgain, oweight, gweight, z_out, mixed32, hidden):
    hcol = hgain.T
    read_sums(mixed, mixed32)
    for s in range(0, HALF, 4):
        sums = [mixed32[pl.ds(s + t, CH, stride=HALF), :] for t in range(4)]
        sums = [layer_norm(values, hcol, 0).astype(BF16) for values in sums]
        for t in range(4):
            hidden[s + t] = sums[t]
    for s in range(0, HALF, 4):
        rows = slice(s * LANES, (s + 4) * LANES)
        gate = sigmoid(jnp.dot(normed[rows, :], gweight, preferred_element_type=F32))
        updates = [
            lax.dot_general(hidden[s + t], oweight, TN, preferred_element_type=F32) for t in range(4)
        ]
        change = gate * jnp.concatenate(updates, axis=0)
        for h in range(2):
            old = [pair[s + t + h * HALF].astype(F32) for t in range(4)]
            new = [
                old[t] + change[t * LANES + h * SLOT : t * LANES + h * SLOT + SIDE] for t in range(4)
            ]
            for t in range(4):
                z_out[s + t + h * HALF] = new[t].astype(BF16)


def middle_kernel(
    pair, mixed, gain, hgain, oweight, gweight, weight, z_out, out, normed, mixed32, hidden, staged, extra
):
    normalize(pair, gain[0:1, :], normed)
    finish(pair, normed, mixed, hgain[0:1, :], oweight[0], gweight[0], z_out, mixed32, hidden)
    normalize(z_out, gain[1:2, :], normed)
    project(normed, weight[1], staged, extra)
    write_messages(staged, out)


def last_kernel(pair, mixed, gain, hgain, oweight, gweight, z_out, normed, mixed32, hidden):
    normalize(pair, gain[1:2, :], normed)
    finish(pair, normed, mixed, hgain[1:2, :], oweight[1], gweight[1], z_out, mixed32, hidden)


def moved(ref, p, base, offset):
    values = ref[p].astype(F32)
    lane = lane_of(EXTRA)
    tail = None
    for g in range(SIDE // PIECE):
        begin = offset + g * PIECE
        part = values[g * EXTRA : (g + 1) * EXTRA]
        shift = (begin - base - SIDE) % LANES
        part = pltpu.roll(part, shift, 1) if shift else part
        tail = part if tail is None else jnp.where((lane - begin) % LANES < PIECE, part, tail)
    shift = (offset - base) % LANES
    main = pltpu.roll(values, shift, 1) if shift else values
    return jnp.concatenate([main, tail], axis=0)


def dense(ref, which, base):
    lane = lane_of(SIDE)
    tiles = [None] * 3
    for b, p in enumerate(which):
        first, offset = divmod(b * SIDE, LANES)
        block = moved(ref, p, base, offset)
        tiles[first] = block if offset == 0 else jnp.where(lane < offset, tiles[first], block)
        if offset + SIDE > LANES:
            tiles[first + 1] = block
    return jnp.concatenate(tiles, axis=1).astype(BF16)


def split_out_kernel(got, me, left, kept, given):
    for a in range(8):
        left[a * SIDE : (a + 1) * SIDE, :] = dense(got, [a * 8 + b for b in range(8)], 0)
    for a in range(4):
        rows = slice(a * SIDE, (a + 1) * SIDE)
        mine, other = (2 * a + me[0]) * 8, (2 * a + 1 - me[0]) * 8
        kept[rows, :] = dense(got, [mine + b for b in range(8)], SLOT)
        given[rows, :] = dense(got, [other + b for b in range(8)], SLOT)


def send_back(total, blocks, place, out):
    lane = lane_of(HALF)
    for a in range(blocks):
        for b in range(0, 4, 2):
            tile = total[a * SIDE : (a + 1) * SIDE, b * SLOT : (b + 2) * SLOT]
            low, high = tile[:HALF], tile[HALF:]
            out[place(a, b)] = jnp.where(lane < SLOT, low, pltpu.roll(high, SLOT, 1)).astype(BF16)
            out[place(a, b + 1)] = jnp.where(lane < SLOT, pltpu.roll(low, SLOT, 1), high).astype(BF16)


def padded(ref):
    pad = jnp.zeros((SLOT - SIDE, ref.shape[1]), BF16)
    pieces = []
    for b in range(4):
        pieces += [ref[b * SIDE : (b + 1) * SIDE, :], pad]
    return jnp.concatenate(pieces, axis=0)


def mix_out_kernel(left, left_c, kept, given_c, kept_y, given_d, me, out):
    for step, (near, far) in enumerate(((kept, given_c), (kept_y, given_d))):
        total = lax.dot_general(left[...], padded(near), NT, preferred_element_type=F32)
        total += lax.dot_general(left_c[...], padded(far), NT, preferred_element_type=F32)
        owner = me[0] if step == 0 else 1 - me[0]
        send_back(total, 8, lambda a, b: a * 8 + (2 * (b // 2) + owner) * 2 + b % 2, out)


def split_in_kernel(got, left, right):
    for r in range(8):
        rows = slice(r * SIDE, (r + 1) * SIDE)
        left[rows, :] = dense(got, [(r + 8 * h) * 4 + b for h in range(2) for b in range(4)], 0)
    lane = lane_of(SIDE)
    for r in range(16):
        for b in range(0, 4, 2):
            low, high = moved(got, r * 4 + b, SLOT, 0), moved(got, r * 4 + b + 1, SLOT, SLOT)
            tile = jnp.where(lane < SLOT, low, high)
            right[r * SIDE : (r + 1) * SIDE, b * SLOT : (b + 2) * SLOT] = tile.astype(BF16)


def mix_in_kernel(right, left, left_c, left_x, left_d, me, out):
    for step, ref in enumerate((left, left_c, left_x, left_d)):
        total = lax.dot_general(ref[:, :192], right[:384, :], TN, preferred_element_type=F32)
        total += lax.dot_general(ref[:, 192:], right[384:, :], TN, preferred_element_type=F32)
        core = me[1] if step % 2 == 0 else 1 - me[1]
        low = me[0] if step < 2 else 1 - me[0]
        send_back(
            total,
            4,
            lambda a, b: (2 * (a // 2) + low) * 16 + (2 * (a % 2) + core) * 4 + b,
            out,
        )


def swap(values, *axes):
    n = 1 << len(axes)
    return lax.ppermute(values, axes, [(i, n - 1 - i) for i in range(n)])


MESSAGE = (CH, MAIN, LANES)
BACK = (CH, HALF, LANES)
BLOCK = (SIDE, SIDE, LANES)


def body(pair, norm_gain, proj_weight, hid_gain, out_weight, gate_weight):
    normed = pltpu.VMEM((HALF * LANES, LANES), BF16)
    staged = pltpu.VMEM((MAIN * STRIDE, LANES), F32)
    extra = pltpu.VMEM((HALF, CH, LANES), F32)
    mixed32 = pltpu.VMEM((CH * HALF, LANES), F32)
    hidden = pltpu.VMEM((HALF, CH, LANES), BF16)
    out_axes, in_axes = ("yh", "zl", "xh", "xl", "zh"), ("yh", "yl", "zl", "xh", "zh")
    core = lax.axis_index("c")

    (sent,) = call(project_kernel, [MESSAGE], 3, [normed, staged, extra])(pair, norm_gain, proj_weight)
    got = lax.all_to_all(sent, out_axes, 0, 0, tiled=True)
    left, kept, given = call(split_out_kernel, [(384, 384), (192, 384), (192, 384)], 1, smem=1)(
        got, core.reshape(1)
    )
    (sent,) = call(mix_out_kernel, [BACK], 6, smem=1)(
        left,
        swap(left, "c"),
        kept,
        swap(given, "c"),
        swap(kept, "yl"),
        swap(given, "yl", "c"),
        lax.axis_index("yl").reshape(1),
    )
    mixed = lax.all_to_all(sent, out_axes, 0, 0, tiled=True)
    first, sent = call(middle_kernel, [BLOCK, MESSAGE], 7, [normed, mixed32, hidden, staged, extra])(
        pair, mixed, norm_gain, hid_gain, out_weight, gate_weight, proj_weight
    )
    got = lax.all_to_all(sent, in_axes, 0, 0, tiled=True)
    left, right = call(split_in_kernel, [(384, 384), (768, 256)], 1)(got)
    left_x = swap(left, "xl")
    (sent,) = call(mix_in_kernel, [BACK], 5, smem=1)(
        right,
        left,
        swap(left, "c"),
        left_x,
        swap(left_x, "c"),
        jnp.stack([lax.axis_index("xl"), core]),
    )
    mixed = lax.all_to_all(sent, in_axes, 0, 0, tiled=True)
    (updated,) = call(last_kernel, [BLOCK], 6, [normed, mixed32, hidden])(
        first, mixed, norm_gain, hid_gain, out_weight, gate_weight
    )
    return updated


def solution(mesh):
    names = ("yh", "yl", "zl", "xh", "xl", "zh", "c")
    fine = Mesh(mesh.devices.reshape(2, 2, 4, 2, 2, 2, 2), names)
    spec = P(names[:3], names[3:], None)
    return jax.shard_map(
        body,
        mesh=fine,
        in_specs=(spec, P(), P(), P(), P(), P()),
        out_specs=spec,
        check_vma=False,
    )
```

time: 177 us -> 145 us (0.82)
  Pallas kernels: 40.2 us -> 13.6 us
  waiting for transfers between devices: 41.9 us -> 35 us
  blocking collectives: 72.5 us -> 74.3 us
    pallas_call x3, Pallas kernels: 26.7 us -> 10.1 us  [the longest x1 4.35 us: body(): call(middle_kernel, [BLOCK, MESSAGE], 7, [normed, mixed32, hidden, staged...]
    ppermute x7, waiting for transfers between devices: 20.4 us -> 13.5 us  [swap(): return lax.ppermute(values, axes, [(i, n - 1 - i) for i in range(n)])]
    pallas_call x1, Pallas kernels: 5.72 us -> 0.49 us  [body(): left, right = call(split_in_kernel, [(384, 384), (768, 256)], 1)(got)]
    pallas_call x1, Pallas kernels: 5.3 us -> 0.54 us  [body(): call(split_out_kernel, [(384, 384), (192, 384), (192, 384)], 1, smem=1)]
    all_to_all x1, blocking collectives: 22.2 us -> 24 us  [body(): mixed = lax.all_to_all(sent, in_axes, 0, 0, tiled=True)]
where the time goes in v3:
time: 145 us; the launch traced here: 144 us
  blocking collectives  74.3 us (51%)
  waiting for transfers between devices  35 us (24%)
  starting transfers between devices  18.5 us (13%)
  Pallas kernels  13.6 us (9%)
  local copies, waits for them, and re-layouts  2.68 us (2%)
    all_to_all x1, blocking collectives, body(): got = lax.all_to_all(sent, in_axes, 0, 0, tiled=True)  27.3 us
    all_to_all x1, blocking collectives, body(): mixed = lax.all_to_all(sent, in_axes, 0, 0, tiled=True)  24 us
    all_to_all x1, blocking collectives, body(): mixed = lax.all_to_all(sent, out_axes, 0, 0, tiled=True)  23 us
    all_to_all x1, waiting for transfers between devices, body(): got = lax.all_to_all(sent, out_axes, 0, 0, tiled=True)  21.5 us
    all_to_all x1, starting transfers between devices, body(): got = lax.all_to_all(sent, out_axes, 0, 0, tiled=True)  14.6 us
    ppermute x7, waiting for transfers between devices, swap(): return lax.ppermute(values, axes, [(i, n - 1 - i) for i in range(n)])  13.5 us
    pallas_call x1, Pallas kernels, body(): call(middle_kernel, [BLOCK, MESSAGE], 7, [normed, mixed32, hidden, staged...  4.35 us
    ppermute x7, starting transfers between devices, swap(): return lax.ppermute(values, axes, [(i, n - 1 - i) for i in range(n)])  3.88 us
  transfers between devices with their start and end apart: 8, of which 5 were waited for; matrix products, arithmetic and copies ran while one was open for 0% of the time, Pallas kernels for 0%

profile of v3, /device:TPU:2, one launch (start us, length us, event | category | flops | bytes accessed | tf_op | source)
XLA Modules:
  0.0 144.3 jit_solution(13180704169973428802)
XLA Ops:
  0.0 1.1 copy-done
  1.1 0.9 copy-done.2
  2.0 0.7 copy-done.6
  2.6 3.2 %shard_map.64 = bf16[64,40,128]{2,1,0:T(8,128)(2,1)} custom-call(bf16[48,48,128]{2,1,0:T(8,128)(2,1)S(1)} %copy-done, f32[2,128]{1,0:T(2,128)S(1)} %copy-done.6, bf16[2,128,256]{2,1,0:T(8,128)(2,1)S(1)} %copy-done.2), custom_call_target="tpu_custom_call" | custom-call | tf_op jit(solution)/shard_map/pallas_call | solution.py:251
  5.9 14.6 %all-to-all-start = ((bf16[64,40,128]{2,1,0:T(8,128)(2,1)}), bf16[64,40,128]{2,1,0:T(8,128)(2,1)S(1)}, u32[]{:S(2)}, u32[]{:S(2)}) async-start(bf16[64,40,128]{2,1,0:T(8,128)(2,1)} %shard_map.64), calls=%async_computation | async-start | bytes 1310720 | tf_op jit(solution)/shard_map/all_to_all | solution.py:252
  20.5 21.5 %all-to-all-done.got = bf16[64,40,128]{2,1,0:T(8,128)(2,1)S(1)} async-done(((bf16[64,40,128]{2,1,0:T(8,128)(2,1)}), bf16[64,40,128]{2,1,0:T(8,128)(2,1)S(1)}, u32[]{:S(2)}, u32[]{:S(2)}) %all-to-all-start) | async-done | bytes 655392 | tf_op jit(solution)/shard_map/all_to_all | solution.py:252
  42.0 0.5 shard_map.65
  42.6 0.1 collective-permute-start
  42.7 0.8 collective-permute-start.2
  43.4 1.1 collective-permute-start.3
  44.5 0.4 collective-permute-start.1
  44.9 4.5 %collective-permute-done.2.kept_y = bf16[192,384]{1,0:T(8,128)(2,1)S(1)} collective-permute-done((bf16[192,384]{1,0:T(8,128)(2,1)S(1)}, bf16[192,384]{1,0:T(8,128)(2,1)S(1)}, u32[]{:S(2)}, u32[]{:S(2)}) %collective-permute-start.2) | collective-permute-done | bytes 147488 | tf_op jit(solution)/shard_map/ppermute | solution.py:234
  49.4 2.2 %collective-permute-done.3.given_d = bf16[192,384]{1,0:T(8,128)(2,1)S(1)} collective-permute-done((bf16[192,384]{1,0:T(8,128)(2,1)S(1)}, bf16[192,384]{1,0:T(8,128)(2,1)S(1)}, u32[]{:S(2)}, u32[]{:S(2)}) %collective-permute-start.3) | collective-permute-done | bytes 147488 | tf_op jit(solution)/shard_map/ppermute | solution.py:234
  51.6 0.0 copy-start.7
  51.6 0.0 copy-start.8
  51.6 0.7 shard_map.66
  52.3 0.0 copy-start.1
  52.4 0.0 copy-start.3
  52.4 0.0 copy-start.4
  52.4 23.0 %all_to_all.20.mixed = bf16[64,24,128]{2,1,0:T(8,128)(2,1)S(1)} all-to-all(bf16[64,24,128]{2,1,0:T(8,128)(2,1)S(1)} %shard_map.66), channel_id=1, replica_groups=mesh['yh'=2,'yl'=2,'zl'=4,'xh'=2,'xl'=2,'zh'=2,'c'=2] {'yh','zl','xh','x..., dimensions={0} | all-to-all | bytes 786432 | tf_op jit(solution)/shard_map/all_to_all | solution.py:265
  75.4 4.4 %shard_map.67 = (bf16[48,48,128]{2,1,0:T(8,128)(2,1)S(1)}, bf16[64,40,128]{2,1,0:T(8,128)(2,1)S(1)}) custom-call(bf16[48,48,128]{2,1,0:T(8,128)(2,1)S(1)} %copy-done.1, bf16[64,24,128]{2,1,0:T(8,128)(2,1)S(1)} %all_to_all.20.mixed, f32[2,128]{1,0:T(2,128)S(1)} %copy-done.7, f32[2,64]{1,0:T(2,128)S(1)} %copy-done.8, bf16[2,64,128]{2,1,0:T(8,128)(2,1)S(1)} %copy-done.5, ...), custom_call_target="tpu_custom_call" | custom-call | tf_op jit(solution)/shard_map/pallas_call | solution.py:266
  79.7 27.3 %all_to_all.21.got = bf16[64,40,128]{2,1,0:T(8,128)(2,1)S(1)} all-to-all(bf16[64,40,128]{2,1,0:T(8,128)(2,1)S(1)} %get-tuple-element.16), channel_id=1, replica_groups=mesh['yh'=2,'yl'=2,'zl'=4,'xh'=2,'xl'=2,'zh'=2,'c'=2] {'yh','yl','zl','x..., dimensions={0} | all-to-all | bytes 1310720 | tf_op jit(solution)/shard_map/all_to_all | solution.py:269
  107.1 0.5 shard_map.68
  107.6 1.5 %collective-permute-start.5 = (bf16[384,384]{1,0:T(8,128)(2,1)S(1)}, bf16[384,384]{1,0:T(8,128)(2,1)S(1)}, u32[]{:S(2)}, u32[]{:S(2)}) collective-permute-start(bf16[384,384]{1,0:T(8,128)(2,1)S(1)} %get-tuple-element.18.left), channel_id=1, source_target_pairs={{0,4},{4,0},{1,5},{5,1},{2,6},{6,2},{3,7},{7,3},{8,12},{12,8},{9,1... | collective-permute-start | bytes 884744 | tf_op jit(solution)/shard_map/ppermute | solution.py:234
  109.1 0.0 collective-permute-start.4
  109.1 5.3 %collective-permute-done.5.left_x = bf16[384,384]{1,0:T(8,128)(2,1)S(1)} collective-permute-done((bf16[384,384]{1,0:T(8,128)(2,1)S(1)}, bf16[384,384]{1,0:T(8,128)(2,1)S(1)}, u32[]{:S(2)}, u32[]{:S(2)}) %collective-permute-start.5) | collective-permute-done | bytes 294944 | tf_op jit(solution)/shard_map/ppermute | solution.py:234
  114.4 0.0 collective-permute-start.6
  114.4 0.1 pad_add_fusion.me
  114.4 1.5 %collective-permute-done.6.left_d = bf16[384,384]{1,0:T(8,128)(2,1)S(1)} collective-permute-done((bf16[384,384]{1,0:T(8,128)(2,1)S(1)}, bf16[384,384]{1,0:T(8,128)(2,1)S(1)}, u32[]{:S(2)}, u32[]{:S(2)}) %collective-permute-start.6) | collective-permute-done | bytes 294944 | tf_op jit(solution)/shard_map/ppermute | solution.py:234
  115.9 1.8 %shard_map.69 = bf16[64,24,128]{2,1,0:T(8,128)(2,1)S(1)} custom-call(bf16[768,256]{1,0:T(8,128)(2,1)S(1)} %get-tuple-element.17.right, bf16[384,384]{1,0:T(8,128)(2,1)S(1)} %get-tuple-element.18.left, bf16[384,384]{1,0:T(8,128)(2,1)S(1)} %collective-permute-done.4.left_c, bf16[384,384]{1,0:T(8,128)(2,1)S(1)} %collective-permute-done.5.left_x, ...), custom_call_target="tpu_custom_call" | custom-call | tf_op jit(solution)/shard_map/pallas_call | solution.py:272
  117.7 24.0 %all_to_all.22.mixed = bf16[64,24,128]{2,1,0:T(8,128)(2,1)S(1)} all-to-all(bf16[64,24,128]{2,1,0:T(8,128)(2,1)S(1)} %shard_map.69), channel_id=1, replica_groups=mesh['yh'=2,'yl'=2,'zl'=4,'xh'=2,'xl'=2,'zh'=2,'c'=2] {'yh','yl','zl','x..., dimensions={0} | all-to-all | bytes 786432 | tf_op jit(solution)/shard_map/all_to_all | solution.py:280
  141.8 2.5 %shard_map.70 = bf16[48,48,128]{2,1,0:T(8,128)(2,1)} custom-call(bf16[48,48,128]{2,1,0:T(8,128)(2,1)S(1)} %get-tuple-element.15.pair, bf16[64,24,128]{2,1,0:T(8,128)(2,1)S(1)} %all_to_all.22.mixed, f32[2,128]{1,0:T(2,128)S(1)} %copy-done.7, f32[2,64]{1,0:T(2,128)S(1)} %copy-done.8, bf16[2,64,128]{2,1,0:T(8,128)(2,1)S(1)} %copy-done.5, ...), custom_call_target="tpu_custom_call" | custom-call | tf_op jit(solution)/shard_map/pallas_call | solution.py:281
  (13 shorter events, 0.0 us)
Async XLA Ops:
  0.0 1.1 copy-start
  1.1 0.9 copy-start.2
  2.0 0.7 copy-start.6
  5.9 36.1 %all-to-all-start = ((bf16[64,40,128]{2,1,0:T(8,128)(2,1)}), bf16[64,40,128]{2,1,0:T(8,128)(2,1)S(1)}, u32[]{:S(2)}, u32[]{:S(2)}) async-start(bf16[64,40,128]{2,1,0:T(8,128)(2,1)} %shard_map.64), calls=%async_computation | async-start | bytes 1310720 | tf_op jit(solution)/shard_map/all_to_all | solution.py:252
  42.6 9.1 %collective-permute-start = (bf16[384,384]{1,0:T(8,128)(2,1)S(1)}, bf16[384,384]{1,0:T(8,128)(2,1)S(1)}, u32[]{:S(2)}, u32[]{:S(2)}) collective-permute-start(bf16[384,384]{1,0:T(8,128)(2,1)S(1)} %get-tuple-element.12.left), channel_id=1, source_target_pairs={{0,1},{1,0},{2,3},{3,2},{4,5},{5,4},{6,7},{7,6},{8,9},{9,8},{10,11... | collective-permute-start | bytes 884744 | tf_op jit(solution)/shard_map/ppermute | solution.py:234
  42.7 6.7 %collective-permute-start.2 = (bf16[192,384]{1,0:T(8,128)(2,1)S(1)}, bf16[192,384]{1,0:T(8,128)(2,1)S(1)}, u32[]{:S(2)}, u32[]{:S(2)}) collective-permute-start(bf16[192,384]{1,0:T(8,128)(2,1)S(1)} %get-tuple-element.13.kept), channel_id=1, source_target_pairs={{0,64},{64,0},{1,65},{65,1},{2,66},{66,2},{3,67},{67,3},{4,68},{68... | collective-permute-start | bytes 442376 | tf_op jit(solution)/shard_map/ppermute | solution.py:234
  43.4 8.2 %collective-permute-start.3 = (bf16[192,384]{1,0:T(8,128)(2,1)S(1)}, bf16[192,384]{1,0:T(8,128)(2,1)S(1)}, u32[]{:S(2)}, u32[]{:S(2)}) collective-permute-start(bf16[192,384]{1,0:T(8,128)(2,1)S(1)} %get-tuple-element.14), channel_id=1, source_target_pairs={{0,65},{1,64},{64,1},{65,0},{2,67},{3,66},{66,3},{67,2},{4,69},{5,... | collective-permute-start | bytes 442376 | tf_op jit(solution)/shard_map/ppermute | solution.py:234
  44.5 7.1 %collective-permute-start.1 = (bf16[192,384]{1,0:T(8,128)(2,1)S(1)}, bf16[192,384]{1,0:T(8,128)(2,1)S(1)}, u32[]{:S(2)}, u32[]{:S(2)}) collective-permute-start(bf16[192,384]{1,0:T(8,128)(2,1)S(1)} %get-tuple-element.14), channel_id=1, source_target_pairs={{0,1},{1,0},{2,3},{3,2},{4,5},{5,4},{6,7},{7,6},{8,9},{9,8},{10,11... | collective-permute-start | bytes 442376 | tf_op jit(solution)/shard_map/ppermute | solution.py:234
  51.6 23.7 %copy-start.5 = (bf16[2,64,128]{2,1,0:T(8,128)(2,1)S(1)}, bf16[2,64,128]{2,1,0:T(8,128)(2,1)}, u32[]{:S(2)}) copy-start(bf16[2,64,128]{2,1,0:T(8,128)(2,1)} %oweight.3) | copy-start | bytes 98308
  51.6 23.7 %copy-start.7 = (f32[2,128]{1,0:T(2,128)S(1)}, f32[2,128]{1,0:T(2,128)}, u32[]{:S(2)}) copy-start(f32[2,128]{1,0:T(2,128)} %gain.5) | copy-start | bytes 3076
  51.6 23.7 %copy-start.8 = (f32[2,64]{1,0:T(2,128)S(1)}, f32[2,64]{1,0:T(2,128)}, u32[]{:S(2)}) copy-start(f32[2,64]{1,0:T(2,128)} %hgain.3) | copy-start | bytes 1540
  52.3 23.0 %copy-start.1 = (bf16[48,48,128]{2,1,0:T(8,128)(2,1)S(1)}, bf16[48,48,128]{2,1,0:T(8,128)(2,1)}, u32[]{:S(2)}) copy-start(bf16[48,48,128]{2,1,0:T(8,128)(2,1)} %pair.3) | copy-start | bytes 1769476
  52.4 23.0 %copy-start.3 = (bf16[2,128,256]{2,1,0:T(8,128)(2,1)S(1)}, bf16[2,128,256]{2,1,0:T(8,128)(2,1)}, u32[]{:S(2)}) copy-start(bf16[2,128,256]{2,1,0:T(8,128)(2,1)} %weight.3) | copy-start | bytes 393220
  52.4 23.0 %copy-start.4 = (bf16[2,128,128]{2,1,0:T(8,128)(2,1)S(1)}, bf16[2,128,128]{2,1,0:T(8,128)(2,1)}, u32[]{:S(2)}) copy-start(bf16[2,128,128]{2,1,0:T(8,128)(2,1)} %gweight.3) | copy-start | bytes 196612
  107.6 6.8 %collective-permute-start.5 = (bf16[384,384]{1,0:T(8,128)(2,1)S(1)}, bf16[384,384]{1,0:T(8,128)(2,1)S(1)}, u32[]{:S(2)}, u32[]{:S(2)}) collective-permute-start(bf16[384,384]{1,0:T(8,128)(2,1)S(1)} %get-tuple-element.18.left), channel_id=1, source_target_pairs={{0,4},{4,0},{1,5},{5,1},{2,6},{6,2},{3,7},{7,3},{8,12},{12,8},{9,1... | collective-permute-start | bytes 884744 | tf_op jit(solution)/shard_map/ppermute | solution.py:234
  109.1 5.3 %collective-permute-start.4 = (bf16[384,384]{1,0:T(8,128)(2,1)S(1)}, bf16[384,384]{1,0:T(8,128)(2,1)S(1)}, u32[]{:S(2)}, u32[]{:S(2)}) collective-permute-start(bf16[384,384]{1,0:T(8,128)(2,1)S(1)} %get-tuple-element.18.left), channel_id=1, source_target_pairs={{0,1},{1,0},{2,3},{3,2},{4,5},{5,4},{6,7},{7,6},{8,9},{9,8},{10,11... | collective-permute-start | bytes 884744 | tf_op jit(solution)/shard_map/ppermute | solution.py:234
  114.4 1.6 %collective-permute-start.6 = (bf16[384,384]{1,0:T(8,128)(2,1)S(1)}, bf16[384,384]{1,0:T(8,128)(2,1)S(1)}, u32[]{:S(2)}, u32[]{:S(2)}) collective-permute-start(bf16[384,384]{1,0:T(8,128)(2,1)S(1)} %collective-permute-done.5.left_x), channel_id=1, source_target_pairs={{0,1},{1,0},{2,3},{3,2},{4,5},{5,4},{6,7},{7,6},{8,9},{9,8},{10,11... | collective-permute-start | bytes 884744 | tf_op jit(solution)/shard_map/ppermute | solution.py:234

commit v4 on v3

--- a/solution.py
+++ b/solution.py
@@ -1,3 +1,5 @@
+import functools
+
 import jax
 import jax.numpy as jnp
 from jax import lax
@@ -22,16 +24,17 @@
 TN = (((0,), (0,)), ((), ()))
 VMEM = pl.BlockSpec(memory_space=pltpu.VMEM)
 SMEM = pl.BlockSpec(memory_space=pltpu.SMEM)
-
-
-def call(kernel, outs, n_in, scratch=(), smem=0):
+HBM = pl.BlockSpec(memory_space=pltpu.HBM)
+
+
+def call(kernel, outs, n_in, scratch=(), smem=0, inputs=VMEM, outputs=VMEM, dtype=BF16, limit=16 << 20):
     return pl.pallas_call(
         kernel,
-        out_shape=[jax.ShapeDtypeStruct(shape, BF16) for shape in outs],
-        in_specs=[VMEM] * n_in + [SMEM] * smem,
-        out_specs=[VMEM] * len(outs),
+        out_shape=[jax.ShapeDtypeStruct(shape, dtype) for shape in outs],
+        in_specs=[inputs] * n_in + [SMEM] * smem,
+        out_specs=[outputs] * len(outs),
         scratch_shapes=scratch,
-        compiler_params=pltpu.CompilerParams(vmem_limit_bytes=16 * 1024 * 1024),
+        compiler_params=pltpu.CompilerParams(vmem_limit_bytes=limit),
     )
 
 
@@ -50,9 +53,10 @@
     return 0.5 * jnp.tanh(0.5 * values) + 0.5
 
 
-def normalize(block, gain, normed):
+def normalize(block, gain, normed, arrive=lambda start: None):
     pad = jnp.zeros((SLOT - SIDE, LANES), BF16)
     for start in range(0, SIDE, GROUP):
+        arrive(start)
         rows = layer_norm(block[start : start + GROUP].astype(F32), gain.reshape(1, 1, LANES), 2)
         rows = rows.astype(BF16)
         for i in range(GROUP):
@@ -90,10 +94,27 @@
         out[channel] = staged[pl.ds(channel, MAIN, stride=STRIDE), :].astype(BF16)
 
 
-def project_kernel(pair, gain, weight, out, normed, staged, extra):
-    normalize(pair, gain[0:1, :], normed)
-    project(normed, weight[0], staged, extra)
+def project_kernel(pair_hbm, gain_hbm, weight_hbm, out, pair, gain, weight, sems, normed, staged, extra):
+    groups = SIDE // GROUP
+    copies = [pltpu.make_async_copy(gain_hbm, gain, sems.at[groups])]
+    for n in range(groups):
+        rows = pl.ds(n * GROUP, GROUP)
+        copies.append(pltpu.make_async_copy(pair_hbm.at[rows], pair.at[rows], sems.at[n]))
+    copies.append(pltpu.make_async_copy(weight_hbm.at[0], weight, sems.at[groups + 1]))
+    for copy in copies:
+        copy.start()
+    copies[0].wait()
+    normalize(pair, gain[0:1, :], normed, lambda start: copies[1 + start // GROUP].wait())
+    copies[-1].wait()
+    project(normed, weight[...], staged, extra)
     write_messages(staged, out)
+
+
+def gate_kernel(p, pair, gain, gweight, gate, normed):
+    normalize(pair, gain[p : p + 1, :], normed)
+    for start in range(0, HALF * LANES, 4 * LANES):
+        rows = slice(start, start + 4 * LANES)
+        gate[rows, :] = sigmoid(jnp.dot(normed[rows, :], gweight[p], preferred_element_type=F32))
 
 
 def read_sums(mixed, mixed32):
@@ -101,7 +122,7 @@
         mixed32[pl.ds(channel * HALF, HALF), :] = mixed[channel].astype(F32)
 
 
-def finish(pair, normed, mixed, hgain, oweight, gweight, z_out, mixed32, hidden):
+def finish(pair, gate, mixed, hgain, oweight, z_out, mixed32, hidden, ready=lambda s: None):
     hcol = hgain.T
     read_sums(mixed, mixed32)
     for s in range(0, HALF, 4):
@@ -110,12 +131,10 @@
         for t in range(4):
             hidden[s + t] = sums[t]
     for s in range(0, HALF, 4):
-        rows = slice(s * LANES, (s + 4) * LANES)
-        gate = sigmoid(jnp.dot(normed[rows, :], gweight, preferred_element_type=F32))
         updates = [
             lax.dot_general(hidden[s + t], oweight, TN, preferred_element_type=F32) for t in range(4)
         ]
-        change = gate * jnp.concatenate(updates, axis=0)
+        change = gate[s * LANES : (s + 4) * LANES, :] * jnp.concatenate(updates, axis=0)
         for h in range(2):
             old = [pair[s + t + h * HALF].astype(F32) for t in range(4)]
             new = [
@@ -123,21 +142,29 @@
             ]
             for t in range(4):
                 z_out[s + t + h * HALF] = new[t].astype(BF16)
+            ready(s + h * HALF)
 
 
 def middle_kernel(
-    pair, mixed, gain, hgain, oweight, gweight, weight, z_out, out, normed, mixed32, hidden, staged, extra
+    pair, gate, mixed, gain, hgain, oweight, weight, z_out, out, normed, mixed32, hidden, staged, extra
 ):
-    normalize(pair, gain[0:1, :], normed)
-    finish(pair, normed, mixed, hgain[0:1, :], oweight[0], gweight[0], z_out, mixed32, hidden)
+    finish(pair, gate, mixed, hgain[0:1, :], oweight[0], z_out, mixed32, hidden)
     normalize(z_out, gain[1:2, :], normed)
     project(normed, weight[1], staged, extra)
     write_messages(staged, out)
 
 
-def last_kernel(pair, mixed, gain, hgain, oweight, gweight, z_out, normed, mixed32, hidden):
-    normalize(pair, gain[1:2, :], normed)
-    finish(pair, normed, mixed, hgain[1:2, :], oweight[1], gweight[1], z_out, mixed32, hidden)
+def last_kernel(pair, gate, mixed, hgain, oweight, z_hbm, z_out, sems, mixed32, hidden):
+    copies = []
+
+    def ready(s):
+        rows = pl.ds(s, 4)
+        copies.append(pltpu.make_async_copy(z_out.at[rows], z_hbm.at[rows], sems.at[s // 4]))
+        copies[-1].start()
+
+    finish(pair, gate, mixed, hgain[1:2, :], oweight[1], z_out, mixed32, hidden, ready)
+    for copy in copies:
+        copy.wait()
 
 
 def moved(ref, p, base, offset):
@@ -167,14 +194,13 @@
     return jnp.concatenate(tiles, axis=1).astype(BF16)
 
 
-def split_out_kernel(got, me, left, kept, given):
+def split_out_kernel(got, me, left, right):
     for a in range(8):
         left[a * SIDE : (a + 1) * SIDE, :] = dense(got, [a * 8 + b for b in range(8)], 0)
     for a in range(4):
-        rows = slice(a * SIDE, (a + 1) * SIDE)
-        mine, other = (2 * a + me[0]) * 8, (2 * a + 1 - me[0]) * 8
-        kept[rows, :] = dense(got, [mine + b for b in range(8)], SLOT)
-        given[rows, :] = dense(got, [other + b for b in range(8)], SLOT)
+        for n, core in enumerate((me[0], 1 - me[0])):
+            start = n * 192 + a * SIDE
+            right[start : start + SIDE, :] = dense(got, [(2 * a + core) * 8 + b for b in range(8)], SLOT)
 
 
 def send_back(total, blocks, place, out):
@@ -187,18 +213,18 @@
             out[place(a, b + 1)] = jnp.where(lane < SLOT, pltpu.roll(low, SLOT, 1), high).astype(BF16)
 
 
-def padded(ref):
+def padded(ref, start):
     pad = jnp.zeros((SLOT - SIDE, ref.shape[1]), BF16)
     pieces = []
     for b in range(4):
-        pieces += [ref[b * SIDE : (b + 1) * SIDE, :], pad]
+        pieces += [ref[start + b * SIDE : start + (b + 1) * SIDE, :], pad]
     return jnp.concatenate(pieces, axis=0)
 
 
-def mix_out_kernel(left, left_c, kept, given_c, kept_y, given_d, me, out):
-    for step, (near, far) in enumerate(((kept, given_c), (kept_y, given_d))):
-        total = lax.dot_general(left[...], padded(near), NT, preferred_element_type=F32)
-        total += lax.dot_general(left_c[...], padded(far), NT, preferred_element_type=F32)
+def mix_out_kernel(left, left_c, right, right_c, right_y, right_yc, me, out):
+    for step, (near, far) in enumerate(((right, right_c), (right_y, right_yc))):
+        total = lax.dot_general(left[...], padded(near, 0), NT, preferred_element_type=F32)
+        total += lax.dot_general(left_c[...], padded(far, 192), NT, preferred_element_type=F32)
         owner = me[0] if step == 0 else 1 - me[0]
         send_back(total, 8, lambda a, b: a * 8 + (2 * (b // 2) + owner) * 2 + b % 2, out)
 
@@ -217,8 +243,9 @@
 
 def mix_in_kernel(right, left, left_c, left_x, left_d, me, out):
     for step, ref in enumerate((left, left_c, left_x, left_d)):
-        total = lax.dot_general(ref[:, :192], right[:384, :], TN, preferred_element_type=F32)
-        total += lax.dot_general(ref[:, 192:], right[384:, :], TN, preferred_element_type=F32)
+        tall = ref[...].T
+        total = jnp.dot(tall[:192], right[:384, :], preferred_element_type=F32)
+        total += jnp.dot(tall[192:], right[384:, :], preferred_element_type=F32)
         core = me[1] if step % 2 == 0 else 1 - me[1]
         low = me[0] if step < 2 else 1 - me[0]
         send_back(
@@ -237,35 +264,46 @@
 MESSAGE = (CH, MAIN, LANES)
 BACK = (CH, HALF, LANES)
 BLOCK = (SIDE, SIDE, LANES)
+GATE = (HALF * LANES, LANES)
 
 
 def body(pair, norm_gain, proj_weight, hid_gain, out_weight, gate_weight):
-    normed = pltpu.VMEM((HALF * LANES, LANES), BF16)
+    normed = pltpu.VMEM(GATE, BF16)
     staged = pltpu.VMEM((MAIN * STRIDE, LANES), F32)
     extra = pltpu.VMEM((HALF, CH, LANES), F32)
     mixed32 = pltpu.VMEM((CH * HALF, LANES), F32)
     hidden = pltpu.VMEM((HALF, CH, LANES), BF16)
+    block = pltpu.VMEM(BLOCK, BF16)
+    gain32, weight = pltpu.VMEM((2, LANES), F32), pltpu.VMEM((LANES, 4 * CH), BF16)
     out_axes, in_axes = ("yh", "zl", "xh", "xl", "zh"), ("yh", "yl", "zl", "xh", "zh")
     core = lax.axis_index("c")
 
-    (sent,) = call(project_kernel, [MESSAGE], 3, [normed, staged, extra])(pair, norm_gain, proj_weight)
+    (sent,) = call(
+        project_kernel,
+        [MESSAGE],
+        3,
+        [block, gain32, weight, pltpu.SemaphoreType.DMA((SIDE // GROUP + 2,)), normed, staged, extra],
+        inputs=HBM,
+        limit=55 << 20,
+    )(pair, norm_gain, proj_weight)
+    (gate,) = call(functools.partial(gate_kernel, 0), [GATE], 3, [normed], dtype=F32)(pair, norm_gain, gate_weight)
     got = lax.all_to_all(sent, out_axes, 0, 0, tiled=True)
-    left, kept, given = call(split_out_kernel, [(384, 384), (192, 384), (192, 384)], 1, smem=1)(
-        got, core.reshape(1)
-    )
+    left, right = call(split_out_kernel, [(384, 384)] * 2, 1, smem=1)(got, core.reshape(1))
+    right_y = swap(right, "yl")
     (sent,) = call(mix_out_kernel, [BACK], 6, smem=1)(
         left,
         swap(left, "c"),
-        kept,
-        swap(given, "c"),
-        swap(kept, "yl"),
-        swap(given, "yl", "c"),
+        right,
+        swap(right, "c"),
+        right_y,
+        swap(right_y, "c"),
         lax.axis_index("yl").reshape(1),
     )
     mixed = lax.all_to_all(sent, out_axes, 0, 0, tiled=True)
     first, sent = call(middle_kernel, [BLOCK, MESSAGE], 7, [normed, mixed32, hidden, staged, extra])(
-        pair, mixed, norm_gain, hid_gain, out_weight, gate_weight, proj_weight
-    )
+        pair, gate, mixed, norm_gain, hid_gain, out_weight, proj_weight
+    )
+    (gate,) = call(functools.partial(gate_kernel, 1), [GATE], 3, [normed], dtype=F32)(first, norm_gain, gate_weight)
     got = lax.all_to_all(sent, in_axes, 0, 0, tiled=True)
     left, right = call(split_in_kernel, [(384, 384), (768, 256)], 1)(got)
     left_x = swap(left, "xl")
@@ -278,9 +316,13 @@
         jnp.stack([lax.axis_index("xl"), core]),
     )
     mixed = lax.all_to_all(sent, in_axes, 0, 0, tiled=True)
-    (updated,) = call(last_kernel, [BLOCK], 6, [normed, mixed32, hidden])(
-        first, mixed, norm_gain, hid_gain, out_weight, gate_weight
-    )
+    (updated,) = call(
+        last_kernel,
+        [BLOCK],
+        5,
+        [block, pltpu.SemaphoreType.DMA((SIDE // 4,)), mixed32, hidden],
+        outputs=HBM,
+    )(first, gate, mixed, hid_gain, out_weight)
     return updated
 
 

time: 145 us -> 142 us (0.979)
  blocking collectives: 74.3 us -> 27.6 us
  waiting for transfers between devices: 35 us -> 67.6 us
  starting transfers between devices: 18.5 us -> 30.6 us
  local copies, waits for them, and re-layouts: 2.68 us -> 0.03 us
  Pallas kernels: 13.6 us -> 15.1 us
    all_to_all x2 -> x0, blocking collectives: 47 us -> none  [the longest x1 24 us: body(): mixed = lax.all_to_all(sent, in_axes, 0, 0, tiled=True)]
    all_to_all x0 -> x2, waiting for transfers between devices: none -> 32.1 us  [the longest x1 16.8 us: body(): mixed = lax.all_to_all(sent, in_axes, 0, 0, tiled=True)]
    all_to_all x0 -> x2, starting transfers between devices: none -> 13.3 us  [the longest x1 7.5 us: body(): mixed = lax.all_to_all(sent, out_axes, 0, 0, tiled=True)]
    unnamed x18 -> x12, local copies, waits for them, and re-layouts: 2.68 us -> 0.03 us
    pallas_call x3 -> x5, Pallas kernels: 6.31 us -> 8.4 us  [the longest x1 4.22 us: body(): call(project_kernel, [MESSAGE], 3, [block, gain32, weight, pltpu.Semaphor...]
    pallas_call x1, Pallas kernels: 4.35 us -> 2.83 us  [body(): call(middle_kernel, [BLOCK, MESSAGE], 7, [normed, mixed32, hidden, staged...]
  transfers between devices with their start and end apart: 8 -> 10, of which waited for: 5 -> 7; matrix products, arithmetic and copies ran while one was open for 0% -> 0% of each run, Pallas kernels for 0% -> 2%
where the time goes in v4:
time: 142 us; the launch traced here: 141 us
  waiting for transfers between devices  67.6 us (48%)
  starting transfers between devices  30.6 us (22%)
  blocking collectives  27.6 us (19%)
  Pallas kernels  15.1 us (11%)
    all_to_all x1, blocking collectives, body(): got = lax.all_to_all(sent, in_axes, 0, 0, tiled=True)  27.6 us
    all_to_all x1, waiting for transfers between devices, body(): got = lax.all_to_all(sent, out_axes, 0, 0, tiled=True)  21.5 us
    all_to_all x1, waiting for transfers between devices, body(): mixed = lax.all_to_all(sent, in_axes, 0, 0, tiled=True)  16.8 us
    all_to_all x1, waiting for transfers between devices, body(): mixed = lax.all_to_all(sent, out_axes, 0, 0, tiled=True)  15.3 us
    all_to_all x1, starting transfers between devices, body(): got = lax.all_to_all(sent, out_axes, 0, 0, tiled=True)  14.7 us
    ppermute x7, waiting for transfers between devices, swap(): return lax.ppermute(values, axes, [(i, n - 1 - i) for i in range(n)])  14.1 us
    all_to_all x1, starting transfers between devices, body(): mixed = lax.all_to_all(sent, out_axes, 0, 0, tiled=True)  7.5 us
    all_to_all x1, starting transfers between devices, body(): mixed = lax.all_to_all(sent, in_axes, 0, 0, tiled=True)  5.82 us
  transfers between devices with their start and end apart: 10, of which 7 were waited for; matrix products, arithmetic and copies ran while one was open for 0% of the time, Pallas kernels for 2%

profile of v4, /device:TPU:2, one launch (start us, length us, event | category | flops | bytes accessed | tf_op | source)
XLA Modules:
  0.0 141.4 jit_solution(12259721210531908864)
XLA Ops:
  0.0 4.2 %shard_map.65 = bf16[64,40,128]{2,1,0:T(8,128)(2,1)} custom-call(bf16[48,48,128]{2,1,0:T(8,128)(2,1)} %pair.3, f32[2,128]{1,0:T(2,128)} %gain.5, bf16[2,128,256]{2,1,0:T(8,128)(2,1)} %weight.1), custom_call_target="tpu_custom_call" | custom-call | tf_op jit(solution)/shard_map/pallas_call | solution.py:281
  4.2 14.7 %all-to-all-start = ((bf16[64,40,128]{2,1,0:T(8,128)(2,1)}), bf16[64,40,128]{2,1,0:T(8,128)(2,1)S(1)}, u32[]{:S(2)}, u32[]{:S(2)}) async-start(bf16[64,40,128]{2,1,0:T(8,128)(2,1)} %shard_map.65), calls=%async_computation | async-start | bytes 1310720 | tf_op jit(solution)/shard_map/all_to_all | solution.py:290
  18.9 21.5 %all-to-all-done.got = bf16[64,40,128]{2,1,0:T(8,128)(2,1)S(1)} async-done(((bf16[64,40,128]{2,1,0:T(8,128)(2,1)}), bf16[64,40,128]{2,1,0:T(8,128)(2,1)S(1)}, u32[]{:S(2)}, u32[]{:S(2)}) %all-to-all-start) | async-done | bytes 655392 | tf_op jit(solution)/shard_map/all_to_all | solution.py:290
  40.4 0.5 shard_map.66
  40.9 0.0 copy-start
  40.9 0.0 copy-start.2
  40.9 0.0 copy-start.4
  40.9 0.9 collective-permute-start.2
  41.8 0.5 collective-permute-start
  42.3 5.4 %collective-permute-done.2.right_y = bf16[384,384]{1,0:T(8,128)(2,1)S(1)} collective-permute-done((bf16[384,384]{1,0:T(8,128)(2,1)S(1)}, bf16[384,384]{1,0:T(8,128)(2,1)S(1)}, u32[]{:S(2)}, u32[]{:S(2)}) %collective-permute-start.2) | collective-permute-done | bytes 294944 | tf_op jit(solution)/shard_map/ppermute | solution.py:261
  47.8 0.0 collective-permute-start.3
  47.8 0.0 collective-permute-done.left_c
  47.8 0.0 collective-permute-done.1.right_c
  47.8 1.6 %collective-permute-done.3.right_yc = bf16[384,384]{1,0:T(8,128)(2,1)S(1)} collective-permute-done((bf16[384,384]{1,0:T(8,128)(2,1)S(1)}, bf16[384,384]{1,0:T(8,128)(2,1)S(1)}, u32[]{:S(2)}, u32[]{:S(2)}) %collective-permute-start.3) | collective-permute-done | bytes 294944 | tf_op jit(solution)/shard_map/ppermute | solution.py:261
  49.3 1.4 %shard_map.67 = bf16[64,24,128]{2,1,0:T(8,128)(2,1)} custom-call(bf16[384,384]{1,0:T(8,128)(2,1)S(1)} %get-tuple-element.11.left, bf16[384,384]{1,0:T(8,128)(2,1)S(1)} %collective-permute-done.left_c, bf16[384,384]{1,0:T(8,128)(2,1)S(1)} %get-tuple-element.12.right, bf16[384,384]{1,0:T(8,128)(2,1)S(1)} %collective-permute-done.1.right_c, ...), custom_call_target="tpu_custom_call" | custom-call | tf_op jit(solution)/shard_map/pallas_call | solution.py:293
  50.8 7.5 %all-to-all-start.1 = ((bf16[64,24,128]{2,1,0:T(8,128)(2,1)}), bf16[64,24,128]{2,1,0:T(8,128)(2,1)S(1)}, u32[]{:S(2)}, u32[]{:S(2)}) async-start(bf16[64,24,128]{2,1,0:T(8,128)(2,1)} %shard_map.67), calls=%async_computation.1 | async-start | bytes 786432 | tf_op jit(solution)/shard_map/all_to_all | solution.py:302
  58.3 1.1 shard_map.64.gate
  59.5 15.3 %all-to-all-done.1.mixed = bf16[64,24,128]{2,1,0:T(8,128)(2,1)S(1)} async-done(((bf16[64,24,128]{2,1,0:T(8,128)(2,1)}), bf16[64,24,128]{2,1,0:T(8,128)(2,1)S(1)}, u32[]{:S(2)}, u32[]{:S(2)}) %all-to-all-start.1) | async-done | bytes 393248 | tf_op jit(solution)/shard_map/all_to_all | solution.py:302
  74.7 2.8 %shard_map.68 = (bf16[48,48,128]{2,1,0:T(8,128)(2,1)S(1)}, bf16[64,40,128]{2,1,0:T(8,128)(2,1)S(1)}) custom-call(bf16[48,48,128]{2,1,0:T(8,128)(2,1)S(1)} %copy-done, f32[3072,128]{1,0:T(8,128)S(1)} %shard_map.64.gate, bf16[64,24,128]{2,1,0:T(8,128)(2,1)S(1)} %all-to-all-done.1.mixed, f32[2,128]{1,0:T(2,128)S(1)} %copy-done.4, f32[2,64]{1,0:T(2,128)S(1)} %copy-done.5, ...), custom_call_target="tpu_custom_call" | custom-call | tf_op jit(solution)/shard_map/pallas_call | solution.py:303
  77.6 27.6 %all_to_all.20.got = bf16[64,40,128]{2,1,0:T(8,128)(2,1)S(1)} all-to-all(bf16[64,40,128]{2,1,0:T(8,128)(2,1)S(1)} %get-tuple-element.14), channel_id=1, replica_groups=mesh['yh'=2,'yl'=2,'zl'=4,'xh'=2,'xl'=2,'zh'=2,'c'=2] {'yh','yl','zl','x..., dimensions={0} | all-to-all | bytes 1310720 | tf_op jit(solution)/shard_map/all_to_all | solution.py:307
  105.2 0.5 shard_map.70
  105.7 1.3 collective-permute-start.5
  107.0 0.0 collective-permute-start.4
  107.0 5.5 %collective-permute-done.5.left_x = bf16[384,384]{1,0:T(8,128)(2,1)S(1)} collective-permute-done((bf16[384,384]{1,0:T(8,128)(2,1)S(1)}, bf16[384,384]{1,0:T(8,128)(2,1)S(1)}, u32[]{:S(2)}, u32[]{:S(2)}) %collective-permute-start.5) | collective-permute-done | bytes 294944 | tf_op jit(solution)/shard_map/ppermute | solution.py:261
  112.5 0.0 collective-permute-start.6
  112.5 0.1 pad_add_fusion.me
  112.6 1.5 %collective-permute-done.6.left_d = bf16[384,384]{1,0:T(8,128)(2,1)S(1)} collective-permute-done((bf16[384,384]{1,0:T(8,128)(2,1)S(1)}, bf16[384,384]{1,0:T(8,128)(2,1)S(1)}, u32[]{:S(2)}, u32[]{:S(2)}) %collective-permute-start.6) | collective-permute-done | bytes 294944 | tf_op jit(solution)/shard_map/ppermute | solution.py:261
  114.1 2.0 %shard_map.71 = bf16[64,24,128]{2,1,0:T(8,128)(2,1)} custom-call(bf16[768,256]{1,0:T(8,128)(2,1)S(1)} %get-tuple-element.15.right, bf16[384,384]{1,0:T(8,128)(2,1)S(1)} %get-tuple-element.16.left, bf16[384,384]{1,0:T(8,128)(2,1)S(1)} %collective-permute-done.4.left_c, bf16[384,384]{1,0:T(8,128)(2,1)S(1)} %collective-permute-done.5.left_x, ...), custom_call_target="tpu_custom_call" | custom-call | tf_op jit(solution)/shard_map/pallas_call | solution.py:310
  116.1 5.8 %all-to-all-start.3 = ((bf16[64,24,128]{2,1,0:T(8,128)(2,1)}), bf16[64,24,128]{2,1,0:T(8,128)(2,1)S(1)}, u32[]{:S(2)}, u32[]{:S(2)}) async-start(bf16[64,24,128]{2,1,0:T(8,128)(2,1)} %shard_map.71), calls=%async_computation.3 | async-start | bytes 786432 | tf_op jit(solution)/shard_map/all_to_all | solution.py:318
  121.9 1.1 shard_map.69.gate
  123.1 16.8 %all-to-all-done.3.mixed = bf16[64,24,128]{2,1,0:T(8,128)(2,1)S(1)} async-done(((bf16[64,24,128]{2,1,0:T(8,128)(2,1)}), bf16[64,24,128]{2,1,0:T(8,128)(2,1)S(1)}, u32[]{:S(2)}, u32[]{:S(2)}) %all-to-all-start.3) | async-done | bytes 393248 | tf_op jit(solution)/shard_map/all_to_all | solution.py:318
  139.9 1.4 shard_map.72
  (11 shorter events, 0.0 us)
Async XLA Ops:
  4.2 36.1 %all-to-all-start = ((bf16[64,40,128]{2,1,0:T(8,128)(2,1)}), bf16[64,40,128]{2,1,0:T(8,128)(2,1)S(1)}, u32[]{:S(2)}, u32[]{:S(2)}) async-start(bf16[64,40,128]{2,1,0:T(8,128)(2,1)} %shard_map.65), calls=%async_computation | async-start | bytes 1310720 | tf_op jit(solution)/shard_map/all_to_all | solution.py:290
  40.9 17.4 %copy-start = (bf16[48,48,128]{2,1,0:T(8,128)(2,1)S(1)}, bf16[48,48,128]{2,1,0:T(8,128)(2,1)}, u32[]{:S(2)}) copy-start(bf16[48,48,128]{2,1,0:T(8,128)(2,1)} %pair.3) | copy-start | bytes 1769476
  40.9 17.4 %copy-start.2 = (bf16[2,128,128]{2,1,0:T(8,128)(2,1)S(1)}, bf16[2,128,128]{2,1,0:T(8,128)(2,1)}, u32[]{:S(2)}) copy-start(bf16[2,128,128]{2,1,0:T(8,128)(2,1)} %gweight.3) | copy-start | bytes 196612
  40.9 17.4 %copy-start.4 = (f32[2,128]{1,0:T(2,128)S(1)}, f32[2,128]{1,0:T(2,128)}, u32[]{:S(2)}) copy-start(f32[2,128]{1,0:T(2,128)} %gain.5) | copy-start | bytes 3076
  40.9 6.8 %collective-permute-start.2 = (bf16[384,384]{1,0:T(8,128)(2,1)S(1)}, bf16[384,384]{1,0:T(8,128)(2,1)S(1)}, u32[]{:S(2)}, u32[]{:S(2)}) collective-permute-start(bf16[384,384]{1,0:T(8,128)(2,1)S(1)} %get-tuple-element.12.right), channel_id=1, source_target_pairs={{0,64},{64,0},{1,65},{65,1},{2,66},{66,2},{3,67},{67,3},{4,68},{68... | collective-permute-start | bytes 884744 | tf_op jit(solution)/shard_map/ppermute | solution.py:261
  41.8 6.0 %collective-permute-start.1 = (bf16[384,384]{1,0:T(8,128)(2,1)S(1)}, bf16[384,384]{1,0:T(8,128)(2,1)S(1)}, u32[]{:S(2)}, u32[]{:S(2)}) collective-permute-start(bf16[384,384]{1,0:T(8,128)(2,1)S(1)} %get-tuple-element.12.right), channel_id=1, source_target_pairs={{0,1},{1,0},{2,3},{3,2},{4,5},{5,4},{6,7},{7,6},{8,9},{9,8},{10,11... | collective-permute-start | bytes 884744 | tf_op jit(solution)/shard_map/ppermute | solution.py:261
  41.8 6.0 %collective-permute-start = (bf16[384,384]{1,0:T(8,128)(2,1)S(1)}, bf16[384,384]{1,0:T(8,128)(2,1)S(1)}, u32[]{:S(2)}, u32[]{:S(2)}) collective-permute-start(bf16[384,384]{1,0:T(8,128)(2,1)S(1)} %get-tuple-element.11.left), channel_id=1, source_target_pairs={{0,1},{1,0},{2,3},{3,2},{4,5},{5,4},{6,7},{7,6},{8,9},{9,8},{10,11... | collective-permute-start | bytes 884744 | tf_op jit(solution)/shard_map/ppermute | solution.py:261
  47.8 1.6 %collective-permute-start.3 = (bf16[384,384]{1,0:T(8,128)(2,1)S(1)}, bf16[384,384]{1,0:T(8,128)(2,1)S(1)}, u32[]{:S(2)}, u32[]{:S(2)}) collective-permute-start(bf16[384,384]{1,0:T(8,128)(2,1)S(1)} %collective-permute-done.2.right_y), channel_id=1, source_target_pairs={{0,1},{1,0},{2,3},{3,2},{4,5},{5,4},{6,7},{7,6},{8,9},{9,8},{10,11... | collective-permute-start | bytes 884744 | tf_op jit(solution)/shard_map/ppermute | solution.py:261
  50.8 24.0 %copy-start.1 = (bf16[2,128,256]{2,1,0:T(8,128)(2,1)S(1)}, bf16[2,128,256]{2,1,0:T(8,128)(2,1)}, u32[]{:S(2)}) copy-start(bf16[2,128,256]{2,1,0:T(8,128)(2,1)} %weight.1) | copy-start | bytes 393220
  50.8 24.0 %copy-start.3 = (bf16[2,64,128]{2,1,0:T(8,128)(2,1)S(1)}, bf16[2,64,128]{2,1,0:T(8,128)(2,1)}, u32[]{:S(2)}) copy-start(bf16[2,64,128]{2,1,0:T(8,128)(2,1)} %oweight.3) | copy-start | bytes 98308
  50.8 24.0 %copy-start.5 = (f32[2,64]{1,0:T(2,128)S(1)}, f32[2,64]{1,0:T(2,128)}, u32[]{:S(2)}) copy-start(f32[2,64]{1,0:T(2,128)} %hgain.3) | copy-start | bytes 1540
  50.8 24.0 %all-to-all-start.1 = ((bf16[64,24,128]{2,1,0:T(8,128)(2,1)}), bf16[64,24,128]{2,1,0:T(8,128)(2,1)S(1)}, u32[]{:S(2)}, u32[]{:S(2)}) async-start(bf16[64,24,128]{2,1,0:T(8,128)(2,1)} %shard_map.67), calls=%async_computation.1 | async-start | bytes 786432 | tf_op jit(solution)/shard_map/all_to_all | solution.py:302
  105.7 6.8 %collective-permute-start.5 = (bf16[384,384]{1,0:T(8,128)(2,1)S(1)}, bf16[384,384]{1,0:T(8,128)(2,1)S(1)}, u32[]{:S(2)}, u32[]{:S(2)}) collective-permute-start(bf16[384,384]{1,0:T(8,128)(2,1)S(1)} %get-tuple-element.16.left), channel_id=1, source_target_pairs={{0,4},{4,0},{1,5},{5,1},{2,6},{6,2},{3,7},{7,3},{8,12},{12,8},{9,1... | collective-permute-start | bytes 884744 | tf_op jit(solution)/shard_map/ppermute | solution.py:261
  107.0 5.6 %collective-permute-start.4 = (bf16[384,384]{1,0:T(8,128)(2,1)S(1)}, bf16[384,384]{1,0:T(8,128)(2,1)S(1)}, u32[]{:S(2)}, u32[]{:S(2)}) collective-permute-start(bf16[384,384]{1,0:T(8,128)(2,1)S(1)} %get-tuple-element.16.left), channel_id=1, source_target_pairs={{0,1},{1,0},{2,3},{3,2},{4,5},{5,4},{6,7},{7,6},{8,9},{9,8},{10,11... | collective-permute-start | bytes 884744 | tf_op jit(solution)/shard_map/ppermute | solution.py:261
  112.5 1.6 %collective-permute-start.6 = (bf16[384,384]{1,0:T(8,128)(2,1)S(1)}, bf16[384,384]{1,0:T(8,128)(2,1)S(1)}, u32[]{:S(2)}, u32[]{:S(2)}) collective-permute-start(bf16[384,384]{1,0:T(8,128)(2,1)S(1)} %collective-permute-done.5.left_x), channel_id=1, source_target_pairs={{0,1},{1,0},{2,3},{3,2},{4,5},{5,4},{6,7},{7,6},{8,9},{9,8},{10,11... | collective-permute-start | bytes 884744 | tf_op jit(solution)/shard_map/ppermute | solution.py:261
  116.1 23.8 %all-to-all-start.3 = ((bf16[64,24,128]{2,1,0:T(8,128)(2,1)}), bf16[64,24,128]{2,1,0:T(8,128)(2,1)S(1)}, u32[]{:S(2)}, u32[]{:S(2)}) async-start(bf16[64,24,128]{2,1,0:T(8,128)(2,1)} %shard_map.71), calls=%async_computation.3 | async-start | bytes 786432 | tf_op jit(solution)/shard_map/all_to_all | solution.py:318

commit v5 on v4

--- a/solution.py
+++ b/solution.py
@@ -194,13 +194,16 @@
     return jnp.concatenate(tiles, axis=1).astype(BF16)
 
 
-def split_out_kernel(got, me, left, right):
-    for a in range(8):
-        left[a * SIDE : (a + 1) * SIDE, :] = dense(got, [a * 8 + b for b in range(8)], 0)
+def out_right_kernel(got, me, right):
     for a in range(4):
         for n, core in enumerate((me[0], 1 - me[0])):
             start = n * 192 + a * SIDE
             right[start : start + SIDE, :] = dense(got, [(2 * a + core) * 8 + b for b in range(8)], SLOT)
+
+
+def out_left_kernel(got, left):
+    for a in range(8):
+        left[a * SIDE : (a + 1) * SIDE, :] = dense(got, [a * 8 + b for b in range(8)], 0)
 
 
 def send_back(total, blocks, place, out):
@@ -221,18 +224,33 @@
     return jnp.concatenate(pieces, axis=0)
 
 
-def mix_out_kernel(left, left_c, right, right_c, right_y, right_yc, me, out):
-    for step, (near, far) in enumerate(((right, right_c), (right_y, right_yc))):
-        total = lax.dot_general(left[...], padded(near, 0), NT, preferred_element_type=F32)
-        total += lax.dot_general(left_c[...], padded(far, 192), NT, preferred_element_type=F32)
-        owner = me[0] if step == 0 else 1 - me[0]
-        send_back(total, 8, lambda a, b: a * 8 + (2 * (b // 2) + owner) * 2 + b % 2, out)
-
-
-def split_in_kernel(got, left, right):
+def out_sums(left, left_c, near, far, place, out):
+    total = lax.dot_general(left[...], padded(near, 0), NT, preferred_element_type=F32)
+    total += lax.dot_general(left_c[...], padded(far, 192), NT, preferred_element_type=F32)
+    send_back(total, 8, place, out)
+
+
+def out_early_kernel(left, left_c, right, right_c, out):
+    out_sums(left, left_c, right, right_c, lambda a, b: a * 4 + b, out)
+
+
+def out_late_kernel(left, left_c, right_y, right_yc, early, me, out):
+    def place(owner):
+        return lambda a, b: a * 8 + (2 * (b // 2) + owner) * 2 + b % 2
+
+    for a in range(8):
+        for b in range(4):
+            out[place(me[0])(a, b)] = early[a * 4 + b]
+    out_sums(left, left_c, right_y, right_yc, place(1 - me[0]), out)
+
+
+def in_left_kernel(got, left):
     for r in range(8):
         rows = slice(r * SIDE, (r + 1) * SIDE)
         left[rows, :] = dense(got, [(r + 8 * h) * 4 + b for h in range(2) for b in range(4)], 0)
+
+
+def in_right_kernel(got, right):
     lane = lane_of(SIDE)
     for r in range(16):
         for b in range(0, 4, 2):
@@ -241,19 +259,28 @@
             right[r * SIDE : (r + 1) * SIDE, b * SLOT : (b + 2) * SLOT] = tile.astype(BF16)
 
 
-def mix_in_kernel(right, left, left_c, left_x, left_d, me, out):
-    for step, ref in enumerate((left, left_c, left_x, left_d)):
-        tall = ref[...].T
-        total = jnp.dot(tall[:192], right[:384, :], preferred_element_type=F32)
-        total += jnp.dot(tall[192:], right[384:, :], preferred_element_type=F32)
-        core = me[1] if step % 2 == 0 else 1 - me[1]
-        low = me[0] if step < 2 else 1 - me[0]
-        send_back(
-            total,
-            4,
-            lambda a, b: (2 * (a // 2) + low) * 16 + (2 * (a % 2) + core) * 4 + b,
-            out,
-        )
+def in_sums(left, right, place, out):
+    tall = left[...].T
+    total = jnp.dot(tall[:192], right[:384, :], preferred_element_type=F32)
+    total += jnp.dot(tall[192:], right[384:, :], preferred_element_type=F32)
+    send_back(total, 4, place, out)
+
+
+def in_early_kernel(right, left, left_c, out):
+    for n, ref in enumerate((left, left_c)):
+        in_sums(ref, right, lambda a, b: n * 16 + a * 4 + b, out)
+
+
+def in_late_kernel(right, left_x, left_d, early, me, core, out):
+    def place(low, core):
+        return lambda a, b: (2 * (a // 2) + low) * 16 + (2 * (a % 2) + core) * 4 + b
+
+    for n, c in enumerate((core[0], 1 - core[0])):
+        for a in range(4):
+            for b in range(4):
+                out[place(me[0], c)(a, b)] = early[n * 16 + a * 4 + b]
+    in_sums(left_x, right, place(1 - me[0], core[0]), out)
+    in_sums(left_d, right, place(1 - me[0], 1 - core[0]), out)
 
 
 def swap(values, *axes):
@@ -263,6 +290,7 @@
 
 MESSAGE = (CH, MAIN, LANES)
 BACK = (CH, HALF, LANES)
+EARLY = (CH // 2, HALF, LANES)
 BLOCK = (SIDE, SIDE, LANES)
 GATE = (HALF * LANES, LANES)
 
@@ -276,7 +304,8 @@
     block = pltpu.VMEM(BLOCK, BF16)
     gain32, weight = pltpu.VMEM((2, LANES), F32), pltpu.VMEM((LANES, 4 * CH), BF16)
     out_axes, in_axes = ("yh", "zl", "xh", "xl", "zh"), ("yh", "yl", "zl", "xh", "zh")
-    core = lax.axis_index("c")
+    tie = lax.optimization_barrier
+    pair, core, low_y, low_x = tie((pair, *(lax.axis_index(name).reshape(1) for name in ("c", "yl", "xl"))))
 
     (sent,) = call(
         project_kernel,
@@ -286,35 +315,33 @@
         inputs=HBM,
         limit=55 << 20,
     )(pair, norm_gain, proj_weight)
-    (gate,) = call(functools.partial(gate_kernel, 0), [GATE], 3, [normed], dtype=F32)(pair, norm_gain, gate_weight)
     got = lax.all_to_all(sent, out_axes, 0, 0, tiled=True)
-    left, right = call(split_out_kernel, [(384, 384)] * 2, 1, smem=1)(got, core.reshape(1))
-    right_y = swap(right, "yl")
-    (sent,) = call(mix_out_kernel, [BACK], 6, smem=1)(
-        left,
-        swap(left, "c"),
-        right,
-        swap(right, "c"),
-        right_y,
-        swap(right_y, "c"),
-        lax.axis_index("yl").reshape(1),
-    )
+    (right,) = call(out_right_kernel, [(384, 384)], 1, smem=1)(got, core)
+    right_y, right_c = swap(right, "yl"), swap(right, "c")
+    got, right = tie((got, right))
+    (left,) = call(out_left_kernel, [(384, 384)], 1)(got)
+    left_c = swap(left, "c")
+    source, left = tie((pair, left))
+    (gate,) = call(functools.partial(gate_kernel, 0), [GATE], 3, [normed], dtype=F32)(source, norm_gain, gate_weight)
+    (early,) = call(out_early_kernel, [EARLY], 4)(left, left_c, right, right_c)
+    right_y, early, gate = tie((right_y, early, gate))
+    right_yc = swap(right_y, "c")
+    (sent,) = call(out_late_kernel, [BACK], 5, smem=1)(left, left_c, right_y, right_yc, early, low_y)
     mixed = lax.all_to_all(sent, out_axes, 0, 0, tiled=True)
     first, sent = call(middle_kernel, [BLOCK, MESSAGE], 7, [normed, mixed32, hidden, staged, extra])(
         pair, gate, mixed, norm_gain, hid_gain, out_weight, proj_weight
     )
-    (gate,) = call(functools.partial(gate_kernel, 1), [GATE], 3, [normed], dtype=F32)(first, norm_gain, gate_weight)
     got = lax.all_to_all(sent, in_axes, 0, 0, tiled=True)
-    left, right = call(split_in_kernel, [(384, 384), (768, 256)], 1)(got)
-    left_x = swap(left, "xl")
-    (sent,) = call(mix_in_kernel, [BACK], 5, smem=1)(
-        right,
-        left,
-        swap(left, "c"),
-        left_x,
-        swap(left_x, "c"),
-        jnp.stack([lax.axis_index("xl"), core]),
-    )
+    (left,) = call(in_left_kernel, [(384, 384)], 1)(got)
+    left_x, left_c = swap(left, "xl"), swap(left, "c")
+    got, left = tie((got, left))
+    (right,) = call(in_right_kernel, [(768, 256)], 1)(got)
+    source, right = tie((first, right))
+    (gate,) = call(functools.partial(gate_kernel, 1), [GATE], 3, [normed], dtype=F32)(source, norm_gain, gate_weight)
+    (early,) = call(in_early_kernel, [EARLY], 3)(right, left, left_c)
+    left_x, early, gate = tie((left_x, early, gate))
+    left_d = swap(left_x, "c")
+    (sent,) = call(in_late_kernel, [BACK], 4, smem=2)(right, left_x, left_d, early, low_x, core)
     mixed = lax.all_to_all(sent, in_axes, 0, 0, tiled=True)
     (updated,) = call(
         last_kernel,

time: 142 us -> 143 us (level)
  blocking collectives: 27.6 us -> 109 us
  waiting for transfers between devices: 67.6 us -> 15.9 us
  starting transfers between devices: 30.6 us -> 2.82 us
    all_to_all x0 -> x3, blocking collectives: none -> 82.2 us  [the longest x1 36.3 us: body(): got = lax.all_to_all(sent, out_axes, 0, 0, tiled=True)]
    all_to_all x3 -> x0, waiting for transfers between devices: 53.5 us -> none  [the longest x1 21.5 us: body(): got = lax.all_to_all(sent, out_axes, 0, 0, tiled=True)]
    all_to_all x3 -> x0, starting transfers between devices: 28 us -> none  [the longest x1 14.7 us: body(): got = lax.all_to_all(sent, out_axes, 0, 0, tiled=True)]
    ppermute x7, waiting for transfers between devices: 14.1 us -> 15.9 us  [swap(): return lax.ppermute(values, axes, [(i, n - 1 - i) for i in range(n)])]
    pallas_call x4 -> x8, Pallas kernels: 4.46 us -> 3.1 us  [the longest x1 0.51 us: body(): early, = call(in_early_kernel, [EARLY], 3)(right, left, left_c)]
  transfers between devices with their start and end apart: 10 -> 7, of which waited for: 7 -> 4; matrix products, arithmetic and copies ran while one was open for 0% -> 0% of each run, Pallas kernels for 2% -> 2%
where the time goes in v5:
time: 143 us; the launch traced here: 142 us
  blocking collectives  109 us (76%)
  waiting for transfers between devices  15.9 us (11%)
  Pallas kernels  13.8 us (10%)
  starting transfers between devices  2.82 us (2%)
    all_to_all x1, blocking collectives, body(): got = lax.all_to_all(sent, out_axes, 0, 0, tiled=True)  36.3 us
    all_to_all x1, blocking collectives, body(): got = lax.all_to_all(sent, in_axes, 0, 0, tiled=True)  27.2 us
    all_to_all x1, blocking collectives, body(): mixed = lax.all_to_all(sent, in_axes, 0, 0, tiled=True)  23.2 us
    all_to_all x1, blocking collectives, body(): mixed = lax.all_to_all(sent, out_axes, 0, 0, tiled=True)  22.7 us
    ppermute x7, waiting for transfers between devices, swap(): return lax.ppermute(values, axes, [(i, n - 1 - i) for i in range(n)])  15.9 us
    pallas_call x1, Pallas kernels, body(): call(project_kernel, [MESSAGE], 3, [block, gain32, weight, pltpu.Semaphor...  4.21 us
  transfers between devices with their start and end apart: 7, of which 4 were waited for; matrix products, arithmetic and copies ran while one was open for 0% of the time, Pallas kernels for 2%

profile of v5, /device:TPU:2, one launch (start us, length us, event | category | flops | bytes accessed | tf_op | source)
XLA Modules:
  0.0 142.2 jit_solution(18024711513182269361)
XLA Ops:
  0.0 4.2 %shard_map.64 = bf16[64,40,128]{2,1,0:T(8,128)(2,1)} custom-call(bf16[48,48,128]{2,1,0:T(8,128)(2,1)} %pair.1, f32[2,128]{1,0:T(2,128)} %gain.5, bf16[2,128,256]{2,1,0:T(8,128)(2,1)} %weight.1), custom_call_target="tpu_custom_call" | custom-call | tf_op jit(solution)/shard_map/pallas_call | solution.py:310
  4.2 0.0 copy-start
  4.2 0.0 copy-start.2
  4.2 0.0 copy-start.4
  4.3 36.3 %all_to_all.20.got = bf16[64,40,128]{2,1,0:T(8,128)(2,1)S(1)} all-to-all(bf16[64,40,128]{2,1,0:T(8,128)(2,1)} %shard_map.64), channel_id=1, replica_groups=mesh['yh'=2,'yl'=2,'zl'=4,'xh'=2,'xl'=2,'zh'=2,'c'=2] {'yh','zl','xh','x..., dimensions={0} | all-to-all | bytes 1310720 | tf_op jit(solution)/shard_map/all_to_all | solution.py:318
  40.5 0.3 shard_map.65.right
  40.8 0.3 shard_map.66.left
  41.1 0.1 collective-permute-start.1
  41.2 0.5 collective-permute-start.2
  41.7 0.7 collective-permute-start
  42.4 1.1 shard_map.68.gate
  43.6 0.5 shard_map.67.early
  44.1 0.0 copy-start.1
  44.1 0.0 copy-start.3
  44.1 0.0 copy-start.5
  44.1 6.7 %collective-permute-done.right_y = bf16[384,384]{1,0:T(8,128)(2,1)S(1)} collective-permute-done((bf16[384,384]{1,0:T(8,128)(2,1)S(1)}, bf16[384,384]{1,0:T(8,128)(2,1)S(1)}, u32[]{:S(2)}, u32[]{:S(2)}) %collective-permute-start) | collective-permute-done | bytes 294944 | tf_op jit(solution)/shard_map/ppermute | solution.py:288
  50.7 1.6 %collective-permute-done.3.right_yc = bf16[384,384]{1,0:T(8,128)(2,1)S(1)} collective-permute-done((bf16[384,384]{1,0:T(8,128)(2,1)S(1)}, bf16[384,384]{1,0:T(8,128)(2,1)S(1)}, u32[]{:S(2)}, u32[]{:S(2)}) %collective-permute-start.3) | collective-permute-done | bytes 294944 | tf_op jit(solution)/shard_map/ppermute | solution.py:288
  52.3 0.5 shard_map.69
  52.8 22.7 %all_to_all.21.mixed = bf16[64,24,128]{2,1,0:T(8,128)(2,1)S(1)} all-to-all(bf16[64,24,128]{2,1,0:T(8,128)(2,1)S(1)} %shard_map.69), channel_id=1, replica_groups=mesh['yh'=2,'yl'=2,'zl'=4,'xh'=2,'xl'=2,'zh'=2,'c'=2] {'yh','zl','xh','x..., dimensions={0} | all-to-all | bytes 786432 | tf_op jit(solution)/shard_map/all_to_all | solution.py:330
  75.5 2.8 %shard_map.70 = (bf16[48,48,128]{2,1,0:T(8,128)(2,1)S(1)}, bf16[64,40,128]{2,1,0:T(8,128)(2,1)S(1)}) custom-call(bf16[48,48,128]{2,1,0:T(8,128)(2,1)S(1)} %copy-done, f32[3072,128]{1,0:T(8,128)S(1)} %shard_map.68.gate, bf16[64,24,128]{2,1,0:T(8,128)(2,1)S(1)} %all_to_all.21.mixed, f32[2,128]{1,0:T(2,128)S(1)} %copy-done.4, f32[2,64]{1,0:T(2,128)S(1)} %copy-done.5, ...), custom_call_target="tpu_custom_call" | custom-call | tf_op jit(solution)/shard_map/pallas_call | solution.py:331
  78.4 27.2 %all_to_all.22.got = bf16[64,40,128]{2,1,0:T(8,128)(2,1)S(1)} all-to-all(bf16[64,40,128]{2,1,0:T(8,128)(2,1)S(1)} %get-tuple-element.36), channel_id=1, replica_groups=mesh['yh'=2,'yl'=2,'zl'=4,'xh'=2,'xl'=2,'zh'=2,'c'=2] {'yh','yl','zl','x..., dimensions={0} | all-to-all | bytes 1310720 | tf_op jit(solution)/shard_map/all_to_all | solution.py:334
  105.6 0.3 shard_map.71.left
  105.9 0.1 collective-permute-start.5
  106.0 1.5 %collective-permute-start.4 = (bf16[384,384]{1,0:T(8,128)(2,1)S(1)}, bf16[384,384]{1,0:T(8,128)(2,1)S(1)}, u32[]{:S(2)}, u32[]{:S(2)}) collective-permute-start(bf16[384,384]{1,0:T(8,128)(2,1)S(1)} %shard_map.71.left), channel_id=1, source_target_pairs={{0,4},{4,0},{1,5},{5,1},{2,6},{6,2},{3,7},{7,3},{8,12},{12,8},{9,1... | collective-permute-start | bytes 884744 | tf_op jit(solution)/shard_map/ppermute | solution.py:288
  107.5 0.3 shard_map.72.right
  107.8 1.1 shard_map.74.gate
  108.9 0.5 shard_map.73.early
  109.4 6.0 %collective-permute-done.4.left_x = bf16[384,384]{1,0:T(8,128)(2,1)S(1)} collective-permute-done((bf16[384,384]{1,0:T(8,128)(2,1)S(1)}, bf16[384,384]{1,0:T(8,128)(2,1)S(1)}, u32[]{:S(2)}, u32[]{:S(2)}) %collective-permute-start.4) | collective-permute-done | bytes 294944 | tf_op jit(solution)/shard_map/ppermute | solution.py:288
  115.5 1.6 %collective-permute-done.6.left_d = bf16[384,384]{1,0:T(8,128)(2,1)S(1)} collective-permute-done((bf16[384,384]{1,0:T(8,128)(2,1)S(1)}, bf16[384,384]{1,0:T(8,128)(2,1)S(1)}, u32[]{:S(2)}, u32[]{:S(2)}) %collective-permute-start.6) | collective-permute-done | bytes 294944 | tf_op jit(solution)/shard_map/ppermute | solution.py:288
  117.0 0.5 shard_map.75
  117.5 23.2 %all_to_all.23.mixed = bf16[64,24,128]{2,1,0:T(8,128)(2,1)S(1)} all-to-all(bf16[64,24,128]{2,1,0:T(8,128)(2,1)S(1)} %shard_map.75), channel_id=1, replica_groups=mesh['yh'=2,'yl'=2,'zl'=4,'xh'=2,'xl'=2,'zh'=2,'c'=2] {'yh','yl','zl','x..., dimensions={0} | all-to-all | bytes 786432 | tf_op jit(solution)/shard_map/all_to_all | solution.py:345
  140.7 1.4 shard_map.76
  (11 shorter events, 0.0 us)
Async XLA Ops:
  4.2 38.2 %copy-start = (bf16[48,48,128]{2,1,0:T(8,128)(2,1)S(1)}, bf16[48,48,128]{2,1,0:T(8,128)(2,1)}, u32[]{:S(2)}) copy-start(bf16[48,48,128]{2,1,0:T(8,128)(2,1)} %pair.1) | copy-start | bytes 1769476
  4.2 38.2 %copy-start.2 = (bf16[2,128,128]{2,1,0:T(8,128)(2,1)S(1)}, bf16[2,128,128]{2,1,0:T(8,128)(2,1)}, u32[]{:S(2)}) copy-start(bf16[2,128,128]{2,1,0:T(8,128)(2,1)} %gweight.3) | copy-start | bytes 196612
  4.2 38.2 %copy-start.4 = (f32[2,128]{1,0:T(2,128)S(1)}, f32[2,128]{1,0:T(2,128)}, u32[]{:S(2)}) copy-start(f32[2,128]{1,0:T(2,128)} %gain.5) | copy-start | bytes 3076
  41.1 2.4 %collective-permute-start.1 = (bf16[384,384]{1,0:T(8,128)(2,1)S(1)}, bf16[384,384]{1,0:T(8,128)(2,1)S(1)}, u32[]{:S(2)}, u32[]{:S(2)}) collective-permute-start(bf16[384,384]{1,0:T(8,128)(2,1)S(1)} %shard_map.66.left), channel_id=1, source_target_pairs={{0,1},{1,0},{2,3},{3,2},{4,5},{5,4},{6,7},{7,6},{8,9},{9,8},{10,11... | collective-permute-start | bytes 884744 | tf_op jit(solution)/shard_map/ppermute | solution.py:288
  41.2 2.3 %collective-permute-start.2 = (bf16[384,384]{1,0:T(8,128)(2,1)S(1)}, bf16[384,384]{1,0:T(8,128)(2,1)S(1)}, u32[]{:S(2)}, u32[]{:S(2)}) collective-permute-start(bf16[384,384]{1,0:T(8,128)(2,1)S(1)} %shard_map.65.right), channel_id=1, source_target_pairs={{0,1},{1,0},{2,3},{3,2},{4,5},{5,4},{6,7},{7,6},{8,9},{9,8},{10,11... | collective-permute-start | bytes 884744 | tf_op jit(solution)/shard_map/ppermute | solution.py:288
  41.7 9.0 %collective-permute-start = (bf16[384,384]{1,0:T(8,128)(2,1)S(1)}, bf16[384,384]{1,0:T(8,128)(2,1)S(1)}, u32[]{:S(2)}, u32[]{:S(2)}) collective-permute-start(bf16[384,384]{1,0:T(8,128)(2,1)S(1)} %shard_map.65.right), channel_id=1, source_target_pairs={{0,64},{64,0},{1,65},{65,1},{2,66},{66,2},{3,67},{67,3},{4,68},{68... | collective-permute-start | bytes 884744 | tf_op jit(solution)/shard_map/ppermute | solution.py:288
  44.1 31.5 %copy-start.1 = (bf16[2,128,256]{2,1,0:T(8,128)(2,1)S(1)}, bf16[2,128,256]{2,1,0:T(8,128)(2,1)}, u32[]{:S(2)}) copy-start(bf16[2,128,256]{2,1,0:T(8,128)(2,1)} %weight.1) | copy-start | bytes 393220
  44.1 31.5 %copy-start.3 = (bf16[2,64,128]{2,1,0:T(8,128)(2,1)S(1)}, bf16[2,64,128]{2,1,0:T(8,128)(2,1)}, u32[]{:S(2)}) copy-start(bf16[2,64,128]{2,1,0:T(8,128)(2,1)} %oweight.3) | copy-start | bytes 98308
  44.1 31.5 %copy-start.5 = (f32[2,64]{1,0:T(2,128)S(1)}, f32[2,64]{1,0:T(2,128)}, u32[]{:S(2)}) copy-start(f32[2,64]{1,0:T(2,128)} %hgain.3) | copy-start | bytes 1540
  50.7 1.6 %collective-permute-start.3 = (bf16[384,384]{1,0:T(8,128)(2,1)S(1)}, bf16[384,384]{1,0:T(8,128)(2,1)S(1)}, u32[]{:S(2)}, u32[]{:S(2)}) collective-permute-start(bf16[384,384]{1,0:T(8,128)(2,1)S(1)} %collective-permute-done.right_y), channel_id=1, source_target_pairs={{0,1},{1,0},{2,3},{3,2},{4,5},{5,4},{6,7},{7,6},{8,9},{9,8},{10,11... | collective-permute-start | bytes 884744 | tf_op jit(solution)/shard_map/ppermute | solution.py:288
  105.9 3.0 %collective-permute-start.5 = (bf16[384,384]{1,0:T(8,128)(2,1)S(1)}, bf16[384,384]{1,0:T(8,128)(2,1)S(1)}, u32[]{:S(2)}, u32[]{:S(2)}) collective-permute-start(bf16[384,384]{1,0:T(8,128)(2,1)S(1)} %shard_map.71.left), channel_id=1, source_target_pairs={{0,1},{1,0},{2,3},{3,2},{4,5},{5,4},{6,7},{7,6},{8,9},{9,8},{10,11... | collective-permute-start | bytes 884744 | tf_op jit(solution)/shard_map/ppermute | solution.py:288
  106.0 9.4 %collective-permute-start.4 = (bf16[384,384]{1,0:T(8,128)(2,1)S(1)}, bf16[384,384]{1,0:T(8,128)(2,1)S(1)}, u32[]{:S(2)}, u32[]{:S(2)}) collective-permute-start(bf16[384,384]{1,0:T(8,128)(2,1)S(1)} %shard_map.71.left), channel_id=1, source_target_pairs={{0,4},{4,0},{1,5},{5,1},{2,6},{6,2},{3,7},{7,3},{8,12},{12,8},{9,1... | collective-permute-start | bytes 884744 | tf_op jit(solution)/shard_map/ppermute | solution.py:288
  115.5 1.6 %collective-permute-start.6 = (bf16[384,384]{1,0:T(8,128)(2,1)S(1)}, bf16[384,384]{1,0:T(8,128)(2,1)S(1)}, u32[]{:S(2)}, u32[]{:S(2)}) collective-permute-start(bf16[384,384]{1,0:T(8,128)(2,1)S(1)} %collective-permute-done.4.left_x), channel_id=1, source_target_pairs={{0,1},{1,0},{2,3},{3,2},{4,5},{5,4},{6,7},{7,6},{8,9},{9,8},{10,11... | collective-permute-start | bytes 884744 | tf_op jit(solution)/shard_map/ppermute | solution.py:288

commit v6 on v4

--- a/solution.py
+++ b/solution.py
@@ -194,13 +194,16 @@
     return jnp.concatenate(tiles, axis=1).astype(BF16)
 
 
-def split_out_kernel(got, me, left, right):
-    for a in range(8):
-        left[a * SIDE : (a + 1) * SIDE, :] = dense(got, [a * 8 + b for b in range(8)], 0)
+def out_right_kernel(got, me, right):
     for a in range(4):
         for n, core in enumerate((me[0], 1 - me[0])):
             start = n * 192 + a * SIDE
             right[start : start + SIDE, :] = dense(got, [(2 * a + core) * 8 + b for b in range(8)], SLOT)
+
+
+def out_left_kernel(got, left):
+    for a in range(8):
+        left[a * SIDE : (a + 1) * SIDE, :] = dense(got, [a * 8 + b for b in range(8)], 0)
 
 
 def send_back(total, blocks, place, out):
@@ -229,10 +232,14 @@
         send_back(total, 8, lambda a, b: a * 8 + (2 * (b // 2) + owner) * 2 + b % 2, out)
 
 
-def split_in_kernel(got, left, right):
+def in_left_kernel(got, out, left):
     for r in range(8):
         rows = slice(r * SIDE, (r + 1) * SIDE)
         left[rows, :] = dense(got, [(r + 8 * h) * 4 + b for h in range(2) for b in range(4)], 0)
+    out[...] = left[...].T
+
+
+def in_right_kernel(got, right):
     lane = lane_of(SIDE)
     for r in range(16):
         for b in range(0, 4, 2):
@@ -241,17 +248,16 @@
             right[r * SIDE : (r + 1) * SIDE, b * SLOT : (b + 2) * SLOT] = tile.astype(BF16)
 
 
-def mix_in_kernel(right, left, left_c, left_x, left_d, me, out):
+def mix_in_kernel(right, left, left_c, left_x, left_d, me, core, out):
     for step, ref in enumerate((left, left_c, left_x, left_d)):
-        tall = ref[...].T
-        total = jnp.dot(tall[:192], right[:384, :], preferred_element_type=F32)
-        total += jnp.dot(tall[192:], right[384:, :], preferred_element_type=F32)
-        core = me[1] if step % 2 == 0 else 1 - me[1]
+        total = jnp.dot(ref[:192, :], right[:384, :], preferred_element_type=F32)
+        total += jnp.dot(ref[192:, :], right[384:, :], preferred_element_type=F32)
+        c = core[0] if step % 2 == 0 else 1 - core[0]
         low = me[0] if step < 2 else 1 - me[0]
         send_back(
             total,
             4,
-            lambda a, b: (2 * (a // 2) + low) * 16 + (2 * (a % 2) + core) * 4 + b,
+            lambda a, b: (2 * (a // 2) + low) * 16 + (2 * (a % 2) + c) * 4 + b,
             out,
         )
 
@@ -276,7 +282,8 @@
     block = pltpu.VMEM(BLOCK, BF16)
     gain32, weight = pltpu.VMEM((2, LANES), F32), pltpu.VMEM((LANES, 4 * CH), BF16)
     out_axes, in_axes = ("yh", "zl", "xh", "xl", "zh"), ("yh", "yl", "zl", "xh", "zh")
-    core = lax.axis_index("c")
+    tie = lax.optimization_barrier
+    pair, core, low_y, low_x = tie((pair, *(lax.axis_index(name).reshape(1) for name in ("c", "yl", "xl"))))
 
     (sent,) = call(
         project_kernel,
@@ -286,35 +293,31 @@
         inputs=HBM,
         limit=55 << 20,
     )(pair, norm_gain, proj_weight)
-    (gate,) = call(functools.partial(gate_kernel, 0), [GATE], 3, [normed], dtype=F32)(pair, norm_gain, gate_weight)
     got = lax.all_to_all(sent, out_axes, 0, 0, tiled=True)
-    left, right = call(split_out_kernel, [(384, 384)] * 2, 1, smem=1)(got, core.reshape(1))
-    right_y = swap(right, "yl")
+    (right,) = call(out_right_kernel, [(384, 384)], 1, smem=1)(got, core)
+    right_y, right_c = swap(right, "yl"), swap(right, "c")
+    got, right = tie((got, right))
+    (left,) = call(out_left_kernel, [(384, 384)], 1)(got)
+    left_c = swap(left, "c")
+    source, left = tie((pair, left))
+    (gate,) = call(functools.partial(gate_kernel, 0), [GATE], 3, [normed], dtype=F32)(source, norm_gain, gate_weight)
+    right_y, gate = tie((right_y, gate))
     (sent,) = call(mix_out_kernel, [BACK], 6, smem=1)(
-        left,
-        swap(left, "c"),
-        right,
-        swap(right, "c"),
-        right_y,
-        swap(right_y, "c"),
-        lax.axis_index("yl").reshape(1),
+        left, left_c, right, right_c, right_y, swap(right_y, "c"), low_y
     )
     mixed = lax.all_to_all(sent, out_axes, 0, 0, tiled=True)
     first, sent = call(middle_kernel, [BLOCK, MESSAGE], 7, [normed, mixed32, hidden, staged, extra])(
         pair, gate, mixed, norm_gain, hid_gain, out_weight, proj_weight
     )
-    (gate,) = call(functools.partial(gate_kernel, 1), [GATE], 3, [normed], dtype=F32)(first, norm_gain, gate_weight)
     got = lax.all_to_all(sent, in_axes, 0, 0, tiled=True)
-    left, right = call(split_in_kernel, [(384, 384), (768, 256)], 1)(got)
-    left_x = swap(left, "xl")
-    (sent,) = call(mix_in_kernel, [BACK], 5, smem=1)(
-        right,
-        left,
-        swap(left, "c"),
-        left_x,
-        swap(left_x, "c"),
-        jnp.stack([lax.axis_index("xl"), core]),
-    )
+    (left,) = call(in_left_kernel, [(384, 384)], 1, [pltpu.VMEM((384, 384), BF16)])(got)
+    left_x, left_c = swap(left, "xl"), swap(left, "c")
+    got, left = tie((got, left))
+    (right,) = call(in_right_kernel, [(768, 256)], 1)(got)
+    source, right = tie((first, right))
+    (gate,) = call(functools.partial(gate_kernel, 1), [GATE], 3, [normed], dtype=F32)(source, norm_gain, gate_weight)
+    left_x, gate = tie((left_x, gate))
+    (sent,) = call(mix_in_kernel, [BACK], 5, smem=2)(right, left, left_c, left_x, swap(left_x, "c"), low_x, core)
     mixed = lax.all_to_all(sent, in_axes, 0, 0, tiled=True)
     (updated,) = call(
         last_kernel,

time: 142 us -> 139 us (0.979)
  blocking collectives: 27.6 us -> 111 us
  waiting for transfers between devices: 67.6 us -> 11.1 us
  starting transfers between devices: 30.6 us -> 2.76 us
  Pallas kernels: 15.1 us -> 13.3 us
    all_to_all x0 -> x3, blocking collectives: none -> 83.4 us  [the longest x1 36.3 us: body(): got = lax.all_to_all(sent, out_axes, 0, 0, tiled=True)]
    all_to_all x3 -> x0, waiting for transfers between devices: 53.5 us -> none  [the longest x1 21.5 us: body(): got = lax.all_to_all(sent, out_axes, 0, 0, tiled=True)]
    all_to_all x3 -> x0, starting transfers between devices: 28 us -> none  [the longest x1 14.7 us: body(): got = lax.all_to_all(sent, out_axes, 0, 0, tiled=True)]
    ppermute x7, waiting for transfers between devices: 14.1 us -> 11.1 us  [swap(): return lax.ppermute(values, axes, [(i, n - 1 - i) for i in range(n)])]
    pallas_call x3 -> x5, Pallas kernels: 3.02 us -> 1.91 us  [the longest x1 0.65 us: body(): call(mix_in_kernel, [BACK], 5, smem=2)]
  transfers between devices with their start and end apart: 10 -> 7, of which waited for: 7 -> 4; matrix products, arithmetic and copies ran while one was open for 0% -> 0% of each run, Pallas kernels for 2% -> 2%
where the time goes in v6:
time: 139 us
  blocking collectives  111 us (80%)
  Pallas kernels  13.3 us (10%)
  waiting for transfers between devices  11.1 us (8%)
  starting transfers between devices  2.76 us (2%)
    all_to_all x1, blocking collectives, body(): got = lax.all_to_all(sent, out_axes, 0, 0, tiled=True)  36.3 us
    all_to_all x1, blocking collectives, body(): got = lax.all_to_all(sent, in_axes, 0, 0, tiled=True)  27.6 us
    all_to_all x1, blocking collectives, body(): mixed = lax.all_to_all(sent, out_axes, 0, 0, tiled=True)  23.6 us
    all_to_all x1, blocking collectives, body(): mixed = lax.all_to_all(sent, in_axes, 0, 0, tiled=True)  23.6 us
    ppermute x7, waiting for transfers between devices, swap(): return lax.ppermute(values, axes, [(i, n - 1 - i) for i in range(n)])  11.1 us
    pallas_call x1, Pallas kernels, body(): call(project_kernel, [MESSAGE], 3, [block, gain32, weight, pltpu.Semaphor...  4.21 us
    pallas_call x1, Pallas kernels, body(): call(middle_kernel, [BLOCK, MESSAGE], 7, [normed, mixed32, hidden, staged...  2.83 us
  transfers between devices with their start and end apart: 7, of which 4 were waited for; matrix products, arithmetic and copies ran while one was open for 0% of the time, Pallas kernels for 2%

profile of v6, /device:TPU:2, one launch (start us, length us, event | category | flops | bytes accessed | tf_op | source)
XLA Modules:
  0.0 138.5 jit_solution(8250136728328570889)
XLA Ops:
  0.0 4.2 %shard_map.64 = bf16[64,40,128]{2,1,0:T(8,128)(2,1)} custom-call(bf16[48,48,128]{2,1,0:T(8,128)(2,1)} %pair.1, f32[2,128]{1,0:T(2,128)} %gain.5, bf16[2,128,256]{2,1,0:T(8,128)(2,1)} %weight.1), custom_call_target="tpu_custom_call" | custom-call | tf_op jit(solution)/shard_map/pallas_call | solution.py:288
  4.2 0.0 copy-start
  4.2 0.0 copy-start.2
  4.2 0.0 copy-start.4
  4.3 36.3 %all_to_all.20.got = bf16[64,40,128]{2,1,0:T(8,128)(2,1)S(1)} all-to-all(bf16[64,40,128]{2,1,0:T(8,128)(2,1)} %shard_map.64), channel_id=1, replica_groups=mesh['yh'=2,'yl'=2,'zl'=4,'xh'=2,'xl'=2,'zh'=2,'c'=2] {'yh','zl','xh','x..., dimensions={0} | all-to-all | bytes 1310720 | tf_op jit(solution)/shard_map/all_to_all | solution.py:296
  40.5 0.3 shard_map.65.right
  40.8 0.8 collective-permute-start
  41.6 0.3 shard_map.66.left
  41.9 0.1 collective-permute-start.1
  42.0 0.5 collective-permute-start.2
  42.5 1.1 shard_map.67.gate
  43.6 0.0 copy-start.1
  43.7 0.0 copy-start.3
  43.7 0.0 copy-start.5
  43.7 3.9 %collective-permute-done.right_y = bf16[384,384]{1,0:T(8,128)(2,1)S(1)} collective-permute-done((bf16[384,384]{1,0:T(8,128)(2,1)S(1)}, bf16[384,384]{1,0:T(8,128)(2,1)S(1)}, u32[]{:S(2)}, u32[]{:S(2)}) %collective-permute-start) | collective-permute-done | bytes 294944 | tf_op jit(solution)/shard_map/ppermute | solution.py:267
  47.6 0.0 collective-permute-start.3
  47.6 0.0 collective-permute-done.1.left_c
  47.6 1.6 %collective-permute-done.3.right_yc = bf16[384,384]{1,0:T(8,128)(2,1)S(1)} collective-permute-done((bf16[384,384]{1,0:T(8,128)(2,1)S(1)}, bf16[384,384]{1,0:T(8,128)(2,1)S(1)}, u32[]{:S(2)}, u32[]{:S(2)}) %collective-permute-start.3) | collective-permute-done | bytes 294944 | tf_op jit(solution)/shard_map/ppermute | solution.py:267
  49.2 0.7 shard_map.68
  49.9 23.6 %all_to_all.21.mixed = bf16[64,24,128]{2,1,0:T(8,128)(2,1)S(1)} all-to-all(bf16[64,24,128]{2,1,0:T(8,128)(2,1)S(1)} %shard_map.68), channel_id=1, replica_groups=mesh['yh'=2,'yl'=2,'zl'=4,'xh'=2,'xl'=2,'zh'=2,'c'=2] {'yh','zl','xh','x..., dimensions={0} | all-to-all | bytes 786432 | tf_op jit(solution)/shard_map/all_to_all | solution.py:308
  73.5 2.8 %shard_map.69 = (bf16[48,48,128]{2,1,0:T(8,128)(2,1)S(1)}, bf16[64,40,128]{2,1,0:T(8,128)(2,1)S(1)}) custom-call(bf16[48,48,128]{2,1,0:T(8,128)(2,1)S(1)} %copy-done, f32[3072,128]{1,0:T(8,128)S(1)} %shard_map.67.gate, bf16[64,24,128]{2,1,0:T(8,128)(2,1)S(1)} %all_to_all.21.mixed, f32[2,128]{1,0:T(2,128)S(1)} %copy-done.4, f32[2,64]{1,0:T(2,128)S(1)} %copy-done.5, ...), custom_call_target="tpu_custom_call" | custom-call | tf_op jit(solution)/shard_map/pallas_call | solution.py:309
  76.4 27.6 %all_to_all.22.got = bf16[64,40,128]{2,1,0:T(8,128)(2,1)S(1)} all-to-all(bf16[64,40,128]{2,1,0:T(8,128)(2,1)S(1)} %get-tuple-element.33), channel_id=1, replica_groups=mesh['yh'=2,'yl'=2,'zl'=4,'xh'=2,'xl'=2,'zh'=2,'c'=2] {'yh','yl','zl','x..., dimensions={0} | all-to-all | bytes 1310720 | tf_op jit(solution)/shard_map/all_to_all | solution.py:312
  104.0 0.4 shard_map.70.left
  104.4 1.4 %collective-permute-start.4 = (bf16[384,384]{1,0:T(8,128)(2,1)S(1)}, bf16[384,384]{1,0:T(8,128)(2,1)S(1)}, u32[]{:S(2)}, u32[]{:S(2)}) collective-permute-start(bf16[384,384]{1,0:T(8,128)(2,1)S(1)} %shard_map.70.left), channel_id=1, source_target_pairs={{0,4},{4,0},{1,5},{5,1},{2,6},{6,2},{3,7},{7,3},{8,12},{12,8},{9,1... | collective-permute-start | bytes 884744 | tf_op jit(solution)/shard_map/ppermute | solution.py:267
  105.8 0.0 collective-permute-start.5
  105.8 0.3 shard_map.71.right
  106.1 1.1 shard_map.72.gate
  107.2 4.0 %collective-permute-done.4.left_x = bf16[384,384]{1,0:T(8,128)(2,1)S(1)} collective-permute-done((bf16[384,384]{1,0:T(8,128)(2,1)S(1)}, bf16[384,384]{1,0:T(8,128)(2,1)S(1)}, u32[]{:S(2)}, u32[]{:S(2)}) %collective-permute-start.4) | collective-permute-done | bytes 294944 | tf_op jit(solution)/shard_map/ppermute | solution.py:267
  111.2 1.6 %collective-permute-done.6.left_d = bf16[384,384]{1,0:T(8,128)(2,1)S(1)} collective-permute-done((bf16[384,384]{1,0:T(8,128)(2,1)S(1)}, bf16[384,384]{1,0:T(8,128)(2,1)S(1)}, u32[]{:S(2)}, u32[]{:S(2)}) %collective-permute-start.6) | collective-permute-done | bytes 294944 | tf_op jit(solution)/shard_map/ppermute | solution.py:267
  112.8 0.6 shard_map.73
  113.4 23.6 %all_to_all.23.mixed = bf16[64,24,128]{2,1,0:T(8,128)(2,1)S(1)} all-to-all(bf16[64,24,128]{2,1,0:T(8,128)(2,1)S(1)} %shard_map.73), channel_id=1, replica_groups=mesh['yh'=2,'yl'=2,'zl'=4,'xh'=2,'xl'=2,'zh'=2,'c'=2] {'yh','yl','zl','x..., dimensions={0} | all-to-all | bytes 786432 | tf_op jit(solution)/shard_map/all_to_all | solution.py:321
  137.0 1.4 shard_map.74
  (9 shorter events, 0.0 us)
Async XLA Ops:
  4.2 38.3 %copy-start = (bf16[48,48,128]{2,1,0:T(8,128)(2,1)S(1)}, bf16[48,48,128]{2,1,0:T(8,128)(2,1)}, u32[]{:S(2)}) copy-start(bf16[48,48,128]{2,1,0:T(8,128)(2,1)} %pair.1) | copy-start | bytes 1769476
  4.2 38.3 %copy-start.2 = (bf16[2,128,128]{2,1,0:T(8,128)(2,1)S(1)}, bf16[2,128,128]{2,1,0:T(8,128)(2,1)}, u32[]{:S(2)}) copy-start(bf16[2,128,128]{2,1,0:T(8,128)(2,1)} %gweight.3) | copy-start | bytes 196612
  4.2 38.3 %copy-start.4 = (f32[2,128]{1,0:T(2,128)S(1)}, f32[2,128]{1,0:T(2,128)}, u32[]{:S(2)}) copy-start(f32[2,128]{1,0:T(2,128)} %gain.5) | copy-start | bytes 3076
  40.8 6.8 %collective-permute-start = (bf16[384,384]{1,0:T(8,128)(2,1)S(1)}, bf16[384,384]{1,0:T(8,128)(2,1)S(1)}, u32[]{:S(2)}, u32[]{:S(2)}) collective-permute-start(bf16[384,384]{1,0:T(8,128)(2,1)S(1)} %shard_map.65.right), channel_id=1, source_target_pairs={{0,64},{64,0},{1,65},{65,1},{2,66},{66,2},{3,67},{67,3},{4,68},{68... | collective-permute-start | bytes 884744 | tf_op jit(solution)/shard_map/ppermute | solution.py:267
  41.9 5.7 %collective-permute-start.1 = (bf16[384,384]{1,0:T(8,128)(2,1)S(1)}, bf16[384,384]{1,0:T(8,128)(2,1)S(1)}, u32[]{:S(2)}, u32[]{:S(2)}) collective-permute-start(bf16[384,384]{1,0:T(8,128)(2,1)S(1)} %shard_map.66.left), channel_id=1, source_target_pairs={{0,1},{1,0},{2,3},{3,2},{4,5},{5,4},{6,7},{7,6},{8,9},{9,8},{10,11... | collective-permute-start | bytes 884744 | tf_op jit(solution)/shard_map/ppermute | solution.py:267
  42.0 5.6 %collective-permute-start.2 = (bf16[384,384]{1,0:T(8,128)(2,1)S(1)}, bf16[384,384]{1,0:T(8,128)(2,1)S(1)}, u32[]{:S(2)}, u32[]{:S(2)}) collective-permute-start(bf16[384,384]{1,0:T(8,128)(2,1)S(1)} %shard_map.65.right), channel_id=1, source_target_pairs={{0,1},{1,0},{2,3},{3,2},{4,5},{5,4},{6,7},{7,6},{8,9},{9,8},{10,11... | collective-permute-start | bytes 884744 | tf_op jit(solution)/shard_map/ppermute | solution.py:267
  43.6 29.9 %copy-start.1 = (bf16[2,128,256]{2,1,0:T(8,128)(2,1)S(1)}, bf16[2,128,256]{2,1,0:T(8,128)(2,1)}, u32[]{:S(2)}) copy-start(bf16[2,128,256]{2,1,0:T(8,128)(2,1)} %weight.1) | copy-start | bytes 393220
  43.7 29.9 %copy-start.3 = (bf16[2,64,128]{2,1,0:T(8,128)(2,1)S(1)}, bf16[2,64,128]{2,1,0:T(8,128)(2,1)}, u32[]{:S(2)}) copy-start(bf16[2,64,128]{2,1,0:T(8,128)(2,1)} %oweight.3) | copy-start | bytes 98308
  43.7 29.9 %copy-start.5 = (f32[2,64]{1,0:T(2,128)S(1)}, f32[2,64]{1,0:T(2,128)}, u32[]{:S(2)}) copy-start(f32[2,64]{1,0:T(2,128)} %hgain.3) | copy-start | bytes 1540
  47.6 1.6 %collective-permute-start.3 = (bf16[384,384]{1,0:T(8,128)(2,1)S(1)}, bf16[384,384]{1,0:T(8,128)(2,1)S(1)}, u32[]{:S(2)}, u32[]{:S(2)}) collective-permute-start(bf16[384,384]{1,0:T(8,128)(2,1)S(1)} %collective-permute-done.right_y), channel_id=1, source_target_pairs={{0,1},{1,0},{2,3},{3,2},{4,5},{5,4},{6,7},{7,6},{8,9},{9,8},{10,11... | collective-permute-start | bytes 884744 | tf_op jit(solution)/shard_map/ppermute | solution.py:267
  104.4 6.8 %collective-permute-start.4 = (bf16[384,384]{1,0:T(8,128)(2,1)S(1)}, bf16[384,384]{1,0:T(8,128)(2,1)S(1)}, u32[]{:S(2)}, u32[]{:S(2)}) collective-permute-start(bf16[384,384]{1,0:T(8,128)(2,1)S(1)} %shard_map.70.left), channel_id=1, source_target_pairs={{0,4},{4,0},{1,5},{5,1},{2,6},{6,2},{3,7},{7,3},{8,12},{12,8},{9,1... | collective-permute-start | bytes 884744 | tf_op jit(solution)/shard_map/ppermute | solution.py:267
  105.8 5.4 %collective-permute-start.5 = (bf16[384,384]{1,0:T(8,128)(2,1)S(1)}, bf16[384,384]{1,0:T(8,128)(2,1)S(1)}, u32[]{:S(2)}, u32[]{:S(2)}) collective-permute-start(bf16[384,384]{1,0:T(8,128)(2,1)S(1)} %shard_map.70.left), channel_id=1, source_target_pairs={{0,1},{1,0},{2,3},{3,2},{4,5},{5,4},{6,7},{7,6},{8,9},{9,8},{10,11... | collective-permute-start | bytes 884744 | tf_op jit(solution)/shard_map/ppermute | solution.py:267
  111.2 1.6 %collective-permute-start.6 = (bf16[384,384]{1,0:T(8,128)(2,1)S(1)}, bf16[384,384]{1,0:T(8,128)(2,1)S(1)}, u32[]{:S(2)}, u32[]{:S(2)}) collective-permute-start(bf16[384,384]{1,0:T(8,128)(2,1)S(1)} %collective-permute-done.4.left_x), channel_id=1, source_target_pairs={{0,1},{1,0},{2,3},{3,2},{4,5},{5,4},{6,7},{7,6},{8,9},{9,8},{10,11... | collective-permute-start | bytes 884744 | tf_op jit(solution)/shard_map/ppermute | solution.py:267

commit v7 on v6

--- a/solution.py
+++ b/solution.py
@@ -15,7 +15,8 @@
 MAIN = 40
 EXTRA = SIDE - MAIN
 STRIDE = 72
-GROUP = 8
+GROUP = 16
+KEPT = 18
 PIECE = 16
 CH = 64
 LANES = 128
@@ -119,14 +120,27 @@
 
 def read_sums(mixed, mixed32):
     for channel in range(CH):
-        mixed32[pl.ds(channel * HALF, HALF), :] = mixed[channel].astype(F32)
+        for t in range(KEPT // 2):
+            tile = mixed[channel, :, t * LANES : (t + 1) * LANES].astype(F32)
+            mixed32[pl.ds(channel * HALF + 2 * t, 2), :] = tile
+
+
+def sums_of(mixed32, s):
+    if s < KEPT:
+        return mixed32[pl.ds(s, CH, stride=HALF), :]
+    lane, sums = lane_of(CH) % SLOT, None
+    for g in range(SIDE // PIECE):
+        part = mixed32[pl.ds(g * (HALF - KEPT) + s - KEPT, CH, stride=HALF), :]
+        part = pltpu.roll(part, LANES - SIDE + g * PIECE, 1)
+        sums = part if sums is None else jnp.where(lane < g * PIECE, sums, part)
+    return sums
 
 
 def finish(pair, gate, mixed, hgain, oweight, z_out, mixed32, hidden, ready=lambda s: None):
     hcol = hgain.T
     read_sums(mixed, mixed32)
     for s in range(0, HALF, 4):
-        sums = [mixed32[pl.ds(s + t, CH, stride=HALF), :] for t in range(4)]
+        sums = [sums_of(mixed32, s + t) for t in range(4)]
         sums = [layer_norm(values, hcol, 0).astype(BF16) for values in sums]
         for t in range(4):
             hidden[s + t] = sums[t]
@@ -212,8 +226,17 @@
         for b in range(0, 4, 2):
             tile = total[a * SIDE : (a + 1) * SIDE, b * SLOT : (b + 2) * SLOT]
             low, high = tile[:HALF], tile[HALF:]
-            out[place(a, b)] = jnp.where(lane < SLOT, low, pltpu.roll(high, SLOT, 1)).astype(BF16)
-            out[place(a, b + 1)] = jnp.where(lane < SLOT, pltpu.roll(low, SLOT, 1), high).astype(BF16)
+            write_sums(jnp.where(lane < SLOT, low, pltpu.roll(high, SLOT, 1)), place(a, b), out)
+            write_sums(jnp.where(lane < SLOT, pltpu.roll(low, SLOT, 1), high), place(a, b + 1), out)
+
+
+def write_sums(rows, p, out):
+    last = rows[16:]
+    spare = [pltpu.roll(last, SIDE - g * PIECE, 1)[KEPT - 16 :] for g in range(SIDE // PIECE)]
+    lane = lane_of(KEPT) % SLOT
+    rows = jnp.where(lane < SIDE, rows[:KEPT], jnp.concatenate(spare, axis=0)).astype(BF16)
+    for t in range(KEPT // 2):
+        out[p, :, t * LANES : (t + 1) * LANES] = rows[2 * t : 2 * t + 2]
 
 
 def padded(ref, start):
@@ -268,7 +291,7 @@
 
 
 MESSAGE = (CH, MAIN, LANES)
-BACK = (CH, HALF, LANES)
+BACK = (CH, 2, KEPT // 2 * LANES)
 BLOCK = (SIDE, SIDE, LANES)
 GATE = (HALF * LANES, LANES)
 

time: 139 us -> 135 us (0.971)
  blocking collectives: 111 us -> 107 us
    all_to_all x1, blocking collectives: 23.6 us -> 21.6 us  [body(): mixed = lax.all_to_all(sent, out_axes, 0, 0, tiled=True)]
    all_to_all x1, blocking collectives: 23.6 us -> 21.7 us  [body(): mixed = lax.all_to_all(sent, in_axes, 0, 0, tiled=True)]
where the time goes in v7:
time: 135 us
  blocking collectives  107 us (79%)
  Pallas kernels  13.7 us (10%)
  waiting for transfers between devices  11.1 us (8%)
  starting transfers between devices  2.83 us (2%)
    all_to_all x1, blocking collectives, body(): got = lax.all_to_all(sent, out_axes, 0, 0, tiled=True)  36.3 us
    all_to_all x1, blocking collectives, body(): got = lax.all_to_all(sent, in_axes, 0, 0, tiled=True)  27.5 us
    all_to_all x1, blocking collectives, body(): mixed = lax.all_to_all(sent, in_axes, 0, 0, tiled=True)  21.7 us
    all_to_all x1, blocking collectives, body(): mixed = lax.all_to_all(sent, out_axes, 0, 0, tiled=True)  21.6 us
    ppermute x7, waiting for transfers between devices, swap(): return lax.ppermute(values, axes, [(i, n - 1 - i) for i in range(n)])  11.1 us
    pallas_call x1, Pallas kernels, body(): call(project_kernel, [MESSAGE], 3, [block, gain32, weight, pltpu.Semaphor...  3.77 us
    pallas_call x1, Pallas kernels, body(): call(middle_kernel, [BLOCK, MESSAGE], 7, [normed, mixed32, hidden, staged...  2.95 us
    ppermute x7, starting transfers between devices, swap(): return lax.ppermute(values, axes, [(i, n - 1 - i) for i in range(n)])  2.83 us
  transfers between devices with their start and end apart: 7, of which 4 were waited for; matrix products, arithmetic and copies ran while one was open for 0% of the time, Pallas kernels for 2%

profile of v7, /device:TPU:2, one launch (start us, length us, event | category | flops | bytes accessed | tf_op | source)
XLA Modules:
  0.0 135.0 jit_solution(7286732557010593975)
XLA Ops:
  0.0 3.8 %shard_map.64 = bf16[64,40,128]{2,1,0:T(8,128)(2,1)} custom-call(bf16[48,48,128]{2,1,0:T(8,128)(2,1)} %pair.1, f32[2,128]{1,0:T(2,128)} %gain.5, bf16[2,128,256]{2,1,0:T(8,128)(2,1)} %weight.1), custom_call_target="tpu_custom_call" | custom-call | tf_op jit(solution)/shard_map/pallas_call | solution.py:311
  3.8 0.0 copy-start
  3.8 0.0 copy-start.2
  3.8 0.0 copy-start.4
  3.8 36.3 %all_to_all.20.got = bf16[64,40,128]{2,1,0:T(8,128)(2,1)S(1)} all-to-all(bf16[64,40,128]{2,1,0:T(8,128)(2,1)} %shard_map.64), channel_id=1, replica_groups=mesh['yh'=2,'yl'=2,'zl'=4,'xh'=2,'xl'=2,'zh'=2,'c'=2] {'yh','zl','xh','x..., dimensions={0} | all-to-all | bytes 1310720 | tf_op jit(solution)/shard_map/all_to_all | solution.py:319
  40.1 0.3 shard_map.65.right
  40.4 0.9 collective-permute-start
  41.2 0.3 shard_map.66.left
  41.6 0.1 collective-permute-start.1
  41.7 0.5 collective-permute-start.2
  42.2 1.1 shard_map.67.gate
  43.3 0.0 copy-start.1
  43.3 0.0 copy-start.3
  43.3 0.0 copy-start.5
  43.3 3.9 %collective-permute-done.right_y = bf16[384,384]{1,0:T(8,128)(2,1)S(1)} collective-permute-done((bf16[384,384]{1,0:T(8,128)(2,1)S(1)}, bf16[384,384]{1,0:T(8,128)(2,1)S(1)}, u32[]{:S(2)}, u32[]{:S(2)}) %collective-permute-start) | collective-permute-done | bytes 294944 | tf_op jit(solution)/shard_map/ppermute | solution.py:290
  47.2 0.0 collective-permute-start.3
  47.2 0.0 collective-permute-done.1.left_c
  47.2 0.0 collective-permute-done.2.right_c
  47.2 1.6 %collective-permute-done.3.right_yc = bf16[384,384]{1,0:T(8,128)(2,1)S(1)} collective-permute-done((bf16[384,384]{1,0:T(8,128)(2,1)S(1)}, bf16[384,384]{1,0:T(8,128)(2,1)S(1)}, u32[]{:S(2)}, u32[]{:S(2)}) %collective-permute-start.3) | collective-permute-done | bytes 294944 | tf_op jit(solution)/shard_map/ppermute | solution.py:290
  48.8 1.0 shard_map.68
  49.8 21.6 %all_to_all.21.mixed = bf16[64,2,1152]{2,1,0:T(2,128)(2,1)S(1)} all-to-all(bf16[64,2,1152]{2,1,0:T(2,128)(2,1)S(1)} %shard_map.68), channel_id=1, replica_groups=mesh['yh'=2,'yl'=2,'zl'=4,'xh'=2,'xl'=2,'zh'=2,'c'=2] {'yh','zl','xh','x..., dimensions={0} | all-to-all | bytes 589824 | tf_op jit(solution)/shard_map/all_to_all | solution.py:331
  71.4 2.9 %shard_map.69 = (bf16[48,48,128]{2,1,0:T(8,128)(2,1)S(1)}, bf16[64,40,128]{2,1,0:T(8,128)(2,1)S(1)}) custom-call(bf16[48,48,128]{2,1,0:T(8,128)(2,1)S(1)} %copy-done, f32[3072,128]{1,0:T(8,128)S(1)} %shard_map.67.gate, bf16[64,2,1152]{2,1,0:T(2,128)(2,1)S(1)} %all_to_all.21.mixed, f32[2,128]{1,0:T(2,128)S(1)} %copy-done.4, f32[2,64]{1,0:T(2,128)S(1)} %copy-done.5, ...), custom_call_target="tpu_custom_call" | custom-call | tf_op jit(solution)/shard_map/pallas_call | solution.py:332
  74.3 27.5 %all_to_all.22.got = bf16[64,40,128]{2,1,0:T(8,128)(2,1)S(1)} all-to-all(bf16[64,40,128]{2,1,0:T(8,128)(2,1)S(1)} %get-tuple-element.33), channel_id=1, replica_groups=mesh['yh'=2,'yl'=2,'zl'=4,'xh'=2,'xl'=2,'zh'=2,'c'=2] {'yh','yl','zl','x..., dimensions={0} | all-to-all | bytes 1310720 | tf_op jit(solution)/shard_map/all_to_all | solution.py:335
  101.9 0.4 shard_map.70.left
  102.3 1.4 %collective-permute-start.4 = (bf16[384,384]{1,0:T(8,128)(2,1)S(1)}, bf16[384,384]{1,0:T(8,128)(2,1)S(1)}, u32[]{:S(2)}, u32[]{:S(2)}) collective-permute-start(bf16[384,384]{1,0:T(8,128)(2,1)S(1)} %shard_map.70.left), channel_id=1, source_target_pairs={{0,4},{4,0},{1,5},{5,1},{2,6},{6,2},{3,7},{7,3},{8,12},{12,8},{9,1... | collective-permute-start | bytes 884744 | tf_op jit(solution)/shard_map/ppermute | solution.py:290
  103.6 0.3 shard_map.71.right
  103.9 1.1 shard_map.72.gate
  105.0 4.1 %collective-permute-done.4.left_x = bf16[384,384]{1,0:T(8,128)(2,1)S(1)} collective-permute-done((bf16[384,384]{1,0:T(8,128)(2,1)S(1)}, bf16[384,384]{1,0:T(8,128)(2,1)S(1)}, u32[]{:S(2)}, u32[]{:S(2)}) %collective-permute-start.4) | collective-permute-done | bytes 294944 | tf_op jit(solution)/shard_map/ppermute | solution.py:290
  109.1 1.6 %collective-permute-done.6.left_d = bf16[384,384]{1,0:T(8,128)(2,1)S(1)} collective-permute-done((bf16[384,384]{1,0:T(8,128)(2,1)S(1)}, bf16[384,384]{1,0:T(8,128)(2,1)S(1)}, u32[]{:S(2)}, u32[]{:S(2)}) %collective-permute-start.6) | collective-permute-done | bytes 294944 | tf_op jit(solution)/shard_map/ppermute | solution.py:290
  110.7 0.9 shard_map.73
  111.5 21.7 %all_to_all.23.mixed = bf16[64,2,1152]{2,1,0:T(2,128)(2,1)S(1)} all-to-all(bf16[64,2,1152]{2,1,0:T(2,128)(2,1)S(1)} %shard_map.73), channel_id=1, replica_groups=mesh['yh'=2,'yl'=2,'zl'=4,'xh'=2,'xl'=2,'zh'=2,'c'=2] {'yh','yl','zl','x..., dimensions={0} | all-to-all | bytes 589824 | tf_op jit(solution)/shard_map/all_to_all | solution.py:344
  133.2 1.7 %shard_map.74 = bf16[48,48,128]{2,1,0:T(8,128)(2,1)} custom-call(bf16[48,48,128]{2,1,0:T(8,128)(2,1)S(1)} %get-tuple-element.35.pair, f32[3072,128]{1,0:T(8,128)S(1)} %shard_map.72.gate, bf16[64,2,1152]{2,1,0:T(2,128)(2,1)S(1)} %all_to_all.23.mixed, f32[2,64]{1,0:T(2,128)S(1)} %copy-done.5, bf16[2,64,128]{2,1,0:T(8,128)(2,1)S(1)} %copy-done.3), custom_call_target="tpu_custom_call" | custom-call | tf_op jit(solution)/shard_map/pallas_call | solution.py:345
  (9 shorter events, 0.0 us)
Async XLA Ops:
  3.8 38.4 %copy-start = (bf16[48,48,128]{2,1,0:T(8,128)(2,1)S(1)}, bf16[48,48,128]{2,1,0:T(8,128)(2,1)}, u32[]{:S(2)}) copy-start(bf16[48,48,128]{2,1,0:T(8,128)(2,1)} %pair.1) | copy-start | bytes 1769476
  3.8 38.4 %copy-start.2 = (bf16[2,128,128]{2,1,0:T(8,128)(2,1)S(1)}, bf16[2,128,128]{2,1,0:T(8,128)(2,1)}, u32[]{:S(2)}) copy-start(bf16[2,128,128]{2,1,0:T(8,128)(2,1)} %gweight.3) | copy-start | bytes 196612
  3.8 38.4 %copy-start.4 = (f32[2,128]{1,0:T(2,128)S(1)}, f32[2,128]{1,0:T(2,128)}, u32[]{:S(2)}) copy-start(f32[2,128]{1,0:T(2,128)} %gain.5) | copy-start | bytes 3076
  40.4 6.8 %collective-permute-start = (bf16[384,384]{1,0:T(8,128)(2,1)S(1)}, bf16[384,384]{1,0:T(8,128)(2,1)S(1)}, u32[]{:S(2)}, u32[]{:S(2)}) collective-permute-start(bf16[384,384]{1,0:T(8,128)(2,1)S(1)} %shard_map.65.right), channel_id=1, source_target_pairs={{0,64},{64,0},{1,65},{65,1},{2,66},{66,2},{3,67},{67,3},{4,68},{68... | collective-permute-start | bytes 884744 | tf_op jit(solution)/shard_map/ppermute | solution.py:290
  41.6 5.6 %collective-permute-start.1 = (bf16[384,384]{1,0:T(8,128)(2,1)S(1)}, bf16[384,384]{1,0:T(8,128)(2,1)S(1)}, u32[]{:S(2)}, u32[]{:S(2)}) collective-permute-start(bf16[384,384]{1,0:T(8,128)(2,1)S(1)} %shard_map.66.left), channel_id=1, source_target_pairs={{0,1},{1,0},{2,3},{3,2},{4,5},{5,4},{6,7},{7,6},{8,9},{9,8},{10,11... | collective-permute-start | bytes 884744 | tf_op jit(solution)/shard_map/ppermute | solution.py:290
  41.7 5.5 %collective-permute-start.2 = (bf16[384,384]{1,0:T(8,128)(2,1)S(1)}, bf16[384,384]{1,0:T(8,128)(2,1)S(1)}, u32[]{:S(2)}, u32[]{:S(2)}) collective-permute-start(bf16[384,384]{1,0:T(8,128)(2,1)S(1)} %shard_map.65.right), channel_id=1, source_target_pairs={{0,1},{1,0},{2,3},{3,2},{4,5},{5,4},{6,7},{7,6},{8,9},{9,8},{10,11... | collective-permute-start | bytes 884744 | tf_op jit(solution)/shard_map/ppermute | solution.py:290
  43.3 28.1 %copy-start.1 = (bf16[2,128,256]{2,1,0:T(8,128)(2,1)S(1)}, bf16[2,128,256]{2,1,0:T(8,128)(2,1)}, u32[]{:S(2)}) copy-start(bf16[2,128,256]{2,1,0:T(8,128)(2,1)} %weight.1) | copy-start | bytes 393220
  43.3 28.1 %copy-start.3 = (bf16[2,64,128]{2,1,0:T(8,128)(2,1)S(1)}, bf16[2,64,128]{2,1,0:T(8,128)(2,1)}, u32[]{:S(2)}) copy-start(bf16[2,64,128]{2,1,0:T(8,128)(2,1)} %oweight.3) | copy-start | bytes 98308
  43.3 28.1 %copy-start.5 = (f32[2,64]{1,0:T(2,128)S(1)}, f32[2,64]{1,0:T(2,128)}, u32[]{:S(2)}) copy-start(f32[2,64]{1,0:T(2,128)} %hgain.3) | copy-start | bytes 1540
  47.2 1.6 %collective-permute-start.3 = (bf16[384,384]{1,0:T(8,128)(2,1)S(1)}, bf16[384,384]{1,0:T(8,128)(2,1)S(1)}, u32[]{:S(2)}, u32[]{:S(2)}) collective-permute-start(bf16[384,384]{1,0:T(8,128)(2,1)S(1)} %collective-permute-done.right_y), channel_id=1, source_target_pairs={{0,1},{1,0},{2,3},{3,2},{4,5},{5,4},{6,7},{7,6},{8,9},{9,8},{10,11... | collective-permute-start | bytes 884744 | tf_op jit(solution)/shard_map/ppermute | solution.py:290
  102.3 6.8 %collective-permute-start.4 = (bf16[384,384]{1,0:T(8,128)(2,1)S(1)}, bf16[384,384]{1,0:T(8,128)(2,1)S(1)}, u32[]{:S(2)}, u32[]{:S(2)}) collective-permute-start(bf16[384,384]{1,0:T(8,128)(2,1)S(1)} %shard_map.70.left), channel_id=1, source_target_pairs={{0,4},{4,0},{1,5},{5,1},{2,6},{6,2},{3,7},{7,3},{8,12},{12,8},{9,1... | collective-permute-start | bytes 884744 | tf_op jit(solution)/shard_map/ppermute | solution.py:290
  103.6 5.4 %collective-permute-start.5 = (bf16[384,384]{1,0:T(8,128)(2,1)S(1)}, bf16[384,384]{1,0:T(8,128)(2,1)S(1)}, u32[]{:S(2)}, u32[]{:S(2)}) collective-permute-start(bf16[384,384]{1,0:T(8,128)(2,1)S(1)} %shard_map.70.left), channel_id=1, source_target_pairs={{0,1},{1,0},{2,3},{3,2},{4,5},{5,4},{6,7},{7,6},{8,9},{9,8},{10,11... | collective-permute-start | bytes 884744 | tf_op jit(solution)/shard_map/ppermute | solution.py:290
  109.1 1.6 %collective-permute-start.6 = (bf16[384,384]{1,0:T(8,128)(2,1)S(1)}, bf16[384,384]{1,0:T(8,128)(2,1)S(1)}, u32[]{:S(2)}, u32[]{:S(2)}) collective-permute-start(bf16[384,384]{1,0:T(8,128)(2,1)S(1)} %collective-permute-done.4.left_x), channel_id=1, source_target_pairs={{0,1},{1,0},{2,3},{3,2},{4,5},{5,4},{6,7},{7,6},{8,9},{9,8},{10,11... | collective-permute-start | bytes 884744 | tf_op jit(solution)/shard_map/ppermute | solution.py:290

commit v8 on v7

--- a/solution.py
+++ b/solution.py
@@ -12,7 +12,9 @@
 SIDE = 48
 HALF = SIDE // 2
 SLOT = 64
-MAIN = 40
+MAIN = 36
+TILE = 4
+TILES = MAIN // TILE
 EXTRA = SIDE - MAIN
 STRIDE = 72
 GROUP = 16
@@ -83,7 +85,7 @@
             for g in range(SIDE // PIECE):
                 extra[g * EXTRA + s + HALF - MAIN] = pltpu.roll(second, SIDE - g * PIECE, 1)
         else:
-            staged[pl.ds((s + HALF) * STRIDE, CH), :] = second
+            staged[pl.ds((s + HALF) * STRIDE, CH), :] = jnp.where(lane % SLOT < SIDE, second, extra[s + HALF])
         staged[pl.ds(s * STRIDE, CH), :] = jnp.where(lane % SLOT < SIDE, first, extra[s])
 
 
@@ -92,7 +94,9 @@
 
 def write_messages(staged, out):
     for channel in range(CH):
-        out[channel] = staged[pl.ds(channel, MAIN, stride=STRIDE), :].astype(BF16)
+        for t in range(TILES):
+            tile = staged[pl.ds(channel + t * TILE * STRIDE, TILE, stride=STRIDE), :]
+            out[channel, :, t * LANES : (t + 1) * LANES] = tile.astype(BF16)
 
 
 def project_kernel(pair_hbm, gain_hbm, weight_hbm, out, pair, gain, weight, sems, normed, staged, extra):
@@ -181,19 +185,26 @@
         copy.wait()
 
 
-def moved(ref, p, base, offset):
-    values = ref[p].astype(F32)
-    lane = lane_of(EXTRA)
-    tail = None
+def moved(got, p, base, offset):
+    values = got[p].astype(F32)
+    tiles = [values[:, t * LANES : (t + 1) * LANES] for t in range(TILES)]
+    main = rolled(jnp.concatenate(tiles, axis=0), offset - base)
+    first = rest = None
     for g in range(SIDE // PIECE):
         begin = offset + g * PIECE
-        part = values[g * EXTRA : (g + 1) * EXTRA]
-        shift = (begin - base - SIDE) % LANES
-        part = pltpu.roll(part, shift, 1) if shift else part
-        tail = part if tail is None else jnp.where((lane - begin) % LANES < PIECE, part, tail)
-    shift = (offset - base) % LANES
-    main = pltpu.roll(values, shift, 1) if shift else values
-    return jnp.concatenate([main, tail], axis=0)
+        shift = begin - base - SIDE
+        head = rolled(tiles[3 * g], shift)
+        tail = rolled(jnp.concatenate(tiles[3 * g + 1 : 3 * g + 3], axis=0), shift)
+        if g == 0:
+            first, rest = head, tail
+        else:
+            first = jnp.where((lane_of(TILE) - begin) % LANES < PIECE, head, first)
+            rest = jnp.where((lane_of(2 * TILE) - begin) % LANES < PIECE, tail, rest)
+    return jnp.concatenate([main, first, rest], axis=0)
+
+
+def rolled(values, shift):
+    return pltpu.roll(values, shift % LANES, 1) if shift % LANES else values
 
 
 def dense(ref, which, base):
@@ -290,7 +301,8 @@
     return lax.ppermute(values, axes, [(i, n - 1 - i) for i in range(n)])
 
 
-MESSAGE = (CH, MAIN, LANES)
+MESSAGE = (CH, TILE, TILES * LANES)
+EXTRAS = (MAIN, CH, LANES)
 BACK = (CH, 2, KEPT // 2 * LANES)
 BLOCK = (SIDE, SIDE, LANES)
 GATE = (HALF * LANES, LANES)
@@ -299,7 +311,7 @@
 def body(pair, norm_gain, proj_weight, hid_gain, out_weight, gate_weight):
     normed = pltpu.VMEM(GATE, BF16)
     staged = pltpu.VMEM((MAIN * STRIDE, LANES), F32)
-    extra = pltpu.VMEM((HALF, CH, LANES), F32)
+    extra = pltpu.VMEM(EXTRAS, F32)
     mixed32 = pltpu.VMEM((CH * HALF, LANES), F32)
     hidden = pltpu.VMEM((HALF, CH, LANES), BF16)
     block = pltpu.VMEM(BLOCK, BF16)

time: 135 us -> 133 us (0.985)
  blocking collectives: 107 us -> 104 us
where the time goes in v8:
time: 133 us
  blocking collectives  104 us (78%)
  Pallas kernels  14.7 us (11%)
  waiting for transfers between devices  11.2 us (8%)
  starting transfers between devices  2.56 us (2%)
    all_to_all x1, blocking collectives, body(): got = lax.all_to_all(sent, out_axes, 0, 0, tiled=True)  34.9 us
    all_to_all x1, blocking collectives, body(): got = lax.all_to_all(sent, in_axes, 0, 0, tiled=True)  26.2 us
    all_to_all x1, blocking collectives, body(): mixed = lax.all_to_all(sent, out_axes, 0, 0, tiled=True)  21.6 us
    all_to_all x1, blocking collectives, body(): mixed = lax.all_to_all(sent, in_axes, 0, 0, tiled=True)  21.5 us
    ppermute x7, waiting for transfers between devices, swap(): return lax.ppermute(values, axes, [(i, n - 1 - i) for i in range(n)])  11.2 us
    pallas_call x1, Pallas kernels, body(): call(project_kernel, [MESSAGE], 3, [block, gain32, weight, pltpu.Semaphor...  4.02 us
    pallas_call x1, Pallas kernels, body(): call(middle_kernel, [BLOCK, MESSAGE], 7, [normed, mixed32, hidden, staged...  3.28 us
  transfers between devices with their start and end apart: 7, of which 4 were waited for; matrix products, arithmetic and copies ran while one was open for 0% of the time, Pallas kernels for 2%

profile of v8, /device:TPU:2, one launch (start us, length us, event | category | flops | bytes accessed | tf_op | source)
XLA Modules:
  0.0 133.1 jit_solution(849827183777237626)
XLA Ops:
  0.0 4.0 %shard_map.64 = bf16[64,4,1152]{2,1,0:T(4,128)(2,1)} custom-call(bf16[48,48,128]{2,1,0:T(8,128)(2,1)} %pair.1, f32[2,128]{1,0:T(2,128)} %gain.5, bf16[2,128,256]{2,1,0:T(8,128)(2,1)} %weight.1), custom_call_target="tpu_custom_call" | custom-call | tf_op jit(solution)/shard_map/pallas_call | solution.py:323
  4.0 0.0 copy-start
  4.0 0.0 copy-start.2
  4.0 0.0 copy-start.4
  4.1 34.9 %all_to_all.20.got = bf16[64,4,1152]{2,1,0:T(4,128)(2,1)S(1)} all-to-all(bf16[64,4,1152]{2,1,0:T(4,128)(2,1)} %shard_map.64), channel_id=1, replica_groups=mesh['yh'=2,'yl'=2,'zl'=4,'xh'=2,'xl'=2,'zh'=2,'c'=2] {'yh','zl','xh','x..., dimensions={0} | all-to-all | bytes 1179648 | tf_op jit(solution)/shard_map/all_to_all | solution.py:331
  39.0 0.4 shard_map.65.right
  39.4 0.8 collective-permute-start
  40.2 0.4 shard_map.66.left
  40.6 0.1 collective-permute-start.1
  40.7 0.5 collective-permute-start.2
  41.2 1.1 shard_map.67.gate
  42.3 0.0 copy-start.1
  42.3 0.0 copy-start.3
  42.3 0.0 copy-start.5
  42.4 3.9 %collective-permute-done.right_y = bf16[384,384]{1,0:T(8,128)(2,1)S(1)} collective-permute-done((bf16[384,384]{1,0:T(8,128)(2,1)S(1)}, bf16[384,384]{1,0:T(8,128)(2,1)S(1)}, u32[]{:S(2)}, u32[]{:S(2)}) %collective-permute-start) | collective-permute-done | bytes 294944 | tf_op jit(solution)/shard_map/ppermute | solution.py:301
  46.2 0.0 collective-permute-start.3
  46.3 1.6 %collective-permute-done.3.right_yc = bf16[384,384]{1,0:T(8,128)(2,1)S(1)} collective-permute-done((bf16[384,384]{1,0:T(8,128)(2,1)S(1)}, bf16[384,384]{1,0:T(8,128)(2,1)S(1)}, u32[]{:S(2)}, u32[]{:S(2)}) %collective-permute-start.3) | collective-permute-done | bytes 294944 | tf_op jit(solution)/shard_map/ppermute | solution.py:301
  47.8 1.0 shard_map.68
  48.8 21.6 %all_to_all.21.mixed = bf16[64,2,1152]{2,1,0:T(2,128)(2,1)S(1)} all-to-all(bf16[64,2,1152]{2,1,0:T(2,128)(2,1)S(1)} %shard_map.68), channel_id=1, replica_groups=mesh['yh'=2,'yl'=2,'zl'=4,'xh'=2,'xl'=2,'zh'=2,'c'=2] {'yh','zl','xh','x..., dimensions={0} | all-to-all | bytes 589824 | tf_op jit(solution)/shard_map/all_to_all | solution.py:343
  70.5 3.3 %shard_map.69 = (bf16[48,48,128]{2,1,0:T(8,128)(2,1)S(1)}, bf16[64,4,1152]{2,1,0:T(4,128)(2,1)S(1)}) custom-call(bf16[48,48,128]{2,1,0:T(8,128)(2,1)S(1)} %copy-done, f32[3072,128]{1,0:T(8,128)S(1)} %shard_map.67.gate, bf16[64,2,1152]{2,1,0:T(2,128)(2,1)S(1)} %all_to_all.21.mixed, f32[2,128]{1,0:T(2,128)S(1)} %copy-done.4, f32[2,64]{1,0:T(2,128)S(1)} %copy-done.5, ...), custom_call_target="tpu_custom_call" | custom-call | tf_op jit(solution)/shard_map/pallas_call | solution.py:344
  73.7 26.2 %all_to_all.22.got = bf16[64,4,1152]{2,1,0:T(4,128)(2,1)S(1)} all-to-all(bf16[64,4,1152]{2,1,0:T(4,128)(2,1)S(1)} %get-tuple-element.33), channel_id=1, replica_groups=mesh['yh'=2,'yl'=2,'zl'=4,'xh'=2,'xl'=2,'zh'=2,'c'=2] {'yh','yl','zl','x..., dimensions={0} | all-to-all | bytes 1179648 | tf_op jit(solution)/shard_map/all_to_all | solution.py:347
  99.9 0.5 shard_map.70.left
  100.4 1.2 collective-permute-start.4
  101.6 0.0 collective-permute-start.5
  101.6 0.4 shard_map.71.right
  102.0 1.1 shard_map.72.gate
  103.1 4.1 %collective-permute-done.4.left_x = bf16[384,384]{1,0:T(8,128)(2,1)S(1)} collective-permute-done((bf16[384,384]{1,0:T(8,128)(2,1)S(1)}, bf16[384,384]{1,0:T(8,128)(2,1)S(1)}, u32[]{:S(2)}, u32[]{:S(2)}) %collective-permute-start.4) | collective-permute-done | bytes 294944 | tf_op jit(solution)/shard_map/ppermute | solution.py:301
  107.3 0.0 collective-permute-done.5.left_c
  107.3 1.6 %collective-permute-done.6.left_d = bf16[384,384]{1,0:T(8,128)(2,1)S(1)} collective-permute-done((bf16[384,384]{1,0:T(8,128)(2,1)S(1)}, bf16[384,384]{1,0:T(8,128)(2,1)S(1)}, u32[]{:S(2)}, u32[]{:S(2)}) %collective-permute-start.6) | collective-permute-done | bytes 294944 | tf_op jit(solution)/shard_map/ppermute | solution.py:301
  108.8 0.9 shard_map.73
  109.7 21.5 %all_to_all.23.mixed = bf16[64,2,1152]{2,1,0:T(2,128)(2,1)S(1)} all-to-all(bf16[64,2,1152]{2,1,0:T(2,128)(2,1)S(1)} %shard_map.73), channel_id=1, replica_groups=mesh['yh'=2,'yl'=2,'zl'=4,'xh'=2,'xl'=2,'zh'=2,'c'=2] {'yh','yl','zl','x..., dimensions={0} | all-to-all | bytes 589824 | tf_op jit(solution)/shard_map/all_to_all | solution.py:356
  131.2 1.7 %shard_map.74 = bf16[48,48,128]{2,1,0:T(8,128)(2,1)} custom-call(bf16[48,48,128]{2,1,0:T(8,128)(2,1)S(1)} %get-tuple-element.35.pair, f32[3072,128]{1,0:T(8,128)S(1)} %shard_map.72.gate, bf16[64,2,1152]{2,1,0:T(2,128)(2,1)S(1)} %all_to_all.23.mixed, f32[2,64]{1,0:T(2,128)S(1)} %copy-done.5, bf16[2,64,128]{2,1,0:T(8,128)(2,1)S(1)} %copy-done.3), custom_call_target="tpu_custom_call" | custom-call | tf_op jit(solution)/shard_map/pallas_call | solution.py:357
  (9 shorter events, 0.0 us)
Async XLA Ops:
  4.0 37.2 %copy-start = (bf16[48,48,128]{2,1,0:T(8,128)(2,1)S(1)}, bf16[48,48,128]{2,1,0:T(8,128)(2,1)}, u32[]{:S(2)}) copy-start(bf16[48,48,128]{2,1,0:T(8,128)(2,1)} %pair.1) | copy-start | bytes 1769476
  4.0 37.2 %copy-start.2 = (bf16[2,128,128]{2,1,0:T(8,128)(2,1)S(1)}, bf16[2,128,128]{2,1,0:T(8,128)(2,1)}, u32[]{:S(2)}) copy-start(bf16[2,128,128]{2,1,0:T(8,128)(2,1)} %gweight.3) | copy-start | bytes 196612
  4.0 37.2 %copy-start.4 = (f32[2,128]{1,0:T(2,128)S(1)}, f32[2,128]{1,0:T(2,128)}, u32[]{:S(2)}) copy-start(f32[2,128]{1,0:T(2,128)} %gain.5) | copy-start | bytes 3076
  39.4 6.8 %collective-permute-start = (bf16[384,384]{1,0:T(8,128)(2,1)S(1)}, bf16[384,384]{1,0:T(8,128)(2,1)S(1)}, u32[]{:S(2)}, u32[]{:S(2)}) collective-permute-start(bf16[384,384]{1,0:T(8,128)(2,1)S(1)} %shard_map.65.right), channel_id=1, source_target_pairs={{0,64},{64,0},{1,65},{65,1},{2,66},{66,2},{3,67},{67,3},{4,68},{68... | collective-permute-start | bytes 884744 | tf_op jit(solution)/shard_map/ppermute | solution.py:301
  40.6 5.6 %collective-permute-start.1 = (bf16[384,384]{1,0:T(8,128)(2,1)S(1)}, bf16[384,384]{1,0:T(8,128)(2,1)S(1)}, u32[]{:S(2)}, u32[]{:S(2)}) collective-permute-start(bf16[384,384]{1,0:T(8,128)(2,1)S(1)} %shard_map.66.left), channel_id=1, source_target_pairs={{0,1},{1,0},{2,3},{3,2},{4,5},{5,4},{6,7},{7,6},{8,9},{9,8},{10,11... | collective-permute-start | bytes 884744 | tf_op jit(solution)/shard_map/ppermute | solution.py:301
  40.7 5.5 %collective-permute-start.2 = (bf16[384,384]{1,0:T(8,128)(2,1)S(1)}, bf16[384,384]{1,0:T(8,128)(2,1)S(1)}, u32[]{:S(2)}, u32[]{:S(2)}) collective-permute-start(bf16[384,384]{1,0:T(8,128)(2,1)S(1)} %shard_map.65.right), channel_id=1, source_target_pairs={{0,1},{1,0},{2,3},{3,2},{4,5},{5,4},{6,7},{7,6},{8,9},{9,8},{10,11... | collective-permute-start | bytes 884744 | tf_op jit(solution)/shard_map/ppermute | solution.py:301
  42.3 28.1 %copy-start.1 = (bf16[2,128,256]{2,1,0:T(8,128)(2,1)S(1)}, bf16[2,128,256]{2,1,0:T(8,128)(2,1)}, u32[]{:S(2)}) copy-start(bf16[2,128,256]{2,1,0:T(8,128)(2,1)} %weight.1) | copy-start | bytes 393220
  42.3 28.1 %copy-start.3 = (bf16[2,64,128]{2,1,0:T(8,128)(2,1)S(1)}, bf16[2,64,128]{2,1,0:T(8,128)(2,1)}, u32[]{:S(2)}) copy-start(bf16[2,64,128]{2,1,0:T(8,128)(2,1)} %oweight.3) | copy-start | bytes 98308
  42.3 28.1 %copy-start.5 = (f32[2,64]{1,0:T(2,128)S(1)}, f32[2,64]{1,0:T(2,128)}, u32[]{:S(2)}) copy-start(f32[2,64]{1,0:T(2,128)} %hgain.3) | copy-start | bytes 1540
  46.2 1.6 %collective-permute-start.3 = (bf16[384,384]{1,0:T(8,128)(2,1)S(1)}, bf16[384,384]{1,0:T(8,128)(2,1)S(1)}, u32[]{:S(2)}, u32[]{:S(2)}) collective-permute-start(bf16[384,384]{1,0:T(8,128)(2,1)S(1)} %collective-permute-done.right_y), channel_id=1, source_target_pairs={{0,1},{1,0},{2,3},{3,2},{4,5},{5,4},{6,7},{7,6},{8,9},{9,8},{10,11... | collective-permute-start | bytes 884744 | tf_op jit(solution)/shard_map/ppermute | solution.py:301
  100.4 6.8 %collective-permute-start.4 = (bf16[384,384]{1,0:T(8,128)(2,1)S(1)}, bf16[384,384]{1,0:T(8,128)(2,1)S(1)}, u32[]{:S(2)}, u32[]{:S(2)}) collective-permute-start(bf16[384,384]{1,0:T(8,128)(2,1)S(1)} %shard_map.70.left), channel_id=1, source_target_pairs={{0,4},{4,0},{1,5},{5,1},{2,6},{6,2},{3,7},{7,3},{8,12},{12,8},{9,1... | collective-permute-start | bytes 884744 | tf_op jit(solution)/shard_map/ppermute | solution.py:301
  101.6 5.6 %collective-permute-start.5 = (bf16[384,384]{1,0:T(8,128)(2,1)S(1)}, bf16[384,384]{1,0:T(8,128)(2,1)S(1)}, u32[]{:S(2)}, u32[]{:S(2)}) collective-permute-start(bf16[384,384]{1,0:T(8,128)(2,1)S(1)} %shard_map.70.left), channel_id=1, source_target_pairs={{0,1},{1,0},{2,3},{3,2},{4,5},{5,4},{6,7},{7,6},{8,9},{9,8},{10,11... | collective-permute-start | bytes 884744 | tf_op jit(solution)/shard_map/ppermute | solution.py:301
  107.3 1.6 %collective-permute-start.6 = (bf16[384,384]{1,0:T(8,128)(2,1)S(1)}, bf16[384,384]{1,0:T(8,128)(2,1)S(1)}, u32[]{:S(2)}, u32[]{:S(2)}) collective-permute-start(bf16[384,384]{1,0:T(8,128)(2,1)S(1)} %collective-permute-done.4.left_x), channel_id=1, source_target_pairs={{0,1},{1,0},{2,3},{3,2},{4,5},{5,4},{6,7},{7,6},{8,9},{9,8},{10,11... | collective-permute-start | bytes 884744 | tf_op jit(solution)/shard_map/ppermute | solution.py:301

commit v9 on v8

--- a/solution.py
+++ b/solution.py
@@ -30,14 +30,14 @@
 HBM = pl.BlockSpec(memory_space=pltpu.HBM)
 
 
-def call(kernel, outs, n_in, scratch=(), smem=0, inputs=VMEM, outputs=VMEM, dtype=BF16, limit=16 << 20):
+def call(kernel, outs, n_in, scratch=(), smem=0, inputs=VMEM, outputs=VMEM, dtype=BF16, pin=False):
     return pl.pallas_call(
         kernel,
-        out_shape=[jax.ShapeDtypeStruct(shape, dtype) for shape in outs],
+        out_shape=[(pltpu.VMEM if pin else jax.ShapeDtypeStruct)(shape, dtype) for shape in outs],
         in_specs=[inputs] * n_in + [SMEM] * smem,
         out_specs=[outputs] * len(outs),
         scratch_shapes=scratch,
-        compiler_params=pltpu.CompilerParams(vmem_limit_bytes=limit),
+        compiler_params=pltpu.CompilerParams(vmem_limit_bytes=16 << 20),
     )
 
 
@@ -258,12 +258,24 @@
     return jnp.concatenate(pieces, axis=0)
 
 
-def mix_out_kernel(left, left_c, right, right_c, right_y, right_yc, me, out):
-    for step, (near, far) in enumerate(((right, right_c), (right_y, right_yc))):
-        total = lax.dot_general(left[...], padded(near, 0), NT, preferred_element_type=F32)
-        total += lax.dot_general(left_c[...], padded(far, 192), NT, preferred_element_type=F32)
-        owner = me[0] if step == 0 else 1 - me[0]
-        send_back(total, 8, lambda a, b: a * 8 + (2 * (b // 2) + owner) * 2 + b % 2, out)
+def out_sums(left, left_c, near, far, place, out):
+    total = lax.dot_general(left[...], padded(near, 0), NT, preferred_element_type=F32)
+    total += lax.dot_general(left_c[...], padded(far, 192), NT, preferred_element_type=F32)
+    send_back(total, 8, place, out)
+
+
+def out_early_kernel(left, left_c, right, right_c, out):
+    out_sums(left, left_c, right, right_c, lambda a, b: a * 4 + b, out)
+
+
+def out_late_kernel(left, left_c, right_y, right_yc, early, me, out):
+    def place(owner):
+        return lambda a, b: a * 8 + (2 * (b // 2) + owner) * 2 + b % 2
+
+    for a in range(8):
+        for b in range(4):
+            out[place(me[0])(a, b)] = early[a * 4 + b]
+    out_sums(left, left_c, right_y, right_yc, place(1 - me[0]), out)
 
 
 def in_left_kernel(got, out, left):
@@ -282,18 +294,27 @@
             right[r * SIDE : (r + 1) * SIDE, b * SLOT : (b + 2) * SLOT] = tile.astype(BF16)
 
 
-def mix_in_kernel(right, left, left_c, left_x, left_d, me, core, out):
-    for step, ref in enumerate((left, left_c, left_x, left_d)):
-        total = jnp.dot(ref[:192, :], right[:384, :], preferred_element_type=F32)
-        total += jnp.dot(ref[192:, :], right[384:, :], preferred_element_type=F32)
-        c = core[0] if step % 2 == 0 else 1 - core[0]
-        low = me[0] if step < 2 else 1 - me[0]
-        send_back(
-            total,
-            4,
-            lambda a, b: (2 * (a // 2) + low) * 16 + (2 * (a % 2) + c) * 4 + b,
-            out,
-        )
+def in_sums(left, right, place, out):
+    total = jnp.dot(left[:192, :], right[:384, :], preferred_element_type=F32)
+    total += jnp.dot(left[192:, :], right[384:, :], preferred_element_type=F32)
+    send_back(total, 4, place, out)
+
+
+def in_early_kernel(right, left, left_c, left_x, out):
+    for n, ref in enumerate((left, left_c, left_x)):
+        in_sums(ref, right, lambda a, b: n * 16 + a * 4 + b, out)
+
+
+def in_late_kernel(right, left_d, early, me, core, out):
+    def place(low, c):
+        return lambda a, b: (2 * (a // 2) + low) * 16 + (2 * (a % 2) + c) * 4 + b
+
+    places = [(me[0], core[0]), (me[0], 1 - core[0]), (1 - me[0], core[0])]
+    for n, at in enumerate(places):
+        for a in range(4):
+            for b in range(4):
+                out[place(*at)(a, b)] = early[n * 16 + a * 4 + b]
+    in_sums(left_d, right, place(1 - me[0], 1 - core[0]), out)
 
 
 def swap(values, *axes):
@@ -326,8 +347,8 @@
         3,
         [block, gain32, weight, pltpu.SemaphoreType.DMA((SIDE // GROUP + 2,)), normed, staged, extra],
         inputs=HBM,
-        limit=55 << 20,
-    )(pair, norm_gain, proj_weight)
+        pin=True,
+    )(*(pltpu.with_memory_space_constraint(x, pltpu.HBM) for x in (pair, norm_gain, proj_weight)))
     got = lax.all_to_all(sent, out_axes, 0, 0, tiled=True)
     (right,) = call(out_right_kernel, [(384, 384)], 1, smem=1)(got, core)
     right_y, right_c = swap(right, "yl"), swap(right, "c")
@@ -336,9 +357,10 @@
     left_c = swap(left, "c")
     source, left = tie((pair, left))
     (gate,) = call(functools.partial(gate_kernel, 0), [GATE], 3, [normed], dtype=F32)(source, norm_gain, gate_weight)
-    right_y, gate = tie((right_y, gate))
-    (sent,) = call(mix_out_kernel, [BACK], 6, smem=1)(
-        left, left_c, right, right_c, right_y, swap(right_y, "c"), low_y
+    right_y, gate, left = tie((right_y, gate, left))
+    (early,) = call(out_early_kernel, [(32, *BACK[1:])], 4)(left, left_c, right, right_c)
+    (sent,) = call(out_late_kernel, [BACK], 5, smem=1)(
+        left, left_c, right_y, swap(right_y, "c"), early, low_y
     )
     mixed = lax.all_to_all(sent, out_axes, 0, 0, tiled=True)
     first, sent = call(middle_kernel, [BLOCK, MESSAGE], 7, [normed, mixed32, hidden, staged, extra])(
@@ -351,8 +373,9 @@
     (right,) = call(in_right_kernel, [(768, 256)], 1)(got)
     source, right = tie((first, right))
     (gate,) = call(functools.partial(gate_kernel, 1), [GATE], 3, [normed], dtype=F32)(source, norm_gain, gate_weight)
-    left_x, gate = tie((left_x, gate))
-    (sent,) = call(mix_in_kernel, [BACK], 5, smem=2)(right, left, left_c, left_x, swap(left_x, "c"), low_x, core)
+    left_x, gate, right = tie((left_x, gate, right))
+    (early,) = call(in_early_kernel, [(48, *BACK[1:])], 4)(right, left, left_c, left_x)
+    (sent,) = call(in_late_kernel, [BACK], 3, smem=2)(right, swap(left_x, "c"), early, low_x, core)
     mixed = lax.all_to_all(sent, in_axes, 0, 0, tiled=True)
     (updated,) = call(
         last_kernel,

time: 133 us -> 132 us (level)
  waiting for transfers between devices: 11.2 us -> 9.87 us
  transfers between devices with their start and end apart: 7 -> 7, of which waited for: 4 -> 4; matrix products, arithmetic and copies ran while one was open for 0% -> 0% of each run, Pallas kernels for 2% -> 3%
where the time goes in v9:
time: 132 us; the launch traced here: 131 us
  blocking collectives  104 us (79%)
  Pallas kernels  14.3 us (11%)
  waiting for transfers between devices  9.87 us (7%)
  starting transfers between devices  2.58 us (2%)
    all_to_all x1, blocking collectives, body(): got = lax.all_to_all(sent, out_axes, 0, 0, tiled=True)  34.7 us
    all_to_all x1, blocking collectives, body(): got = lax.all_to_all(sent, in_axes, 0, 0, tiled=True)  26.4 us
    all_to_all x1, blocking collectives, body(): mixed = lax.all_to_all(sent, out_axes, 0, 0, tiled=True)  21.6 us
    all_to_all x1, blocking collectives, body(): mixed = lax.all_to_all(sent, in_axes, 0, 0, tiled=True)  21.6 us
    ppermute x7, waiting for transfers between devices, swap(): return lax.ppermute(values, axes, [(i, n - 1 - i) for i in range(n)])  9.87 us
    pallas_call x1, Pallas kernels, body(): call(middle_kernel, [BLOCK, MESSAGE], 7, [normed, mixed32, hidden, staged...  3.29 us
    pallas_call x1, Pallas kernels, body(): call(project_kernel, [MESSAGE], 3, [block, gain32, weight, pltpu.Semaphor...  3.21 us
  transfers between devices with their start and end apart: 7, of which 4 were waited for; matrix products, arithmetic and copies ran while one was open for 0% of the time, Pallas kernels for 3%

profile of v9, /device:TPU:2, one launch (start us, length us, event | category | flops | bytes accessed | tf_op | source)
XLA Modules:
  0.0 131.4 jit_solution(17704241732901624848)
XLA Ops:
  0.0 3.2 %shard_map.64 = bf16[64,4,1152]{2,1,0:T(4,128)(2,1)S(1)} custom-call(bf16[48,48,128]{2,1,0:T(8,128)(2,1)} %pair.1, f32[2,128]{1,0:T(2,128)} %gain.5, bf16[2,128,256]{2,1,0:T(8,128)(2,1)} %weight.1), custom_call_target="tpu_custom_call" | custom-call | tf_op jit(solution)/shard_map/pallas_call | solution.py:344
  3.2 0.0 copy-start
  3.2 0.0 copy-start.2
  3.2 0.0 copy-start.4
  3.2 34.7 %all_to_all.20.got = bf16[64,4,1152]{2,1,0:T(4,128)(2,1)S(1)} all-to-all(bf16[64,4,1152]{2,1,0:T(4,128)(2,1)S(1)} %shard_map.64), channel_id=1, replica_groups=mesh['yh'=2,'yl'=2,'zl'=4,'xh'=2,'xl'=2,'zh'=2,'c'=2] {'yh','zl','xh','x..., dimensions={0} | all-to-all | bytes 1179648 | tf_op jit(solution)/shard_map/all_to_all | solution.py:352
  38.0 0.4 shard_map.65.right
  38.4 0.8 collective-permute-start
  39.2 0.4 shard_map.66.left
  39.6 0.1 collective-permute-start.1
  39.7 0.5 collective-permute-start.3
  40.2 1.1 shard_map.67.gate
  41.3 0.0 copy-start.1
  41.3 0.0 copy-start.3
  41.3 0.0 copy-start.5
  41.3 3.9 %collective-permute-done.right_y = bf16[384,384]{1,0:T(8,128)(2,1)S(1)} collective-permute-done((bf16[384,384]{1,0:T(8,128)(2,1)S(1)}, bf16[384,384]{1,0:T(8,128)(2,1)S(1)}, u32[]{:S(2)}, u32[]{:S(2)}) %collective-permute-start) | collective-permute-done | bytes 294944 | tf_op jit(solution)/shard_map/ppermute | solution.py:322
  45.2 0.0 collective-permute-start.2
  45.2 0.6 shard_map.68.early
  45.8 1.0 collective-permute-done.2.right_yc
  46.8 0.6 shard_map.69
  47.4 21.6 %all_to_all.21.mixed = bf16[64,2,1152]{2,1,0:T(2,128)(2,1)S(1)} all-to-all(bf16[64,2,1152]{2,1,0:T(2,128)(2,1)S(1)} %shard_map.69), channel_id=1, replica_groups=mesh['yh'=2,'yl'=2,'zl'=4,'xh'=2,'xl'=2,'zh'=2,'c'=2] {'yh','zl','xh','x..., dimensions={0} | all-to-all | bytes 589824 | tf_op jit(solution)/shard_map/all_to_all | solution.py:365
  69.0 3.3 %shard_map.70 = (bf16[48,48,128]{2,1,0:T(8,128)(2,1)S(1)}, bf16[64,4,1152]{2,1,0:T(4,128)(2,1)S(1)}) custom-call(bf16[48,48,128]{2,1,0:T(8,128)(2,1)S(1)} %copy-done, f32[3072,128]{1,0:T(8,128)S(1)} %shard_map.67.gate, bf16[64,2,1152]{2,1,0:T(2,128)(2,1)S(1)} %all_to_all.21.mixed, f32[2,128]{1,0:T(2,128)S(1)} %copy-done.4, f32[2,64]{1,0:T(2,128)S(1)} %copy-done.5, ...), custom_call_target="tpu_custom_call" | custom-call | tf_op jit(solution)/shard_map/pallas_call | solution.py:366
  72.3 26.4 %all_to_all.22.got = bf16[64,4,1152]{2,1,0:T(4,128)(2,1)S(1)} all-to-all(bf16[64,4,1152]{2,1,0:T(4,128)(2,1)S(1)} %get-tuple-element.36), channel_id=1, replica_groups=mesh['yh'=2,'yl'=2,'zl'=4,'xh'=2,'xl'=2,'zh'=2,'c'=2] {'yh','yl','zl','x..., dimensions={0} | all-to-all | bytes 1179648 | tf_op jit(solution)/shard_map/all_to_all | solution.py:369
  98.7 0.5 shard_map.71.left
  99.2 1.2 collective-permute-start.4
  100.4 0.4 shard_map.72.right
  100.8 1.1 shard_map.73.gate
  101.9 4.1 %collective-permute-done.4.left_x = bf16[384,384]{1,0:T(8,128)(2,1)S(1)} collective-permute-done((bf16[384,384]{1,0:T(8,128)(2,1)S(1)}, bf16[384,384]{1,0:T(8,128)(2,1)S(1)}, u32[]{:S(2)}, u32[]{:S(2)}) %collective-permute-start.4) | collective-permute-done | bytes 294944 | tf_op jit(solution)/shard_map/ppermute | solution.py:322
  106.0 0.7 shard_map.74.early
  106.7 0.9 collective-permute-done.5.left_d
  107.6 0.5 shard_map.75
  108.1 21.6 %all_to_all.23.mixed = bf16[64,2,1152]{2,1,0:T(2,128)(2,1)S(1)} all-to-all(bf16[64,2,1152]{2,1,0:T(2,128)(2,1)S(1)} %shard_map.75), channel_id=1, replica_groups=mesh['yh'=2,'yl'=2,'zl'=4,'xh'=2,'xl'=2,'zh'=2,'c'=2] {'yh','yl','zl','x..., dimensions={0} | all-to-all | bytes 589824 | tf_op jit(solution)/shard_map/all_to_all | solution.py:379
  129.6 1.7 %shard_map.76 = bf16[48,48,128]{2,1,0:T(8,128)(2,1)} custom-call(bf16[48,48,128]{2,1,0:T(8,128)(2,1)S(1)} %get-tuple-element.38.pair, f32[3072,128]{1,0:T(8,128)S(1)} %shard_map.73.gate, bf16[64,2,1152]{2,1,0:T(2,128)(2,1)S(1)} %all_to_all.23.mixed, f32[2,64]{1,0:T(2,128)S(1)} %copy-done.5, bf16[2,64,128]{2,1,0:T(8,128)(2,1)S(1)} %copy-done.3), custom_call_target="tpu_custom_call" | custom-call | tf_op jit(solution)/shard_map/pallas_call | solution.py:380
  (11 shorter events, 0.0 us)
Async XLA Ops:
  3.2 37.0 %copy-start = (bf16[48,48,128]{2,1,0:T(8,128)(2,1)S(1)}, bf16[48,48,128]{2,1,0:T(8,128)(2,1)}, u32[]{:S(2)}) copy-start(bf16[48,48,128]{2,1,0:T(8,128)(2,1)} %pair.1) | copy-start | bytes 1769476
  3.2 37.0 %copy-start.2 = (bf16[2,128,128]{2,1,0:T(8,128)(2,1)S(1)}, bf16[2,128,128]{2,1,0:T(8,128)(2,1)}, u32[]{:S(2)}) copy-start(bf16[2,128,128]{2,1,0:T(8,128)(2,1)} %gweight.3) | copy-start | bytes 196612
  3.2 37.0 %copy-start.4 = (f32[2,128]{1,0:T(2,128)S(1)}, f32[2,128]{1,0:T(2,128)}, u32[]{:S(2)}) copy-start(f32[2,128]{1,0:T(2,128)} %gain.5) | copy-start | bytes 3076
  38.4 6.8 %collective-permute-start = (bf16[384,384]{1,0:T(8,128)(2,1)S(1)}, bf16[384,384]{1,0:T(8,128)(2,1)S(1)}, u32[]{:S(2)}, u32[]{:S(2)}) collective-permute-start(bf16[384,384]{1,0:T(8,128)(2,1)S(1)} %shard_map.65.right), channel_id=1, source_target_pairs={{0,64},{64,0},{1,65},{65,1},{2,66},{66,2},{3,67},{67,3},{4,68},{68... | collective-permute-start | bytes 884744 | tf_op jit(solution)/shard_map/ppermute | solution.py:322
  39.6 5.6 %collective-permute-start.1 = (bf16[384,384]{1,0:T(8,128)(2,1)S(1)}, bf16[384,384]{1,0:T(8,128)(2,1)S(1)}, u32[]{:S(2)}, u32[]{:S(2)}) collective-permute-start(bf16[384,384]{1,0:T(8,128)(2,1)S(1)} %shard_map.66.left), channel_id=1, source_target_pairs={{0,1},{1,0},{2,3},{3,2},{4,5},{5,4},{6,7},{7,6},{8,9},{9,8},{10,11... | collective-permute-start | bytes 884744 | tf_op jit(solution)/shard_map/ppermute | solution.py:322
  39.7 5.5 %collective-permute-start.3 = (bf16[384,384]{1,0:T(8,128)(2,1)S(1)}, bf16[384,384]{1,0:T(8,128)(2,1)S(1)}, u32[]{:S(2)}, u32[]{:S(2)}) collective-permute-start(bf16[384,384]{1,0:T(8,128)(2,1)S(1)} %shard_map.65.right), channel_id=1, source_target_pairs={{0,1},{1,0},{2,3},{3,2},{4,5},{5,4},{6,7},{7,6},{8,9},{9,8},{10,11... | collective-permute-start | bytes 884744 | tf_op jit(solution)/shard_map/ppermute | solution.py:322
  41.3 27.7 %copy-start.1 = (bf16[2,128,256]{2,1,0:T(8,128)(2,1)S(1)}, bf16[2,128,256]{2,1,0:T(8,128)(2,1)}, u32[]{:S(2)}) copy-start(bf16[2,128,256]{2,1,0:T(8,128)(2,1)} %weight.1) | copy-start | bytes 393220
  41.3 27.7 %copy-start.3 = (bf16[2,64,128]{2,1,0:T(8,128)(2,1)S(1)}, bf16[2,64,128]{2,1,0:T(8,128)(2,1)}, u32[]{:S(2)}) copy-start(bf16[2,64,128]{2,1,0:T(8,128)(2,1)} %oweight.3) | copy-start | bytes 98308
  41.3 27.7 %copy-start.5 = (f32[2,64]{1,0:T(2,128)S(1)}, f32[2,64]{1,0:T(2,128)}, u32[]{:S(2)}) copy-start(f32[2,64]{1,0:T(2,128)} %hgain.3) | copy-start | bytes 1540
  45.2 1.6 %collective-permute-start.2 = (bf16[384,384]{1,0:T(8,128)(2,1)S(1)}, bf16[384,384]{1,0:T(8,128)(2,1)S(1)}, u32[]{:S(2)}, u32[]{:S(2)}) collective-permute-start(bf16[384,384]{1,0:T(8,128)(2,1)S(1)} %collective-permute-done.right_y), channel_id=1, source_target_pairs={{0,1},{1,0},{2,3},{3,2},{4,5},{5,4},{6,7},{7,6},{8,9},{9,8},{10,11... | collective-permute-start | bytes 884744 | tf_op jit(solution)/shard_map/ppermute | solution.py:322
  99.2 6.8 %collective-permute-start.4 = (bf16[384,384]{1,0:T(8,128)(2,1)S(1)}, bf16[384,384]{1,0:T(8,128)(2,1)S(1)}, u32[]{:S(2)}, u32[]{:S(2)}) collective-permute-start(bf16[384,384]{1,0:T(8,128)(2,1)S(1)} %shard_map.71.left), channel_id=1, source_target_pairs={{0,4},{4,0},{1,5},{5,1},{2,6},{6,2},{3,7},{7,3},{8,12},{12,8},{9,1... | collective-permute-start | bytes 884744 | tf_op jit(solution)/shard_map/ppermute | solution.py:322
  100.4 5.6 %collective-permute-start.6 = (bf16[384,384]{1,0:T(8,128)(2,1)S(1)}, bf16[384,384]{1,0:T(8,128)(2,1)S(1)}, u32[]{:S(2)}, u32[]{:S(2)}) collective-permute-start(bf16[384,384]{1,0:T(8,128)(2,1)S(1)} %shard_map.71.left), channel_id=1, source_target_pairs={{0,1},{1,0},{2,3},{3,2},{4,5},{5,4},{6,7},{7,6},{8,9},{9,8},{10,11... | collective-permute-start | bytes 884744 | tf_op jit(solution)/shard_map/ppermute | solution.py:322
  106.0 1.6 %collective-permute-start.5 = (bf16[384,384]{1,0:T(8,128)(2,1)S(1)}, bf16[384,384]{1,0:T(8,128)(2,1)S(1)}, u32[]{:S(2)}, u32[]{:S(2)}) collective-permute-start(bf16[384,384]{1,0:T(8,128)(2,1)S(1)} %collective-permute-done.4.left_x), channel_id=1, source_target_pairs={{0,1},{1,0},{2,3},{3,2},{4,5},{5,4},{6,7},{7,6},{8,9},{9,8},{10,11... | collective-permute-start | bytes 884744 | tf_op jit(solution)/shard_map/ppermute | solution.py:322

commit v10 on v9

--- a/solution.py
+++ b/solution.py
@@ -17,7 +17,6 @@
 TILES = MAIN // TILE
 EXTRA = SIDE - MAIN
 STRIDE = 72
-GROUP = 16
 KEPT = 18
 PIECE = 16
 CH = 64
@@ -56,16 +55,17 @@
     return 0.5 * jnp.tanh(0.5 * values) + 0.5
 
 
-def normalize(block, gain, normed, arrive=lambda start: None):
+def normalize(block, gain, normed):
     pad = jnp.zeros((SLOT - SIDE, LANES), BF16)
-    for start in range(0, SIDE, GROUP):
-        arrive(start)
-        rows = layer_norm(block[start : start + GROUP].astype(F32), gain.reshape(1, 1, LANES), 2)
-        rows = rows.astype(BF16)
-        for i in range(GROUP):
-            base = place_of(start + i)
-            normed[base : base + SIDE, :] = rows[i]
-            normed[base + SIDE : base + SLOT, :] = pad
+    share = jnp.full((LANES, LANES), 1 / LANES, BF16)
+    tokens = block[...].reshape(SIDE * SIDE, LANES)
+    centred = tokens.astype(F32) - jnp.dot(tokens, share, preferred_element_type=F32)
+    var = jnp.mean(centred * centred, axis=1, keepdims=True)
+    rows = (centred * lax.rsqrt(var + EPS) * gain).astype(BF16)
+    for i in range(SIDE):
+        base = place_of(i)
+        normed[base : base + SIDE, :] = rows[i * SIDE : (i + 1) * SIDE]
+        normed[base + SIDE : base + SLOT, :] = pad
 
 
 def place_of(i):
@@ -100,17 +100,13 @@
 
 
 def project_kernel(pair_hbm, gain_hbm, weight_hbm, out, pair, gain, weight, sems, normed, staged, extra):
-    groups = SIDE // GROUP
-    copies = [pltpu.make_async_copy(gain_hbm, gain, sems.at[groups])]
-    for n in range(groups):
-        rows = pl.ds(n * GROUP, GROUP)
-        copies.append(pltpu.make_async_copy(pair_hbm.at[rows], pair.at[rows], sems.at[n]))
-    copies.append(pltpu.make_async_copy(weight_hbm.at[0], weight, sems.at[groups + 1]))
+    places = ((gain_hbm, gain), (pair_hbm, pair), (weight_hbm.at[0], weight))
+    copies = [pltpu.make_async_copy(source, target, sems.at[n]) for n, (source, target) in enumerate(places)]
     for copy in copies:
         copy.start()
-    copies[0].wait()
-    normalize(pair, gain[0:1, :], normed, lambda start: copies[1 + start // GROUP].wait())
-    copies[-1].wait()
+    for copy in copies:
+        copy.wait()
+    normalize(pair, gain[0:1, :], normed)
     project(normed, weight[...], staged, extra)
     write_messages(staged, out)
 
@@ -140,7 +136,7 @@
     return sums
 
 
-def finish(pair, gate, mixed, hgain, oweight, z_out, mixed32, hidden, ready=lambda s: None):
+def finish(pair, gate, mixed, hgain, oweight, z_out, mixed32, hidden):
     hcol = hgain.T
     read_sums(mixed, mixed32)
     for s in range(0, HALF, 4):
@@ -160,7 +156,6 @@
             ]
             for t in range(4):
                 z_out[s + t + h * HALF] = new[t].astype(BF16)
-            ready(s + h * HALF)
 
 
 def middle_kernel(
@@ -172,17 +167,11 @@
     write_messages(staged, out)
 
 
-def last_kernel(pair, gate, mixed, hgain, oweight, z_hbm, z_out, sems, mixed32, hidden):
-    copies = []
-
-    def ready(s):
-        rows = pl.ds(s, 4)
-        copies.append(pltpu.make_async_copy(z_out.at[rows], z_hbm.at[rows], sems.at[s // 4]))
-        copies[-1].start()
-
-    finish(pair, gate, mixed, hgain[1:2, :], oweight[1], z_out, mixed32, hidden, ready)
-    for copy in copies:
-        copy.wait()
+def last_kernel(pair, gate, mixed, hgain, oweight, z_hbm, z_out, sem, mixed32, hidden):
+    finish(pair, gate, mixed, hgain[1:2, :], oweight[1], z_out, mixed32, hidden)
+    copy = pltpu.make_async_copy(z_out, z_hbm, sem)
+    copy.start()
+    copy.wait()
 
 
 def moved(got, p, base, offset):
@@ -345,7 +334,7 @@
         project_kernel,
         [MESSAGE],
         3,
-        [block, gain32, weight, pltpu.SemaphoreType.DMA((SIDE // GROUP + 2,)), normed, staged, extra],
+        [block, gain32, weight, pltpu.SemaphoreType.DMA((3,)), normed, staged, extra],
         inputs=HBM,
         pin=True,
     )(*(pltpu.with_memory_space_constraint(x, pltpu.HBM) for x in (pair, norm_gain, proj_weight)))
@@ -381,7 +370,7 @@
         last_kernel,
         [BLOCK],
         5,
-        [block, pltpu.SemaphoreType.DMA((SIDE // 4,)), mixed32, hidden],
+        [block, pltpu.SemaphoreType.DMA, mixed32, hidden],
         outputs=HBM,
     )(first, gate, mixed, hid_gain, out_weight)
     return updated

time: 132 us -> 130 us (0.985)
  Pallas kernels: 14.3 us -> 12.7 us
where the time goes in v10:
time: 130 us
  blocking collectives  104 us (80%)
  Pallas kernels  12.7 us (10%)
  waiting for transfers between devices  10.2 us (8%)
  starting transfers between devices  2.56 us (2%)
    all_to_all x1, blocking collectives, body(): got = lax.all_to_all(sent, out_axes, 0, 0, tiled=True)  34.7 us
    all_to_all x1, blocking collectives, body(): got = lax.all_to_all(sent, in_axes, 0, 0, tiled=True)  26.2 us
    all_to_all x1, blocking collectives, body(): mixed = lax.all_to_all(sent, out_axes, 0, 0, tiled=True)  21.6 us
    all_to_all x1, blocking collectives, body(): mixed = lax.all_to_all(sent, in_axes, 0, 0, tiled=True)  21.5 us
    ppermute x7, waiting for transfers between devices, swap(): return lax.ppermute(values, axes, [(i, n - 1 - i) for i in range(n)])  10.2 us
    pallas_call x1, Pallas kernels, body(): call(project_kernel, [MESSAGE], 3, [block, gain32, weight, pltpu.Semaphor...  2.74 us
  transfers between devices with their start and end apart: 7, of which 4 were waited for; matrix products, arithmetic and copies ran while one was open for 0% of the time, Pallas kernels for 3%

profile of v10, /device:TPU:2, one launch (start us, length us, event | category | flops | bytes accessed | tf_op | source)
XLA Modules:
  0.0 130.0 jit_solution(17773166535015891109)
XLA Ops:
  0.0 2.7 %shard_map.64 = bf16[64,4,1152]{2,1,0:T(4,128)(2,1)S(1)} custom-call(bf16[48,48,128]{2,1,0:T(8,128)(2,1)} %pair.1, f32[2,128]{1,0:T(2,128)} %gain.5, bf16[2,128,256]{2,1,0:T(8,128)(2,1)} %weight.1), custom_call_target="tpu_custom_call" | custom-call | tf_op jit(solution)/shard_map/pallas_call | solution.py:333
  2.8 0.0 copy-start
  2.8 0.0 copy-start.2
  2.8 0.0 copy-start.4
  2.8 34.7 %all_to_all.20.got = bf16[64,4,1152]{2,1,0:T(4,128)(2,1)S(1)} all-to-all(bf16[64,4,1152]{2,1,0:T(4,128)(2,1)S(1)} %shard_map.64), channel_id=1, replica_groups=mesh['yh'=2,'yl'=2,'zl'=4,'xh'=2,'xl'=2,'zh'=2,'c'=2] {'yh','zl','xh','x..., dimensions={0} | all-to-all | bytes 1179648 | tf_op jit(solution)/shard_map/all_to_all | solution.py:341
  37.5 0.4 shard_map.65.right
  38.0 0.8 collective-permute-start
  38.7 0.4 shard_map.66.left
  39.1 0.1 collective-permute-start.1
  39.2 0.5 collective-permute-start.3
  39.7 0.9 shard_map.67.gate
  40.7 0.0 copy-start.1
  40.7 0.0 copy-start.3
  40.7 0.0 copy-start.5
  40.7 4.1 %collective-permute-done.right_y = bf16[384,384]{1,0:T(8,128)(2,1)S(1)} collective-permute-done((bf16[384,384]{1,0:T(8,128)(2,1)S(1)}, bf16[384,384]{1,0:T(8,128)(2,1)S(1)}, u32[]{:S(2)}, u32[]{:S(2)}) %collective-permute-start) | collective-permute-done | bytes 294944 | tf_op jit(solution)/shard_map/ppermute | solution.py:311
  44.8 0.0 collective-permute-done.3.right_c
  44.8 0.6 shard_map.68.early
  45.4 1.0 collective-permute-done.2.right_yc
  46.3 0.6 shard_map.69
  46.9 21.6 %all_to_all.21.mixed = bf16[64,2,1152]{2,1,0:T(2,128)(2,1)S(1)} all-to-all(bf16[64,2,1152]{2,1,0:T(2,128)(2,1)S(1)} %shard_map.69), channel_id=1, replica_groups=mesh['yh'=2,'yl'=2,'zl'=4,'xh'=2,'xl'=2,'zh'=2,'c'=2] {'yh','zl','xh','x..., dimensions={0} | all-to-all | bytes 589824 | tf_op jit(solution)/shard_map/all_to_all | solution.py:354
  68.6 2.4 %shard_map.70 = (bf16[48,48,128]{2,1,0:T(8,128)(2,1)S(1)}, bf16[64,4,1152]{2,1,0:T(4,128)(2,1)S(1)}) custom-call(bf16[48,48,128]{2,1,0:T(8,128)(2,1)S(1)} %copy-done, f32[3072,128]{1,0:T(8,128)S(1)} %shard_map.67.gate, bf16[64,2,1152]{2,1,0:T(2,128)(2,1)S(1)} %all_to_all.21.mixed, f32[2,128]{1,0:T(2,128)S(1)} %copy-done.4, f32[2,64]{1,0:T(2,128)S(1)} %copy-done.5, ...), custom_call_target="tpu_custom_call" | custom-call | tf_op jit(solution)/shard_map/pallas_call | solution.py:355
  71.0 26.2 %all_to_all.22.got = bf16[64,4,1152]{2,1,0:T(4,128)(2,1)S(1)} all-to-all(bf16[64,4,1152]{2,1,0:T(4,128)(2,1)S(1)} %get-tuple-element.36), channel_id=1, replica_groups=mesh['yh'=2,'yl'=2,'zl'=4,'xh'=2,'xl'=2,'zh'=2,'c'=2] {'yh','yl','zl','x..., dimensions={0} | all-to-all | bytes 1179648 | tf_op jit(solution)/shard_map/all_to_all | solution.py:358
  97.3 0.5 shard_map.71.left
  97.7 1.2 collective-permute-start.4
  99.0 0.4 shard_map.72.right
  99.3 0.9 shard_map.73.gate
  100.3 4.3 %collective-permute-done.4.left_x = bf16[384,384]{1,0:T(8,128)(2,1)S(1)} collective-permute-done((bf16[384,384]{1,0:T(8,128)(2,1)S(1)}, bf16[384,384]{1,0:T(8,128)(2,1)S(1)}, u32[]{:S(2)}, u32[]{:S(2)}) %collective-permute-start.4) | collective-permute-done | bytes 294944 | tf_op jit(solution)/shard_map/ppermute | solution.py:311
  104.6 0.7 shard_map.74.early
  105.3 0.9 collective-permute-done.5.left_d
  106.1 0.5 shard_map.75
  106.6 21.5 %all_to_all.23.mixed = bf16[64,2,1152]{2,1,0:T(2,128)(2,1)S(1)} all-to-all(bf16[64,2,1152]{2,1,0:T(2,128)(2,1)S(1)} %shard_map.75), channel_id=1, replica_groups=mesh['yh'=2,'yl'=2,'zl'=4,'xh'=2,'xl'=2,'zh'=2,'c'=2] {'yh','yl','zl','x..., dimensions={0} | all-to-all | bytes 589824 | tf_op jit(solution)/shard_map/all_to_all | solution.py:368
  128.1 1.7 %shard_map.76 = bf16[48,48,128]{2,1,0:T(8,128)(2,1)} custom-call(bf16[48,48,128]{2,1,0:T(8,128)(2,1)S(1)} %get-tuple-element.38.pair, f32[3072,128]{1,0:T(8,128)S(1)} %shard_map.73.gate, bf16[64,2,1152]{2,1,0:T(2,128)(2,1)S(1)} %all_to_all.23.mixed, f32[2,64]{1,0:T(2,128)S(1)} %copy-done.5, bf16[2,64,128]{2,1,0:T(8,128)(2,1)S(1)} %copy-done.3), custom_call_target="tpu_custom_call" | custom-call | tf_op jit(solution)/shard_map/pallas_call | solution.py:369
  (11 shorter events, 0.0 us)
Async XLA Ops:
  2.8 37.0 %copy-start = (bf16[48,48,128]{2,1,0:T(8,128)(2,1)S(1)}, bf16[48,48,128]{2,1,0:T(8,128)(2,1)}, u32[]{:S(2)}) copy-start(bf16[48,48,128]{2,1,0:T(8,128)(2,1)} %pair.1) | copy-start | bytes 1769476
  2.8 37.0 %copy-start.2 = (bf16[2,128,128]{2,1,0:T(8,128)(2,1)S(1)}, bf16[2,128,128]{2,1,0:T(8,128)(2,1)}, u32[]{:S(2)}) copy-start(bf16[2,128,128]{2,1,0:T(8,128)(2,1)} %gweight.3) | copy-start | bytes 196612
  2.8 37.0 %copy-start.4 = (f32[2,128]{1,0:T(2,128)S(1)}, f32[2,128]{1,0:T(2,128)}, u32[]{:S(2)}) copy-start(f32[2,128]{1,0:T(2,128)} %gain.5) | copy-start | bytes 3076
  38.0 6.8 %collective-permute-start = (bf16[384,384]{1,0:T(8,128)(2,1)S(1)}, bf16[384,384]{1,0:T(8,128)(2,1)S(1)}, u32[]{:S(2)}, u32[]{:S(2)}) collective-permute-start(bf16[384,384]{1,0:T(8,128)(2,1)S(1)} %shard_map.65.right), channel_id=1, source_target_pairs={{0,64},{64,0},{1,65},{65,1},{2,66},{66,2},{3,67},{67,3},{4,68},{68... | collective-permute-start | bytes 884744 | tf_op jit(solution)/shard_map/ppermute | solution.py:311
  39.1 5.6 %collective-permute-start.1 = (bf16[384,384]{1,0:T(8,128)(2,1)S(1)}, bf16[384,384]{1,0:T(8,128)(2,1)S(1)}, u32[]{:S(2)}, u32[]{:S(2)}) collective-permute-start(bf16[384,384]{1,0:T(8,128)(2,1)S(1)} %shard_map.66.left), channel_id=1, source_target_pairs={{0,1},{1,0},{2,3},{3,2},{4,5},{5,4},{6,7},{7,6},{8,9},{9,8},{10,11... | collective-permute-start | bytes 884744 | tf_op jit(solution)/shard_map/ppermute | solution.py:311
  39.2 5.5 %collective-permute-start.3 = (bf16[384,384]{1,0:T(8,128)(2,1)S(1)}, bf16[384,384]{1,0:T(8,128)(2,1)S(1)}, u32[]{:S(2)}, u32[]{:S(2)}) collective-permute-start(bf16[384,384]{1,0:T(8,128)(2,1)S(1)} %shard_map.65.right), channel_id=1, source_target_pairs={{0,1},{1,0},{2,3},{3,2},{4,5},{5,4},{6,7},{7,6},{8,9},{9,8},{10,11... | collective-permute-start | bytes 884744 | tf_op jit(solution)/shard_map/ppermute | solution.py:311
  40.7 27.9 %copy-start.1 = (bf16[2,128,256]{2,1,0:T(8,128)(2,1)S(1)}, bf16[2,128,256]{2,1,0:T(8,128)(2,1)}, u32[]{:S(2)}) copy-start(bf16[2,128,256]{2,1,0:T(8,128)(2,1)} %weight.1) | copy-start | bytes 393220
  40.7 27.9 %copy-start.3 = (bf16[2,64,128]{2,1,0:T(8,128)(2,1)S(1)}, bf16[2,64,128]{2,1,0:T(8,128)(2,1)}, u32[]{:S(2)}) copy-start(bf16[2,64,128]{2,1,0:T(8,128)(2,1)} %oweight.3) | copy-start | bytes 98308
  40.7 27.9 %copy-start.5 = (f32[2,64]{1,0:T(2,128)S(1)}, f32[2,64]{1,0:T(2,128)}, u32[]{:S(2)}) copy-start(f32[2,64]{1,0:T(2,128)} %hgain.3) | copy-start | bytes 1540
  44.8 1.6 %collective-permute-start.2 = (bf16[384,384]{1,0:T(8,128)(2,1)S(1)}, bf16[384,384]{1,0:T(8,128)(2,1)S(1)}, u32[]{:S(2)}, u32[]{:S(2)}) collective-permute-start(bf16[384,384]{1,0:T(8,128)(2,1)S(1)} %collective-permute-done.right_y), channel_id=1, source_target_pairs={{0,1},{1,0},{2,3},{3,2},{4,5},{5,4},{6,7},{7,6},{8,9},{9,8},{10,11... | collective-permute-start | bytes 884744 | tf_op jit(solution)/shard_map/ppermute | solution.py:311
  97.7 6.8 %collective-permute-start.4 = (bf16[384,384]{1,0:T(8,128)(2,1)S(1)}, bf16[384,384]{1,0:T(8,128)(2,1)S(1)}, u32[]{:S(2)}, u32[]{:S(2)}) collective-permute-start(bf16[384,384]{1,0:T(8,128)(2,1)S(1)} %shard_map.71.left), channel_id=1, source_target_pairs={{0,4},{4,0},{1,5},{5,1},{2,6},{6,2},{3,7},{7,3},{8,12},{12,8},{9,1... | collective-permute-start | bytes 884744 | tf_op jit(solution)/shard_map/ppermute | solution.py:311
  99.0 5.6 %collective-permute-start.6 = (bf16[384,384]{1,0:T(8,128)(2,1)S(1)}, bf16[384,384]{1,0:T(8,128)(2,1)S(1)}, u32[]{:S(2)}, u32[]{:S(2)}) collective-permute-start(bf16[384,384]{1,0:T(8,128)(2,1)S(1)} %shard_map.71.left), channel_id=1, source_target_pairs={{0,1},{1,0},{2,3},{3,2},{4,5},{5,4},{6,7},{7,6},{8,9},{9,8},{10,11... | collective-permute-start | bytes 884744 | tf_op jit(solution)/shard_map/ppermute | solution.py:311
  104.6 1.6 %collective-permute-start.5 = (bf16[384,384]{1,0:T(8,128)(2,1)S(1)}, bf16[384,384]{1,0:T(8,128)(2,1)S(1)}, u32[]{:S(2)}, u32[]{:S(2)}) collective-permute-start(bf16[384,384]{1,0:T(8,128)(2,1)S(1)} %collective-permute-done.4.left_x), channel_id=1, source_target_pairs={{0,1},{1,0},{2,3},{3,2},{4,5},{5,4},{6,7},{7,6},{8,9},{9,8},{10,11... | collective-permute-start | bytes 884744 | tf_op jit(solution)/shard_map/ppermute | solution.py:311

commit v11 on v10

--- a/solution.py
+++ b/solution.py
@@ -136,7 +136,7 @@
     return sums
 
 
-def finish(pair, gate, mixed, hgain, oweight, z_out, mixed32, hidden):
+def finish(pair, gate, mixed, hgain, oweight, z_out, mixed32, hidden, ready=lambda s: None):
     hcol = hgain.T
     read_sums(mixed, mixed32)
     for s in range(0, HALF, 4):
@@ -156,6 +156,7 @@
             ]
             for t in range(4):
                 z_out[s + t + h * HALF] = new[t].astype(BF16)
+        ready(s + 4)
 
 
 def middle_kernel(
@@ -167,11 +168,18 @@
     write_messages(staged, out)
 
 
-def last_kernel(pair, gate, mixed, hgain, oweight, z_hbm, z_out, sem, mixed32, hidden):
-    finish(pair, gate, mixed, hgain[1:2, :], oweight[1], z_out, mixed32, hidden)
-    copy = pltpu.make_async_copy(z_out, z_hbm, sem)
-    copy.start()
-    copy.wait()
+def last_kernel(pair, gate, mixed, hgain, oweight, z_hbm, z_out, sems, mixed32, hidden):
+    copies = []
+
+    def ready(s):
+        for start in (s - HALF // 2, s + HALF // 2) if s % (HALF // 2) == 0 else ():
+            rows = pl.ds(start, HALF // 2)
+            copies.append(pltpu.make_async_copy(z_out.at[rows], z_hbm.at[rows], sems.at[len(copies)]))
+            copies[-1].start()
+
+    finish(pair, gate, mixed, hgain[1:2, :], oweight[1], z_out, mixed32, hidden, ready)
+    for copy in copies:
+        copy.wait()
 
 
 def moved(got, p, base, offset):
@@ -234,9 +242,9 @@
     last = rows[16:]
     spare = [pltpu.roll(last, SIDE - g * PIECE, 1)[KEPT - 16 :] for g in range(SIDE // PIECE)]
     lane = lane_of(KEPT) % SLOT
-    rows = jnp.where(lane < SIDE, rows[:KEPT], jnp.concatenate(spare, axis=0)).astype(BF16)
+    rows = jnp.where(lane < SIDE, rows[:KEPT], jnp.concatenate(spare, axis=0))
     for t in range(KEPT // 2):
-        out[p, :, t * LANES : (t + 1) * LANES] = rows[2 * t : 2 * t + 2]
+        out[p, :, t * LANES : (t + 1) * LANES] = rows[2 * t : 2 * t + 2].astype(BF16)
 
 
 def padded(ref, start):
@@ -320,9 +328,9 @@
 
 def body(pair, norm_gain, proj_weight, hid_gain, out_weight, gate_weight):
     normed = pltpu.VMEM(GATE, BF16)
-    staged = pltpu.VMEM((MAIN * STRIDE, LANES), F32)
+    staged = pltpu.VMEM(((MAIN + 1) * STRIDE, LANES), F32)
     extra = pltpu.VMEM(EXTRAS, F32)
-    mixed32 = pltpu.VMEM((CH * HALF, LANES), F32)
+    mixed32 = pltpu.VMEM(((CH + 1) * HALF, LANES), F32)
     hidden = pltpu.VMEM((HALF, CH, LANES), BF16)
     block = pltpu.VMEM(BLOCK, BF16)
     gain32, weight = pltpu.VMEM((2, LANES), F32), pltpu.VMEM((LANES, 4 * CH), BF16)
@@ -370,7 +378,7 @@
         last_kernel,
         [BLOCK],
         5,
-        [block, pltpu.SemaphoreType.DMA, mixed32, hidden],
+        [block, pltpu.SemaphoreType.DMA((4,)), mixed32, hidden],
         outputs=HBM,
     )(first, gate, mixed, hid_gain, out_weight)
     return updated

time: 130 us -> 130 us (level)
  no operation moved by 1% of the time
where the time goes in v11:
time: 130 us
  blocking collectives  104 us (80%)
  Pallas kernels  12.7 us (10%)
  waiting for transfers between devices  10.3 us (8%)
  starting transfers between devices  2.56 us (2%)
    all_to_all x1, blocking collectives, body(): got = lax.all_to_all(sent, out_axes, 0, 0, tiled=True)  34.7 us
    all_to_all x1, blocking collectives, body(): got = lax.all_to_all(sent, in_axes, 0, 0, tiled=True)  26.2 us
    all_to_all x1, blocking collectives, body(): mixed = lax.all_to_all(sent, out_axes, 0, 0, tiled=True)  21.6 us
    all_to_all x1, blocking collectives, body(): mixed = lax.all_to_all(sent, in_axes, 0, 0, tiled=True)  21.5 us
    ppermute x7, waiting for transfers between devices, swap(): return lax.ppermute(values, axes, [(i, n - 1 - i) for i in range(n)])  10.3 us
    pallas_call x1, Pallas kernels, body(): call(project_kernel, [MESSAGE], 3, [block, gain32, weight, pltpu.Semaphor...  2.74 us
  transfers between devices with their start and end apart: 7, of which 4 were waited for; matrix products, arithmetic and copies ran while one was open for 0% of the time, Pallas kernels for 3%

profile of v11, /device:TPU:2, one launch (start us, length us, event | category | flops | bytes accessed | tf_op | source)
XLA Modules:
  0.0 130.0 jit_solution(14119106094187292434)
XLA Ops:
  0.0 2.7 %shard_map.64 = bf16[64,4,1152]{2,1,0:T(4,128)(2,1)S(1)} custom-call(bf16[48,48,128]{2,1,0:T(8,128)(2,1)} %pair.1, f32[2,128]{1,0:T(2,128)} %gain.5, bf16[2,128,256]{2,1,0:T(8,128)(2,1)} %weight.1), custom_call_target="tpu_custom_call" | custom-call | tf_op jit(solution)/shard_map/pallas_call | solution.py:341
  2.8 0.0 copy-start
  2.8 0.0 copy-start.2
  2.8 0.0 copy-start.4
  2.8 34.7 %all_to_all.20.got = bf16[64,4,1152]{2,1,0:T(4,128)(2,1)S(1)} all-to-all(bf16[64,4,1152]{2,1,0:T(4,128)(2,1)S(1)} %shard_map.64), channel_id=1, replica_groups=mesh['yh'=2,'yl'=2,'zl'=4,'xh'=2,'xl'=2,'zh'=2,'c'=2] {'yh','zl','xh','x..., dimensions={0} | all-to-all | bytes 1179648 | tf_op jit(solution)/shard_map/all_to_all | solution.py:349
  37.5 0.4 shard_map.65.right
  38.0 0.8 collective-permute-start
  38.7 0.4 shard_map.66.left
  39.1 0.1 collective-permute-start.1
  39.2 0.5 collective-permute-start.3
  39.7 0.9 shard_map.67.gate
  40.7 0.0 copy-start.1
  40.7 0.0 copy-start.3
  40.7 0.0 copy-start.5
  40.7 4.1 %collective-permute-done.right_y = bf16[384,384]{1,0:T(8,128)(2,1)S(1)} collective-permute-done((bf16[384,384]{1,0:T(8,128)(2,1)S(1)}, bf16[384,384]{1,0:T(8,128)(2,1)S(1)}, u32[]{:S(2)}, u32[]{:S(2)}) %collective-permute-start) | collective-permute-done | bytes 294944 | tf_op jit(solution)/shard_map/ppermute | solution.py:319
  44.8 0.0 collective-permute-start.2
  44.8 0.6 shard_map.68.early
  45.4 1.0 collective-permute-done.2.right_yc
  46.4 0.6 shard_map.69
  46.9 21.6 %all_to_all.21.mixed = bf16[64,2,1152]{2,1,0:T(2,128)(2,1)S(1)} all-to-all(bf16[64,2,1152]{2,1,0:T(2,128)(2,1)S(1)} %shard_map.69), channel_id=1, replica_groups=mesh['yh'=2,'yl'=2,'zl'=4,'xh'=2,'xl'=2,'zh'=2,'c'=2] {'yh','zl','xh','x..., dimensions={0} | all-to-all | bytes 589824 | tf_op jit(solution)/shard_map/all_to_all | solution.py:362
  68.6 2.5 %shard_map.70 = (bf16[48,48,128]{2,1,0:T(8,128)(2,1)S(1)}, bf16[64,4,1152]{2,1,0:T(4,128)(2,1)S(1)}) custom-call(bf16[48,48,128]{2,1,0:T(8,128)(2,1)S(1)} %copy-done, f32[3072,128]{1,0:T(8,128)S(1)} %shard_map.67.gate, bf16[64,2,1152]{2,1,0:T(2,128)(2,1)S(1)} %all_to_all.21.mixed, f32[2,128]{1,0:T(2,128)S(1)} %copy-done.4, f32[2,64]{1,0:T(2,128)S(1)} %copy-done.5, ...), custom_call_target="tpu_custom_call" | custom-call | tf_op jit(solution)/shard_map/pallas_call | solution.py:363
  71.1 26.2 %all_to_all.22.got = bf16[64,4,1152]{2,1,0:T(4,128)(2,1)S(1)} all-to-all(bf16[64,4,1152]{2,1,0:T(4,128)(2,1)S(1)} %get-tuple-element.36), channel_id=1, replica_groups=mesh['yh'=2,'yl'=2,'zl'=4,'xh'=2,'xl'=2,'zh'=2,'c'=2] {'yh','yl','zl','x..., dimensions={0} | all-to-all | bytes 1179648 | tf_op jit(solution)/shard_map/all_to_all | solution.py:366
  97.3 0.5 shard_map.71.left
  97.8 1.2 collective-permute-start.4
  99.0 0.4 shard_map.72.right
  99.3 0.9 shard_map.73.gate
  100.3 4.3 %collective-permute-done.4.left_x = bf16[384,384]{1,0:T(8,128)(2,1)S(1)} collective-permute-done((bf16[384,384]{1,0:T(8,128)(2,1)S(1)}, bf16[384,384]{1,0:T(8,128)(2,1)S(1)}, u32[]{:S(2)}, u32[]{:S(2)}) %collective-permute-start.4) | collective-permute-done | bytes 294944 | tf_op jit(solution)/shard_map/ppermute | solution.py:319
  104.6 0.7 shard_map.74.early
  105.3 0.9 collective-permute-done.5.left_d
  106.1 0.5 shard_map.75
  106.6 21.5 %all_to_all.23.mixed = bf16[64,2,1152]{2,1,0:T(2,128)(2,1)S(1)} all-to-all(bf16[64,2,1152]{2,1,0:T(2,128)(2,1)S(1)} %shard_map.75), channel_id=1, replica_groups=mesh['yh'=2,'yl'=2,'zl'=4,'xh'=2,'xl'=2,'zh'=2,'c'=2] {'yh','yl','zl','x..., dimensions={0} | all-to-all | bytes 589824 | tf_op jit(solution)/shard_map/all_to_all | solution.py:376
  128.1 1.7 %shard_map.76 = bf16[48,48,128]{2,1,0:T(8,128)(2,1)} custom-call(bf16[48,48,128]{2,1,0:T(8,128)(2,1)S(1)} %get-tuple-element.38.pair, f32[3072,128]{1,0:T(8,128)S(1)} %shard_map.73.gate, bf16[64,2,1152]{2,1,0:T(2,128)(2,1)S(1)} %all_to_all.23.mixed, f32[2,64]{1,0:T(2,128)S(1)} %copy-done.5, bf16[2,64,128]{2,1,0:T(8,128)(2,1)S(1)} %copy-done.3), custom_call_target="tpu_custom_call" | custom-call | tf_op jit(solution)/shard_map/pallas_call | solution.py:377
  (11 shorter events, 0.0 us)
Async XLA Ops:
  2.8 37.0 %copy-start = (bf16[48,48,128]{2,1,0:T(8,128)(2,1)S(1)}, bf16[48,48,128]{2,1,0:T(8,128)(2,1)}, u32[]{:S(2)}) copy-start(bf16[48,48,128]{2,1,0:T(8,128)(2,1)} %pair.1) | copy-start | bytes 1769476
  2.8 37.0 %copy-start.2 = (bf16[2,128,128]{2,1,0:T(8,128)(2,1)S(1)}, bf16[2,128,128]{2,1,0:T(8,128)(2,1)}, u32[]{:S(2)}) copy-start(bf16[2,128,128]{2,1,0:T(8,128)(2,1)} %gweight.3) | copy-start | bytes 196612
  2.8 37.0 %copy-start.4 = (f32[2,128]{1,0:T(2,128)S(1)}, f32[2,128]{1,0:T(2,128)}, u32[]{:S(2)}) copy-start(f32[2,128]{1,0:T(2,128)} %gain.5) | copy-start | bytes 3076
  38.0 6.8 %collective-permute-start = (bf16[384,384]{1,0:T(8,128)(2,1)S(1)}, bf16[384,384]{1,0:T(8,128)(2,1)S(1)}, u32[]{:S(2)}, u32[]{:S(2)}) collective-permute-start(bf16[384,384]{1,0:T(8,128)(2,1)S(1)} %shard_map.65.right), channel_id=1, source_target_pairs={{0,64},{64,0},{1,65},{65,1},{2,66},{66,2},{3,67},{67,3},{4,68},{68... | collective-permute-start | bytes 884744 | tf_op jit(solution)/shard_map/ppermute | solution.py:319
  39.1 5.6 %collective-permute-start.1 = (bf16[384,384]{1,0:T(8,128)(2,1)S(1)}, bf16[384,384]{1,0:T(8,128)(2,1)S(1)}, u32[]{:S(2)}, u32[]{:S(2)}) collective-permute-start(bf16[384,384]{1,0:T(8,128)(2,1)S(1)} %shard_map.66.left), channel_id=1, source_target_pairs={{0,1},{1,0},{2,3},{3,2},{4,5},{5,4},{6,7},{7,6},{8,9},{9,8},{10,11... | collective-permute-start | bytes 884744 | tf_op jit(solution)/shard_map/ppermute | solution.py:319
  39.2 5.5 %collective-permute-start.3 = (bf16[384,384]{1,0:T(8,128)(2,1)S(1)}, bf16[384,384]{1,0:T(8,128)(2,1)S(1)}, u32[]{:S(2)}, u32[]{:S(2)}) collective-permute-start(bf16[384,384]{1,0:T(8,128)(2,1)S(1)} %shard_map.65.right), channel_id=1, source_target_pairs={{0,1},{1,0},{2,3},{3,2},{4,5},{5,4},{6,7},{7,6},{8,9},{9,8},{10,11... | collective-permute-start | bytes 884744 | tf_op jit(solution)/shard_map/ppermute | solution.py:319
  40.7 27.9 %copy-start.1 = (bf16[2,128,256]{2,1,0:T(8,128)(2,1)S(1)}, bf16[2,128,256]{2,1,0:T(8,128)(2,1)}, u32[]{:S(2)}) copy-start(bf16[2,128,256]{2,1,0:T(8,128)(2,1)} %weight.1) | copy-start | bytes 393220
  40.7 27.9 %copy-start.3 = (bf16[2,64,128]{2,1,0:T(8,128)(2,1)S(1)}, bf16[2,64,128]{2,1,0:T(8,128)(2,1)}, u32[]{:S(2)}) copy-start(bf16[2,64,128]{2,1,0:T(8,128)(2,1)} %oweight.3) | copy-start | bytes 98308
  40.7 27.9 %copy-start.5 = (f32[2,64]{1,0:T(2,128)S(1)}, f32[2,64]{1,0:T(2,128)}, u32[]{:S(2)}) copy-start(f32[2,64]{1,0:T(2,128)} %hgain.3) | copy-start | bytes 1540
  44.8 1.6 %collective-permute-start.2 = (bf16[384,384]{1,0:T(8,128)(2,1)S(1)}, bf16[384,384]{1,0:T(8,128)(2,1)S(1)}, u32[]{:S(2)}, u32[]{:S(2)}) collective-permute-start(bf16[384,384]{1,0:T(8,128)(2,1)S(1)} %collective-permute-done.right_y), channel_id=1, source_target_pairs={{0,1},{1,0},{2,3},{3,2},{4,5},{5,4},{6,7},{7,6},{8,9},{9,8},{10,11... | collective-permute-start | bytes 884744 | tf_op jit(solution)/shard_map/ppermute | solution.py:319
  97.8 6.8 %collective-permute-start.4 = (bf16[384,384]{1,0:T(8,128)(2,1)S(1)}, bf16[384,384]{1,0:T(8,128)(2,1)S(1)}, u32[]{:S(2)}, u32[]{:S(2)}) collective-permute-start(bf16[384,384]{1,0:T(8,128)(2,1)S(1)} %shard_map.71.left), channel_id=1, source_target_pairs={{0,4},{4,0},{1,5},{5,1},{2,6},{6,2},{3,7},{7,3},{8,12},{12,8},{9,1... | collective-permute-start | bytes 884744 | tf_op jit(solution)/shard_map/ppermute | solution.py:319
  99.0 5.6 %collective-permute-start.6 = (bf16[384,384]{1,0:T(8,128)(2,1)S(1)}, bf16[384,384]{1,0:T(8,128)(2,1)S(1)}, u32[]{:S(2)}, u32[]{:S(2)}) collective-permute-start(bf16[384,384]{1,0:T(8,128)(2,1)S(1)} %shard_map.71.left), channel_id=1, source_target_pairs={{0,1},{1,0},{2,3},{3,2},{4,5},{5,4},{6,7},{7,6},{8,9},{9,8},{10,11... | collective-permute-start | bytes 884744 | tf_op jit(solution)/shard_map/ppermute | solution.py:319
  104.6 1.6 %collective-permute-start.5 = (bf16[384,384]{1,0:T(8,128)(2,1)S(1)}, bf16[384,384]{1,0:T(8,128)(2,1)S(1)}, u32[]{:S(2)}, u32[]{:S(2)}) collective-permute-start(bf16[384,384]{1,0:T(8,128)(2,1)S(1)} %collective-permute-done.4.left_x), channel_id=1, source_target_pairs={{0,1},{1,0},{2,3},{3,2},{4,5},{5,4},{6,7},{7,6},{8,9},{9,8},{10,11... | collective-permute-start | bytes 884744 | tf_op jit(solution)/shard_map/ppermute | solution.py:319

commit v12 on v11

--- a/solution.py
+++ b/solution.py
@@ -73,12 +73,12 @@
 
 
 def project(normed, weight, staged, extra):
-    wt = weight.astype(F32).T.astype(BF16)
+    wt = (0.5 * weight.astype(F32)).T.astype(BF16)
     lane = lane_of(CH)
     for s in ORDER:
         proj = lax.dot_general(wt, normed[s * LANES : (s + 1) * LANES, :], NT, preferred_element_type=F32)
-        left = sigmoid(proj[:CH]) * proj[CH : 2 * CH]
-        right = sigmoid(proj[2 * CH : 3 * CH]) * proj[3 * CH :]
+        left = (jnp.tanh(proj[:CH]) + 1.0) * proj[CH : 2 * CH]
+        right = (jnp.tanh(proj[2 * CH : 3 * CH]) + 1.0) * proj[3 * CH :]
         first = jnp.where(lane < SLOT, left, pltpu.roll(right, SLOT, 1))
         second = jnp.where(lane < SLOT, pltpu.roll(left, SLOT, 1), right)
         if s + HALF >= MAIN:

time: 130 us -> 130 us (level)
  no operation moved by 1% of the time
where the time goes in v12:
time: 130 us
  blocking collectives  104 us (80%)
  Pallas kernels  12.6 us (10%)
  waiting for transfers between devices  10.2 us (8%)
  starting transfers between devices  2.57 us (2%)
    all_to_all x1, blocking collectives, body(): got = lax.all_to_all(sent, out_axes, 0, 0, tiled=True)  34.7 us
    all_to_all x1, blocking collectives, body(): got = lax.all_to_all(sent, in_axes, 0, 0, tiled=True)  26.2 us
    all_to_all x1, blocking collectives, body(): mixed = lax.all_to_all(sent, out_axes, 0, 0, tiled=True)  21.7 us
    all_to_all x1, blocking collectives, body(): mixed = lax.all_to_all(sent, in_axes, 0, 0, tiled=True)  21.5 us
    ppermute x7, waiting for transfers between devices, swap(): return lax.ppermute(values, axes, [(i, n - 1 - i) for i in range(n)])  10.2 us
    pallas_call x1, Pallas kernels, body(): call(project_kernel, [MESSAGE], 3, [block, gain32, weight, pltpu.Semaphor...  2.74 us
  transfers between devices with their start and end apart: 7, of which 4 were waited for; matrix products, arithmetic and copies ran while one was open for 0% of the time, Pallas kernels for 3%

profile of v12, /device:TPU:2, one launch (start us, length us, event | category | flops | bytes accessed | tf_op | source)
XLA Modules:
  0.0 129.9 jit_solution(4038128752549553450)
XLA Ops:
  0.0 2.7 %shard_map.64 = bf16[64,4,1152]{2,1,0:T(4,128)(2,1)S(1)} custom-call(bf16[48,48,128]{2,1,0:T(8,128)(2,1)} %pair.1, f32[2,128]{1,0:T(2,128)} %gain.5, bf16[2,128,256]{2,1,0:T(8,128)(2,1)} %weight.1), custom_call_target="tpu_custom_call" | custom-call | tf_op jit(solution)/shard_map/pallas_call | solution.py:341
  2.7 0.0 copy-start
  2.8 0.0 copy-start.2
  2.8 0.0 copy-start.4
  2.8 34.7 %all_to_all.20.got = bf16[64,4,1152]{2,1,0:T(4,128)(2,1)S(1)} all-to-all(bf16[64,4,1152]{2,1,0:T(4,128)(2,1)S(1)} %shard_map.64), channel_id=1, replica_groups=mesh['yh'=2,'yl'=2,'zl'=4,'xh'=2,'xl'=2,'zh'=2,'c'=2] {'yh','zl','xh','x..., dimensions={0} | all-to-all | bytes 1179648 | tf_op jit(solution)/shard_map/all_to_all | solution.py:349
  37.5 0.4 shard_map.65.right
  38.0 0.8 collective-permute-start
  38.7 0.4 shard_map.66.left
  39.1 0.1 collective-permute-start.1
  39.2 0.5 collective-permute-start.3
  39.7 0.9 shard_map.67.gate
  40.7 0.0 copy-start.1
  40.7 0.0 copy-start.3
  40.7 0.0 copy-start.5
  40.7 4.1 %collective-permute-done.right_y = bf16[384,384]{1,0:T(8,128)(2,1)S(1)} collective-permute-done((bf16[384,384]{1,0:T(8,128)(2,1)S(1)}, bf16[384,384]{1,0:T(8,128)(2,1)S(1)}, u32[]{:S(2)}, u32[]{:S(2)}) %collective-permute-start) | collective-permute-done | bytes 294944 | tf_op jit(solution)/shard_map/ppermute | solution.py:319
  44.8 0.0 collective-permute-start.2
  44.8 0.6 shard_map.68.early
  45.4 1.0 collective-permute-done.2.right_yc
  46.3 0.6 shard_map.69
  46.9 21.7 %all_to_all.21.mixed = bf16[64,2,1152]{2,1,0:T(2,128)(2,1)S(1)} all-to-all(bf16[64,2,1152]{2,1,0:T(2,128)(2,1)S(1)} %shard_map.69), channel_id=1, replica_groups=mesh['yh'=2,'yl'=2,'zl'=4,'xh'=2,'xl'=2,'zh'=2,'c'=2] {'yh','zl','xh','x..., dimensions={0} | all-to-all | bytes 589824 | tf_op jit(solution)/shard_map/all_to_all | solution.py:362
  68.6 2.4 %shard_map.70 = (bf16[48,48,128]{2,1,0:T(8,128)(2,1)S(1)}, bf16[64,4,1152]{2,1,0:T(4,128)(2,1)S(1)}) custom-call(bf16[48,48,128]{2,1,0:T(8,128)(2,1)S(1)} %copy-done, f32[3072,128]{1,0:T(8,128)S(1)} %shard_map.67.gate, bf16[64,2,1152]{2,1,0:T(2,128)(2,1)S(1)} %all_to_all.21.mixed, f32[2,128]{1,0:T(2,128)S(1)} %copy-done.4, f32[2,64]{1,0:T(2,128)S(1)} %copy-done.5, ...), custom_call_target="tpu_custom_call" | custom-call | tf_op jit(solution)/shard_map/pallas_call | solution.py:363
  71.0 26.2 %all_to_all.22.got = bf16[64,4,1152]{2,1,0:T(4,128)(2,1)S(1)} all-to-all(bf16[64,4,1152]{2,1,0:T(4,128)(2,1)S(1)} %get-tuple-element.36), channel_id=1, replica_groups=mesh['yh'=2,'yl'=2,'zl'=4,'xh'=2,'xl'=2,'zh'=2,'c'=2] {'yh','yl','zl','x..., dimensions={0} | all-to-all | bytes 1179648 | tf_op jit(solution)/shard_map/all_to_all | solution.py:366
  97.2 0.5 shard_map.71.left
  97.7 1.2 collective-permute-start.4
  98.9 0.4 shard_map.72.right
  99.3 0.9 shard_map.73.gate
  100.2 4.3 %collective-permute-done.4.left_x = bf16[384,384]{1,0:T(8,128)(2,1)S(1)} collective-permute-done((bf16[384,384]{1,0:T(8,128)(2,1)S(1)}, bf16[384,384]{1,0:T(8,128)(2,1)S(1)}, u32[]{:S(2)}, u32[]{:S(2)}) %collective-permute-start.4) | collective-permute-done | bytes 294944 | tf_op jit(solution)/shard_map/ppermute | solution.py:319
  104.5 0.7 shard_map.74.early
  105.2 0.9 collective-permute-done.5.left_d
  106.1 0.5 shard_map.75
  106.5 21.5 %all_to_all.23.mixed = bf16[64,2,1152]{2,1,0:T(2,128)(2,1)S(1)} all-to-all(bf16[64,2,1152]{2,1,0:T(2,128)(2,1)S(1)} %shard_map.75), channel_id=1, replica_groups=mesh['yh'=2,'yl'=2,'zl'=4,'xh'=2,'xl'=2,'zh'=2,'c'=2] {'yh','yl','zl','x..., dimensions={0} | all-to-all | bytes 589824 | tf_op jit(solution)/shard_map/all_to_all | solution.py:376
  128.1 1.7 %shard_map.76 = bf16[48,48,128]{2,1,0:T(8,128)(2,1)} custom-call(bf16[48,48,128]{2,1,0:T(8,128)(2,1)S(1)} %get-tuple-element.38.pair, f32[3072,128]{1,0:T(8,128)S(1)} %shard_map.73.gate, bf16[64,2,1152]{2,1,0:T(2,128)(2,1)S(1)} %all_to_all.23.mixed, f32[2,64]{1,0:T(2,128)S(1)} %copy-done.5, bf16[2,64,128]{2,1,0:T(8,128)(2,1)S(1)} %copy-done.3), custom_call_target="tpu_custom_call" | custom-call | tf_op jit(solution)/shard_map/pallas_call | solution.py:377
  (11 shorter events, 0.0 us)
Async XLA Ops:
  2.7 37.0 %copy-start = (bf16[48,48,128]{2,1,0:T(8,128)(2,1)S(1)}, bf16[48,48,128]{2,1,0:T(8,128)(2,1)}, u32[]{:S(2)}) copy-start(bf16[48,48,128]{2,1,0:T(8,128)(2,1)} %pair.1) | copy-start | bytes 1769476
  2.8 37.0 %copy-start.2 = (bf16[2,128,128]{2,1,0:T(8,128)(2,1)S(1)}, bf16[2,128,128]{2,1,0:T(8,128)(2,1)}, u32[]{:S(2)}) copy-start(bf16[2,128,128]{2,1,0:T(8,128)(2,1)} %gweight.3) | copy-start | bytes 196612
  2.8 37.0 %copy-start.4 = (f32[2,128]{1,0:T(2,128)S(1)}, f32[2,128]{1,0:T(2,128)}, u32[]{:S(2)}) copy-start(f32[2,128]{1,0:T(2,128)} %gain.5) | copy-start | bytes 3076
  38.0 6.8 %collective-permute-start = (bf16[384,384]{1,0:T(8,128)(2,1)S(1)}, bf16[384,384]{1,0:T(8,128)(2,1)S(1)}, u32[]{:S(2)}, u32[]{:S(2)}) collective-permute-start(bf16[384,384]{1,0:T(8,128)(2,1)S(1)} %shard_map.65.right), channel_id=1, source_target_pairs={{0,64},{64,0},{1,65},{65,1},{2,66},{66,2},{3,67},{67,3},{4,68},{68... | collective-permute-start | bytes 884744 | tf_op jit(solution)/shard_map/ppermute | solution.py:319
  39.1 5.6 %collective-permute-start.1 = (bf16[384,384]{1,0:T(8,128)(2,1)S(1)}, bf16[384,384]{1,0:T(8,128)(2,1)S(1)}, u32[]{:S(2)}, u32[]{:S(2)}) collective-permute-start(bf16[384,384]{1,0:T(8,128)(2,1)S(1)} %shard_map.66.left), channel_id=1, source_target_pairs={{0,1},{1,0},{2,3},{3,2},{4,5},{5,4},{6,7},{7,6},{8,9},{9,8},{10,11... | collective-permute-start | bytes 884744 | tf_op jit(solution)/shard_map/ppermute | solution.py:319
  39.2 5.5 %collective-permute-start.3 = (bf16[384,384]{1,0:T(8,128)(2,1)S(1)}, bf16[384,384]{1,0:T(8,128)(2,1)S(1)}, u32[]{:S(2)}, u32[]{:S(2)}) collective-permute-start(bf16[384,384]{1,0:T(8,128)(2,1)S(1)} %shard_map.65.right), channel_id=1, source_target_pairs={{0,1},{1,0},{2,3},{3,2},{4,5},{5,4},{6,7},{7,6},{8,9},{9,8},{10,11... | collective-permute-start | bytes 884744 | tf_op jit(solution)/shard_map/ppermute | solution.py:319
  40.7 27.9 %copy-start.1 = (bf16[2,128,256]{2,1,0:T(8,128)(2,1)S(1)}, bf16[2,128,256]{2,1,0:T(8,128)(2,1)}, u32[]{:S(2)}) copy-start(bf16[2,128,256]{2,1,0:T(8,128)(2,1)} %weight.1) | copy-start | bytes 393220
  40.7 27.9 %copy-start.3 = (bf16[2,64,128]{2,1,0:T(8,128)(2,1)S(1)}, bf16[2,64,128]{2,1,0:T(8,128)(2,1)}, u32[]{:S(2)}) copy-start(bf16[2,64,128]{2,1,0:T(8,128)(2,1)} %oweight.3) | copy-start | bytes 98308
  40.7 27.9 %copy-start.5 = (f32[2,64]{1,0:T(2,128)S(1)}, f32[2,64]{1,0:T(2,128)}, u32[]{:S(2)}) copy-start(f32[2,64]{1,0:T(2,128)} %hgain.3) | copy-start | bytes 1540
  44.8 1.6 %collective-permute-start.2 = (bf16[384,384]{1,0:T(8,128)(2,1)S(1)}, bf16[384,384]{1,0:T(8,128)(2,1)S(1)}, u32[]{:S(2)}, u32[]{:S(2)}) collective-permute-start(bf16[384,384]{1,0:T(8,128)(2,1)S(1)} %collective-permute-done.right_y), channel_id=1, source_target_pairs={{0,1},{1,0},{2,3},{3,2},{4,5},{5,4},{6,7},{7,6},{8,9},{9,8},{10,11... | collective-permute-start | bytes 884744 | tf_op jit(solution)/shard_map/ppermute | solution.py:319
  97.7 6.8 %collective-permute-start.4 = (bf16[384,384]{1,0:T(8,128)(2,1)S(1)}, bf16[384,384]{1,0:T(8,128)(2,1)S(1)}, u32[]{:S(2)}, u32[]{:S(2)}) collective-permute-start(bf16[384,384]{1,0:T(8,128)(2,1)S(1)} %shard_map.71.left), channel_id=1, source_target_pairs={{0,4},{4,0},{1,5},{5,1},{2,6},{6,2},{3,7},{7,3},{8,12},{12,8},{9,1... | collective-permute-start | bytes 884744 | tf_op jit(solution)/shard_map/ppermute | solution.py:319
  98.9 5.6 %collective-permute-start.6 = (bf16[384,384]{1,0:T(8,128)(2,1)S(1)}, bf16[384,384]{1,0:T(8,128)(2,1)S(1)}, u32[]{:S(2)}, u32[]{:S(2)}) collective-permute-start(bf16[384,384]{1,0:T(8,128)(2,1)S(1)} %shard_map.71.left), channel_id=1, source_target_pairs={{0,1},{1,0},{2,3},{3,2},{4,5},{5,4},{6,7},{7,6},{8,9},{9,8},{10,11... | collective-permute-start | bytes 884744 | tf_op jit(solution)/shard_map/ppermute | solution.py:319
  104.5 1.6 %collective-permute-start.5 = (bf16[384,384]{1,0:T(8,128)(2,1)S(1)}, bf16[384,384]{1,0:T(8,128)(2,1)S(1)}, u32[]{:S(2)}, u32[]{:S(2)}) collective-permute-start(bf16[384,384]{1,0:T(8,128)(2,1)S(1)} %collective-permute-done.4.left_x), channel_id=1, source_target_pairs={{0,1},{1,0},{2,3},{3,2},{4,5},{5,4},{6,7},{7,6},{8,9},{9,8},{10,11... | collective-permute-start | bytes 884744 | tf_op jit(solution)/shard_map/ppermute | solution.py:319
